TPU v7x, 128 devices: a whole 4x4x4 slice. The times are simulated.
128 devices in a mesh: harm: 16 (over x, z_hi, core), mode: 8 (over y, z_lo).
Axes of the slice: x: 4, y: 4, z: 4 (z_hi: 2, z_lo: 2; z = z_hi * 2 + z_lo), core: 2. Of those that a mesh axis runs over, the one named last changes fastest.
Arguments:
- mode_vectors: float32 [49152, 1024], P('harm', 'mode'), may hold values from -0.09375 to 0.09375
- weights: float32 [49152, 1024], P('harm', 'mode'), may hold values from -0.1875 to 0.1875
- cotangent: float32 [49152, 1024], P('harm', 'mode'), may hold values from -6 to 6
- eigenvalues: float32 [1024], replicated, may hold values from 0 to 4
- eigen_cotangent: float32 [1024], replicated, may hold values from -6 to 6
- slab_rows: int32 [4096], replicated, may hold values from 0 to 49151, as said below
Outputs:
- slab: float32 [4096, 49152], P('mode', 'harm')
Inputs may be any that keep to these rules, and one draw needn't show every extreme that they name: `slab_rows`: each block of 3072 consecutive harmonics (0 to 3071, 3072 to 6143 and so on) holds exactly 256 of the slab rows.
All inputs are finite; a program needn't handle non-finite values.
Results may differ from a plain program's by a relative error of at most 0.0001.
Values sent between devices are 32-bit elements; how exact they have to be, the bound alone decides.
No kernel may reach another device: no remote copies, remote signals or barrier semaphores. Data moves between devices by JAX's collectives and lax.ppermute only.
A program may use at most 128 MiB of HBM per device.

v0:
```python
import jax
import jax.numpy as jnp
from jax import lax
from jax.sharding import Mesh
from jax.sharding import PartitionSpec as P

MODE = ("mode_0", "mode_1")


regular = 0.01
highest = lax.Precision.HIGHEST


def gathered_by_axis(array, axes, dim):
    whole = array
    for number in range(len(axes) - 1, -1, -1):
        whole = lax.all_gather(whole, axes[number], axis=dim, tiled=True)
    return whole


def in_blocks(array, dim, length):
    before, after = (array.shape[:dim], array.shape[dim + 1 :])
    return jnp.moveaxis(array.reshape(*before, length, -1, *after), dim, 0)


def summed_on_arrival(array, axis, dim):
    length = lax.axis_size(axis)
    parts = lax.all_to_all(in_blocks(array, dim, length), axis, 0, 0, tiled=True)
    return jnp.sum(parts, axis=0)


def in_order(parts, dim):
    dims = list(parts.shape[1:])
    dims[dim] *= parts.shape[0]
    return jnp.moveaxis(parts, 0, dim).reshape(dims)


def sent_to_all(array, axis):
    length = lax.axis_size(axis)
    return lax.all_to_all(
        jnp.broadcast_to(array[None], (length, *array.shape)), axis, 0, 0, tiled=True
    )


def gathered_copies(array, axis, dim):
    return in_order(sent_to_all(array, axis), dim)


def weigh_gap(block, eigenvalues, eigen_cotangent, row_first, col_first):
    row_count = block.shape[0]
    col_count = block.shape[1]
    eigen_rows = lax.dynamic_slice_in_dim(eigenvalues, row_first, row_count)
    eigen_cols = lax.dynamic_slice_in_dim(eigenvalues, col_first, col_count)
    slope_cols = lax.dynamic_slice_in_dim(eigen_cotangent, col_first, col_count)
    differ = eigen_cols[None, :] - eigen_rows[:, None]
    factor = differ / (differ * differ + regular)
    row_ids = row_first + lax.broadcasted_iota(jnp.int32, (row_count, col_count), 0)
    col_ids = col_first + lax.broadcasted_iota(jnp.int32, (row_count, col_count), 1)
    return factor * block + jnp.where(row_ids == col_ids, slope_cols[None, :], 0.0)


def local(mode_vectors, weights, cotangent, eigenvalues, eigen_cotangent, slab_rows):
    harm_index = lax.axis_index("harm")
    mode_index = lax.axis_index(MODE)
    mode_width = mode_vectors.shape[1]
    col_first = mode_index * mode_width
    vectors_full = gathered_by_axis(mode_vectors, MODE, 1)
    gram_part = lax.dot_general(
        vectors_full,
        cotangent,
        (((0,), (0,)), ((), ())),
        precision=highest,
        preferred_element_type=jnp.float32,
    )
    share_block = summed_on_arrival(gram_part, "harm", 0)
    share_rows = share_block.shape[0]
    weighted_share = weigh_gap(
        share_block, eigenvalues, eigen_cotangent, harm_index * share_rows, col_first
    )
    weighted = gathered_copies(weighted_share, "harm", 0)
    block_height = weights.shape[0]
    total_rows = slab_rows.shape[0]
    block_rows = total_rows // lax.axis_size("harm")
    block_of = slab_rows // block_height
    arranged = jnp.argsort(block_of, stable=True)
    own_slots = lax.dynamic_slice_in_dim(arranged, harm_index * block_rows, block_rows)
    own_harmonics = jnp.take(slab_rows, own_slots, axis=0) - harm_index * block_height
    local_weights = jnp.take(weights, own_harmonics, axis=0)
    block_weights = gathered_copies(local_weights, MODE, 1)
    block_z = jnp.dot(
        block_weights, weighted, precision=highest, preferred_element_type=jnp.float32
    )
    arranged_z = lax.all_gather(block_z, "harm", axis=0, tiled=True)
    inverse = (
        jnp.zeros((total_rows,), jnp.int32)
        .at[arranged]
        .set(jnp.arange(total_rows, dtype=jnp.int32))
    )
    ordered_z = jnp.take(arranged_z, inverse, axis=0)
    owned_rows = lax.all_to_all(ordered_z, MODE, split_axis=0, concat_axis=1, tiled=True)
    return lax.dot_general(
        owned_rows,
        vectors_full,
        (((1,), (1,)), ((), ())),
        precision=highest,
        preferred_element_type=jnp.float32,
    )


def solution(mesh):
    torus = Mesh(mesh.devices.reshape(mesh.shape["harm"], 4, 2), ("harm", "mode_0", "mode_1"))
    return jax.shard_map(
        local,
        mesh=torus,
        in_specs=(P("harm", MODE), P("harm", MODE), P("harm", MODE), P(), P(), P()),
        out_specs=P(MODE, "harm"),
        check_vma=False,
    )
```

profile of v0, /device:TPU:0, one launch (start us, length us, event | category | flops | bytes accessed | tf_op | source)
XLA Modules:
  0.0 408.0 jit_solution(13173204455241433102)
XLA Ops:
  6.5 0.0 copy-start
  6.5 0.0 copy-start.1
  6.5 0.0 all-gather.4.cloned.1.call-start
  6.5 0.7 all-gather.4.cloned.1.call-update
  7.3 0.0 all-gather.6.cloned.1.call-start
  7.3 51.7 %all-gather.4.cloned.1.call-done = f32[3072,256]{1,0:T(8,128)} async-done(((f32[3072,128]{1,0:T(8,128)}), f32[3072,256]{1,0:T(8,128)}) %all-gather.4.cloned.1.call-update) | async-done | bytes 3145744 | tf_op jit(solution)/shard_map/all_gather | solution.py:17
  59.0 0.0 all-gather.6.cloned.1.call-update
  59.0 0.0 copy-done.1
  59.1 5.8 %sort.17 = (s32[4096]{0:T(1024)}, s32[4096]{0:T(1024)S(1)}) sort(s32[4096]{0:T(1024)S(1)} %add_select_fusion, s32[4096]{0:T(1024)S(1)} %iota.19), dimensions={0}, to_apply=%region_0.0 | sort | flops 49152 | bytes 65536 | tf_op jit(solution)/shard_map/jit(argsort)/sort | solution.py:85
  64.8 0.1 compare_select_fusion.3
  64.9 1.7 gather_fusion
  66.7 113.6 %all-gather.6.cloned.1.call-done = f32[3072,1024]{1,0:T(8,128)} async-done(((f32[3072,256]{1,0:T(8,128)}), f32[3072,1024]{1,0:T(8,128)}) %all-gather.6.cloned.1.call-update) | async-done | bytes 12582928 | tf_op jit(solution)/shard_map/all_gather | solution.py:17
  180.2 0.0 copy-done
  180.2 23.3 %fusion.8 = f32[1024,128]{1,0:T(8,128)} fusion(f32[3072,1024]{1,0:T(8,128)} %all-gather.6.cloned.1.call-done, f32[3072,128]{1,0:T(8,128)S(1)} %copy-done), kind=kOutput, calls=%fused_computation.30 | convolution fusion | flops 4831838208 | bytes 14680064 | tf_op jit(solution)/shard_map/dot_general | solution.py:68
  203.5 7.0 %all-to-all-start.1 = ((f32[16,64,128]{2,1,0:T(8,128)}), f32[16,64,128]{2,1,0:T(8,128)S(1)}, u32[]{:S(2)}, u32[]{:S(2)}) async-start(f32[16,64,128]{2,1,0:T(8,128)} %bitcast.2), calls=%async_computation.1 | async-start | bytes 1048576 | tf_op jit(solution)/shard_map/all_to_all | solution.py:28
  210.5 0.1 compare_and_fusion.1
  210.6 2.1 gather_fusion.1
  212.7 0.1 broadcast_select_fusion.1
  212.8 0.1 copy.7
  212.9 9.9 %all-to-all-done.1 = f32[16,64,128]{2,1,0:T(8,128)S(1)} async-done(((f32[16,64,128]{2,1,0:T(8,128)}), f32[16,64,128]{2,1,0:T(8,128)S(1)}, u32[]{:S(2)}, u32[]{:S(2)}) %all-to-all-start.1) | async-done | bytes 524320 | tf_op jit(solution)/shard_map/all_to_all | solution.py:28
  222.8 1.1 broadcast_in_dim.69
  223.9 4.1 %all-to-all-start = ((f32[8,256,128]{1,2,0:T(8,128)}), f32[8,256,128]{1,2,0:T(8,128)S(1)}, u32[]{:S(2)}, u32[]{:S(2)}) async-start(f32[8,256,128]{1,2,0:T(8,128)} %broadcast_in_dim.69), calls=%async_computation | async-start | bytes 2097152 | tf_op jit(solution)/shard_map/all_to_all | solution.py:40
  228.0 0.0 all-gather.8.cloned.1.call-start
  228.1 0.8 dynamic_slice.14
  228.8 0.8 dynamic_slice.13
  229.6 0.8 dynamic_slice.15
  230.4 0.1 fusion.2
  230.5 12.5 %all-to-all-done = f32[8,256,128]{1,2,0:T(8,128)S(1)} async-done(((f32[8,256,128]{1,2,0:T(8,128)}), f32[8,256,128]{1,2,0:T(8,128)S(1)}, u32[]{:S(2)}, u32[]{:S(2)}) %all-to-all-start) | async-done | bytes 1048608 | tf_op jit(solution)/shard_map/all_to_all | solution.py:40
  243.0 17.0 %all_to_all.31 = f32[16,64,128]{2,1,0:T(8,128)S(1)} all-to-all(f32[16,64,128]{2,1,0:T(8,128)S(1)} %broadcast_in_dim.72), channel_id=1, replica_groups=mesh['harm'=16,'mode_0'=4,'mode_1'=2] {'harm'}, dimensions={0} | all-to-all | bytes 1048576 | tf_op jit(solution)/shard_map/all_to_all | solution.py:40
  260.0 2.5 fusion.9
  262.5 0.0 all-gather.8.cloned.1.call-update
  262.5 15.5 %scatter_custom_fusion = s32[4096]{0:T(1024)S(1)} fusion(s32[4096]{0:T(1024)S(1)} %compare_select_fusion.1, s32[4096]{0:T(1024)S(1)} %iota.20, s32[]{:T(128)} %constant.35.clone.1), kind=kCustom, calls=%fused_computation.19 | custom fusion | bytes 16388 | tf_op jit(solution)/shard_map/scatter | solution.py:97
  278.1 27.4 %all-gather.8.cloned.1.call-done = f32[4096,128]{1,0:T(8,128)} async-done(((f32[256,128]{1,0:T(8,128)}), f32[4096,128]{1,0:T(8,128)}) %all-gather.8.cloned.1.call-update) | async-done | bytes 2097168 | tf_op jit(solution)/shard_map/all_gather | solution.py:93
  305.5 15.8 %gather_fusion.2 = f32[4096,128]{1,0:T(8,128)} fusion(f32[4096,128]{1,0:T(8,128)} %all-gather.8.cloned.1.call-done, s32[4096]{0:T(1024)S(1)} %fusion.4), kind=kCustom, calls=%fused_computation.2 | custom fusion | bytes 4210688 | tf_op jit(solution)/shard_map/jit(_take)/gather | solution.py:99
  321.3 2.9 copy.8
  324.2 1.8 broadcast_select_fusion
  326.0 31.2 %all_to_all.32 = f32[8,512,128]{1,2,0:T(8,128)S(1)} all-to-all(f32[8,512,128]{1,2,0:T(8,128)S(1)} %broadcast_select_fusion), channel_id=1, replica_groups=mesh['harm'=16,'mode_0'=4,'mode_1'=2] {'mode_0','mode_1'}, dimensions={0} | all-to-all | bytes 4194304 | tf_op jit(solution)/shard_map/all_to_all | solution.py:100
  357.2 44.2 %fusion.10 = f32[512,3072]{1,0:T(8,128)} fusion(f32[512,1024]{0,1:T(8,128)S(1)} %bitcast.16, f32[3072,1024]{1,0:T(8,128)} %all-gather.6.cloned.1.call-done), kind=kOutput, calls=%fused_computation.32 | convolution fusion | flops 19327352832 | bytes 20971520 | tf_op jit(solution)/shard_map/dot_general | solution.py:101
  (13 shorter events, 0.2 us)
Async XLA Ops:
  6.5 173.7 %copy-start = (f32[3072,128]{1,0:T(8,128)S(1)}, f32[3072,128]{1,0:T(8,128)}, u32[]{:S(2)}) copy-start(f32[3072,128]{1,0:T(8,128)} %param.8) | copy-start | bytes 4718596
  6.5 52.5 %copy-start.1 = (s32[4096]{0:T(1024)S(1)}, s32[4096]{0:T(1024)}, u32[]{:S(2)}) copy-start(s32[4096]{0:T(1024)} %param.11) | copy-start | bytes 49156
  6.5 52.5 %all-gather.4.cloned.1.call-start = ((), (), s32[]{:S(2)}) async-start(), calls=%async_computation.4 | async-start | bytes 4718592 | tf_op jit(solution)/shard_map/all_gather | solution.py:17
  7.3 173.0 %all-gather.6.cloned.1.call-start = ((), (), s32[]{:S(2)}) async-start(), calls=%async_computation.5 | async-start | bytes 15728640 | tf_op jit(solution)/shard_map/all_gather | solution.py:17
  203.5 19.3 %all-to-all-start.1 = ((f32[16,64,128]{2,1,0:T(8,128)}), f32[16,64,128]{2,1,0:T(8,128)S(1)}, u32[]{:S(2)}, u32[]{:S(2)}) async-start(f32[16,64,128]{2,1,0:T(8,128)} %bitcast.2), calls=%async_computation.1 | async-start | bytes 1048576 | tf_op jit(solution)/shard_map/all_to_all | solution.py:28
  223.9 19.1 %all-to-all-start = ((f32[8,256,128]{1,2,0:T(8,128)}), f32[8,256,128]{1,2,0:T(8,128)S(1)}, u32[]{:S(2)}, u32[]{:S(2)}) async-start(f32[8,256,128]{1,2,0:T(8,128)} %broadcast_in_dim.69), calls=%async_computation | async-start | bytes 2097152 | tf_op jit(solution)/shard_map/all_to_all | solution.py:40
  228.0 77.5 %all-gather.8.cloned.1.call-start = ((), (), s32[]{:S(2)}) async-start(), calls=%async_computation.6 | async-start | bytes 2228224 | tf_op jit(solution)/shard_map/all_gather | solution.py:93
Sparse Core Ops, SparseCore 0:
  9.0 49.9 all-gather.3
  60.7 119.5 all-gather.5
  262.6 42.8 all-gather.7
where the time goes:
time: 409 us; the launch traced here: 408 us
  waiting for transfers between devices  216 us (53%)
  matrix products  70 us (17%)
  blocking collectives  48.2 us (12%)
  local copies, waits for them, and re-layouts  41.6 us (10%)
  between operations  13.3 us (3%)
  starting transfers between devices  11.2 us (3%)
  other arithmetic  8.06 us (2%)
    all_gather x2, waiting for transfers between devices, gathered_by_axis(): whole = lax.all_gather(whole, axes[number], axis=dim, tiled=True)  165 us
    dot_general x1, matrix products, local(): lax.dot_general(owned_rows, vectors_full, (((1,), (1,)), ((), ())), preci...  44.2 us
    all_to_all x1, blocking collectives, local(): lax.all_to_all(ordered_z, MODE, split_axis=0, concat_axis=1, tiled=True)  31.2 us
    all_gather x1, waiting for transfers between devices, local(): arranged_z = lax.all_gather(block_z, 'harm', axis=0, tiled=True)  27.4 us
    dot_general x1, matrix products, local(): lax.dot_general(vectors_full, cotangent, (((0,), (0,)), ((), ())), precis...  23.3 us
    gather x2, local copies, waits for them, and re-layouts, local(): ordered_z = jnp.take(arranged_z, inverse, axis=0)  18.7 us
    all_to_all x1, blocking collectives, sent_to_all(): lax.all_to_all(jnp.broadcast_to(array[None], (length, *array.shape)), axi...  17 us
    scatter x1, local copies, waits for them, and re-layouts, local(): inverse = jnp.zeros((total_rows,), jnp.int32).at[arranged].set(jnp.arange...  15.5 us
  transfers between devices with their start and end apart: 5, of which 5 were waited for; matrix products, arithmetic and copies ran while one was open for 7% of the time, Pallas kernels for 0%

commit v1 on v0

v1 whole, which is shorter than its diff:
```python
import jax
import jax.numpy as jnp
from jax import lax
from jax.experimental import pallas as pl
from jax.experimental.pallas import tpu as pltpu
from jax.sharding import Mesh
from jax.sharding import PartitionSpec as P

HARM = ("x", "zh", "c")
MODE = ("y", "zl")
SIZES = {"x": 4, "zh": 2, "c": 2, "y": 4, "zl": 2}
regular = 0.01
TILE = 256
VMEM = 60 * 1024 * 1024


def shifted(array, axis, step):
    n = SIZES[axis]
    return lax.ppermute(array, axis, [(i, (i + step) % n) for i in range(n)])


def pick(parts, number):
    return lax.dynamic_index_in_dim(parts, number, 0, keepdims=False)


def slot_of(offset):
    return jnp.where(offset == 0, 0, jnp.where(offset == 3, 1, jnp.where(offset == 1, 2, 3)))


def ring_parts(array, axis):
    return jnp.stack([array, shifted(array, axis, 1), shifted(array, axis, -1), shifted(array, axis, 2)])


def split(value):
    high = value.astype(jnp.bfloat16)
    low = (value - high.astype(jnp.float32)).astype(jnp.bfloat16)
    return high, low


def three_pass(a, b, dims):
    a_high, a_low = a
    b_high, b_low = b
    def dot(p, q):
        return lax.dot_general(p, q, (dims, ((), ())), preferred_element_type=jnp.float32)
    return dot(a_high, b_high) + dot(a_high, b_low) + dot(a_low, b_high)


def gram_part(cots, blocks):
    rows = cots[0].shape[0]
    tile = 512
    steps = rows // tile
    flat, plan, firsts = [], [], []
    for block in blocks:
        first, pieces = 0, []
        for piece in block:
            count = piece.shape[0] // tile
            pieces.append((len(flat), first, count))
            flat.append(piece)
            firsts.append((first, count))
            first += count
        plan.append(pieces)

    def body(*refs):
        cot_refs, piece_refs, out = refs[: len(cots)], refs[len(cots) : -1], refs[-1]
        step = pl.program_id(0)

        @pl.when(step == 0)
        def _():
            out[...] = jnp.zeros_like(out)

        cot = split(jnp.concatenate([r[...] for r in cot_refs], axis=1))
        found = []
        for pieces in plan:
            value = piece_refs[pieces[0][0]][...]
            for index, first, _ in pieces[1:]:
                value = jnp.where(step >= first, piece_refs[index][...], value)
            found.append(value)
        block = split(jnp.concatenate(found, axis=1) if len(found) > 1 else found[0])
        out[...] += three_pass(cot, block, ((0,), (0,)))

    def spec(first, count):
        return pl.BlockSpec((tile, 128), lambda i: (jnp.clip(i - first, 0, count - 1), 0))

    width, cols = 128 * len(cots), 128 * len(blocks)
    return pl.pallas_call(
        body,
        grid=(steps,),
        in_specs=[spec(0, steps) for _ in cots] + [spec(f, n) for f, n in firsts],
        out_specs=pl.BlockSpec((width, cols), lambda i: (0, 0)),
        out_shape=jax.ShapeDtypeStruct((width, cols), jnp.float32),
        compiler_params=pltpu.CompilerParams(vmem_limit_bytes=VMEM),
        cost_estimate=pl.CostEstimate(
            flops=6 * rows * width * cols, bytes_accessed=4 * rows * (width + cols), transcendentals=0
        ),
    )(*cots, *flat)


def slab_part(z, blocks):
    total = sum(p.shape[0] for p in blocks[0])
    steps = total // TILE
    depth = z.shape[1]
    flat, plan, firsts = [], [], []
    for block in blocks:
        first, pieces = 0, []
        for piece in block:
            count = piece.shape[0] // TILE
            pieces.append((len(flat), first, count))
            flat.append(piece)
            firsts.append((first, count))
            first += count
        plan.append(pieces)

    def body(z_ref, *refs):
        piece_refs, out, z_high, z_low = refs[:-3], refs[-3], refs[-2], refs[-1]
        step = pl.program_id(0)

        @pl.when(step == 0)
        def _():
            z_high[...], z_low[...] = split(z_ref[...])

        found = []
        for pieces in plan:
            value = piece_refs[pieces[0][0]][...]
            for index, first, _ in pieces[1:]:
                value = jnp.where(step >= first, piece_refs[index][...], value)
            found.append(value)
        x = split(jnp.concatenate(found, axis=1))
        out[...] = three_pass((z_high[...], z_low[...]), x, ((1,), (1,)))

    def spec(first, count):
        return pl.BlockSpec((TILE, 128), lambda i: (jnp.clip(i - first, 0, count - 1), 0))

    return pl.pallas_call(
        body,
        grid=(steps,),
        in_specs=[pl.BlockSpec(z.shape, lambda i: (0, 0))] + [spec(f, n) for f, n in firsts],
        out_specs=pl.BlockSpec((z.shape[0], TILE), lambda i: (0, i)),
        out_shape=jax.ShapeDtypeStruct((z.shape[0], total), jnp.float32),
        scratch_shapes=[pltpu.VMEM(z.shape, jnp.bfloat16), pltpu.VMEM(z.shape, jnp.bfloat16)],
        compiler_params=pltpu.CompilerParams(vmem_limit_bytes=VMEM),
        cost_estimate=pl.CostEstimate(
            flops=6 * total * z.shape[0] * depth,
            bytes_accessed=4 * (total * depth + total * z.shape[0]),
            transcendentals=0,
        ),
    )(z, *flat)


def slab_weights(weights, slab_rows, x, zh, c, y, zl):
    height = weights.shape[0]
    total = slab_rows.shape[0]
    count = total // 16
    harm = (x * 2 + zh) * 2 + c
    arranged = jnp.argsort(slab_rows // height, stable=True).astype(jnp.int32)
    place = jnp.argsort(arranged).astype(jnp.int32)
    own_slots = lax.dynamic_slice_in_dim(arranged, harm * count, count)
    own = jnp.take(slab_rows, own_slots, axis=0, mode="clip") - harm * height
    rows = jnp.take(weights, own, axis=0, mode="clip")
    pair = jnp.stack([rows, shifted(rows, "zh", 1)])
    ring = ring_parts(pair, "x")
    every = jnp.stack([ring, shifted(ring, "c", 1)])
    every = every.reshape(-1, 128)
    share = total // 8 // 8
    wanted = lax.dynamic_slice_in_dim(place.reshape(8, 8, share), x * 2 + c, 1, axis=1).reshape(-1)
    source, row = wanted // count, wanted % count
    source_x, source_zh, source_c = source // 4, (source // 2) % 2, source % 2
    held = (
        ((source_c != c) * 4 + slot_of((source_x - x) % 4)) * 2 + (source_zh != zh)
    ) * count + row
    chosen = jnp.take(every, held, axis=0, mode="clip").reshape(8, share, 128)
    came = lax.all_to_all(chosen, MODE, 0, 0, tiled=True).reshape(4, 2, share, 128)
    came = jnp.where(zl == 0, came, came[:, ::-1])
    came = came.transpose(2, 1, 0, 3).reshape(share, 1024)
    return lax.all_gather(came, ("x", "c"), axis=0, tiled=True)


def local(mode_vectors, weights, cotangent, eigenvalues, eigen_cotangent, slab_rows):
    x, zh, c, y, zl = (lax.axis_index(a) for a in ("x", "zh", "c", "y", "zl"))
    rows = mode_vectors.shape[0]
    half = rows // 2
    cut = rows * 3 // 4
    mid = TILE * ((cut // 2) // TILE)

    below = shifted(mode_vectors, "y", 1)
    above = shifted(mode_vectors, "y", -1)
    other_cot = shifted(cotangent, "zl", 1)
    far = [shifted(below[:half], "y", 1), shifted(above[half:], "y", -1)]
    other_a = shifted(mode_vectors[:mid], "zl", 1)
    other_b = shifted(mode_vectors[mid:cut], "zl", 1)
    other_c = shifted(mode_vectors[cut:], "zl", 1)
    other_below_a = shifted(other_a, "y", 1)
    other_above_a = shifted(other_a, "y", -1)
    other_below_b = shifted(other_b, "y", 1)
    other_above_b = shifted(other_b, "y", -1)
    other_far = [shifted(other_below_a, "y", 1), shifted(other_above_b, "y", -1)]
    other_below_c = shifted(below[cut:], "zl", 1)
    other_above_c = shifted(above[cut:], "zl", 1)
    other_far_c = shifted(far[1][cut - half :], "zl", 1)

    picked = slab_weights(weights, slab_rows, x, zh, c, y, zl)

    near = gram_part([cotangent, other_cot], [[mode_vectors], [below], [above]])
    last = gram_part([cotangent, other_cot], [far])
    gram = jnp.concatenate([near, last], axis=1)
    gram = jnp.where(zl == 0, gram, jnp.roll(gram, 128, axis=0))
    gram = gram.reshape(4, 2, 32, 512)
    core = lax.dynamic_index_in_dim(gram, c, 1, keepdims=False) + shifted(
        lax.dynamic_index_in_dim(gram, 1 - c, 1, keepdims=False), "c", 1
    )
    total = (
        pick(core, x)
        + shifted(pick(core, (x + 1) % 4), "x", 1)
        + shifted(pick(core, (x + 3) % 4), "x", -1)
        + shifted(pick(core, (x + 2) % 4), "x", 2)
    )
    total = total + shifted(total, "zh", 1)
    parts = total.reshape(32, 4, 128)
    parts = jnp.stack(
        [lax.dynamic_index_in_dim(parts, slot_of((k - y) % 4), 1, keepdims=False) for k in range(4)], axis=1
    )
    j_first = (y * 2 + x // 2) * 128 + ((x % 2) * 2 + c) * 32
    eigen_j = lax.dynamic_slice_in_dim(eigenvalues, j_first, 32)
    slope_j = lax.dynamic_slice_in_dim(eigen_cotangent, j_first, 32)
    eigen_i = lax.dynamic_index_in_dim(eigenvalues.reshape(4, 2, 128), zl, 1, keepdims=False)
    differ = eigen_j[:, None, None] - eigen_i[None]
    factor = differ / (differ * differ + regular)
    shape = parts.shape
    j_ids = j_first + lax.broadcasted_iota(jnp.int32, shape, 0)
    i_ids = (lax.broadcasted_iota(jnp.int32, shape, 1) * 2 + zl) * 128 + lax.broadcasted_iota(jnp.int32, shape, 2)
    weighted = factor * parts + jnp.where(j_ids == i_ids, slope_j[:, None, None], 0.0)
    weighted = weighted.reshape(32, 512)

    weighted = jnp.concatenate([weighted, shifted(weighted, "zl", 1)], axis=1)
    weighted = ring_parts(weighted, "y").reshape(128, 1024)
    z = lax.dot_general(
        weighted, picked, (((1,), (1,)), ((), ())),
        precision=lax.Precision.HIGH, preferred_element_type=jnp.float32,
    )
    z = ring_parts(z, "x")
    cores = jnp.stack([z, shifted(z, "c", 1)])
    cores = jnp.where(c == 0, cores, cores[::-1])
    ordered = jnp.stack(
        [lax.dynamic_index_in_dim(cores, slot_of(((q ^ (2 * zl)) - x) % 4), 1, keepdims=False) for q in range(4)]
    )
    ordered = ordered.reshape(2, 2, 2, 4, 32, -1).transpose(5, 0, 3, 1, 2, 4).reshape(-1, 1024)
    blocks = [
        [mode_vectors], [below], [above], far,
        [other_a, other_b, other_c],
        [other_below_a, other_below_b, other_below_c],
        [other_above_a, other_above_b, other_above_c],
        [*other_far, other_far_c],
    ]
    return slab_part(ordered, blocks)


def solution(mesh):
    torus = Mesh(mesh.devices.reshape(4, 2, 2, 4, 2), ("x", "zh", "c", "y", "zl"))
    return jax.shard_map(
        local,
        mesh=torus,
        in_specs=(P(HARM, MODE), P(HARM, MODE), P(HARM, MODE), P(), P(), P()),
        out_specs=P(MODE, HARM),
        check_vma=False,
    )
```

time: 409 us -> 253 us (0.62)
  waiting for transfers between devices: 216 us -> 107 us
  matrix products: 70 us -> 2.93 us
  blocking collectives: 48.2 us -> 0 us
  starting transfers between devices: 11.2 us -> 49.9 us
  Pallas kernels: 0 us -> 31.3 us
  local copies, waits for them, and re-layouts: 41.6 us -> 22.4 us
  other arithmetic: 8.06 us -> 23.7 us
    all_gather x3 -> x1, waiting for transfers between devices: 193 us -> 0.01 us  [slab_weights(): return lax.all_gather(came, ('x', 'c'), axis=0, tiled=True)]
    ppermute x0 -> x35, waiting for transfers between devices: none -> 84.4 us  [shifted(): return lax.ppermute(array, axis, [(i, (i + step) % n) for i in range(n)])]
    dot_general x3 -> x1, matrix products: 70 us -> 2.93 us  [local(): lax.dot_general(weighted, picked, (((1,), (1,)), ((), ())), precision=lax...]
    all_to_all x2 -> x0, blocking collectives: 48.2 us -> none  [the longest x1 31.2 us: local(): lax.all_to_all(ordered_z, MODE, split_axis=0, concat_axis=1, tiled=True)]
    ppermute x0 -> x35, starting transfers between devices: none -> 44.9 us  [shifted(): return lax.ppermute(array, axis, [(i, (i + step) % n) for i in range(n)])]
    pallas_call x0 -> x3, Pallas kernels: none -> 31.3 us  [the longest x1 18.1 us: slab_part(): pl.pallas_call(body, grid=(steps,), in_specs=[pl.BlockSpec(z.shape, lambd...]
    gather x4 -> x3, local copies, waits for them, and re-layouts: 22.5 us -> 5.9 us  [the longest x1 3.21 us: slab_weights(): chosen = jnp.take(every, held, axis=0, mode='clip').reshape(8, share, 128)]
    scatter x1 -> x0, local copies, waits for them, and re-layouts: 15.5 us -> none  [local(): inverse = jnp.zeros((total_rows,), jnp.int32).at[arranged].set(jnp.arange...]
  transfers between devices with their start and end apart: 5 -> 37, of which waited for: 5 -> 24; matrix products, arithmetic and copies ran while one was open for 7% -> 13% of each run, Pallas kernels for 0% -> 5%
where the time goes in v1:
time: 253 us; the launch traced here: 251 us
  waiting for transfers between devices  107 us (42%)
  starting transfers between devices  49.9 us (20%)
  Pallas kernels  31.3 us (12%)
  other arithmetic  23.7 us (9%)
  local copies, waits for them, and re-layouts  22.4 us (9%)
  between operations  13.9 us (5%)
  matrix products  2.93 us (1%)
    ppermute x35, waiting for transfers between devices, shifted(): return lax.ppermute(array, axis, [(i, (i + step) % n) for i in range(n)])  84.4 us
    ppermute x35, starting transfers between devices, shifted(): return lax.ppermute(array, axis, [(i, (i + step) % n) for i in range(n)])  44.9 us
    all_to_all x1, waiting for transfers between devices, slab_weights(): lax.all_to_all(chosen, MODE, 0, 0, tiled=True).reshape(4, 2, share, 128)  22.6 us
    pallas_call x1, Pallas kernels, slab_part(): pl.pallas_call(body, grid=(steps,), in_specs=[pl.BlockSpec(z.shape, lambd...  18.1 us
    pallas_call x2, Pallas kernels, gram_part(): pl.pallas_call(body, grid=(steps,), in_specs=[spec(0, steps) for _ in cot...  13.2 us
    sort x1, other arithmetic, slab_weights(): arranged = jnp.argsort(slab_rows // height, stable=True).astype(jnp.int32)  5.78 us
    sort x1, other arithmetic, slab_weights(): place = jnp.argsort(arranged).astype(jnp.int32)  5.77 us
  transfers between devices with their start and end apart: 37, of which 24 were waited for; matrix products, arithmetic and copies ran while one was open for 13% of the time, Pallas kernels for 5%

profile of v1, /device:TPU:0, one launch (start us, length us, event | category | flops | bytes accessed | tf_op | source)
XLA Modules:
  0.0 251.2 jit_solution(15945445430525288908)
XLA Ops:
  7.4 5.8 %sort.34 = (s32[4096]{0:T(1024)}, s32[4096]{0:T(1024)S(1)}) sort(s32[4096]{0:T(1024)S(1)} %add_select_fusion, s32[4096]{0:T(1024)S(1)} %iota.35), dimensions={0}, to_apply=%region_0.1 | sort | flops 49152 | bytes 65536 | tf_op jit(solution)/shard_map/jit(argsort)/sort | solution.py:154
  13.3 2.0 gather_fusion
  16.0 4.0 %collective-permute-start.14 = (f32[256,128]{1,0:T(8,128)S(1)}, f32[256,128]{1,0:T(8,128)S(1)}, u32[]{:S(2)}, u32[]{:S(2)}) collective-permute-start(f32[256,128]{1,0:T(8,128)S(1)} %gather_fusion.1), channel_id=1, source_target_pairs={{0,16},{16,0},{1,17},{17,1},{2,18},{18,2},{3,19},{19,3},{4,20},{20... | collective-permute-start | bytes 393224 | tf_op jit(solution)/shard_map/ppermute | solution.py:19
  20.0 3.5 %collective-permute-done.14 = f32[256,128]{1,0:T(8,128)S(1)} collective-permute-done((f32[256,128]{1,0:T(8,128)S(1)}, f32[256,128]{1,0:T(8,128)S(1)}, u32[]{:S(2)}, u32[]{:S(2)}) %collective-permute-start.14) | collective-permute-done | bytes 131104 | tf_op jit(solution)/shard_map/ppermute | solution.py:19
  23.6 2.8 %collective-permute-start.16 = (f32[2,256,128]{2,1,0:T(8,128)S(1)}, f32[2,256,128]{2,1,0:T(8,128)S(1)}, u32[]{:S(2)}, u32[]{:S(2)}) collective-permute-start(f32[2,256,128]{2,1,0:T(8,128)S(1)} %get-tuple-element.18), channel_id=1, source_target_pairs={{0,96},{32,0},{64,32},{96,64},{1,97},{33,1},{65,33},{97,65},{2,98}... | collective-permute-start | bytes 786440 | tf_op jit(solution)/shard_map/ppermute | solution.py:19
  26.4 2.3 collective-permute-start.17
  28.7 8.4 %collective-permute-done.16 = f32[2,256,128]{2,1,0:T(8,128)S(1)} collective-permute-done((f32[2,256,128]{2,1,0:T(8,128)S(1)}, f32[2,256,128]{2,1,0:T(8,128)S(1)}, u32[]{:S(2)}, u32[]{:S(2)}) %collective-permute-start.16) | collective-permute-done | bytes 262176 | tf_op jit(solution)/shard_map/ppermute | solution.py:19
  37.1 3.4 %collective-permute-done.15 = f32[2,256,128]{2,1,0:T(8,128)S(1)} collective-permute-done((f32[2,256,128]{2,1,0:T(8,128)S(1)}, f32[2,256,128]{2,1,0:T(8,128)S(1)}, u32[]{:S(2)}, u32[]{:S(2)}) %collective-permute-start.15) | collective-permute-done | bytes 262176 | tf_op jit(solution)/shard_map/ppermute | solution.py:19
  40.4 1.5 fusion.17
  42.0 3.0 %collective-permute-start.2 = (f32[3072,128]{1,0:T(8,128)S(1)}, f32[3072,128]{1,0:T(8,128)}, u32[]{:S(2)}, u32[]{:S(2)}) collective-permute-start(f32[3072,128]{1,0:T(8,128)S(1)} %copy-done.2), channel_id=1, source_target_pairs={{0,6},{2,0},{4,2},{6,4},{1,7},{3,1},{5,3},{7,5},{8,14},{10,8},{12,... | collective-permute-start | bytes 4718600 | tf_op jit(solution)/shard_map/ppermute | solution.py:19
  46.0 5.8 %sort.35 = (s32[4096]{0:T(1024)}, s32[4096]{0:T(1024)S(1)}) sort(s32[4096]{0:T(1024)S(1)} %get-tuple-element.7, s32[4096]{0:T(1024)S(1)} %iota.36), dimensions={0}, to_apply=%region_1.2 | sort | flops 49152 | bytes 65536 | tf_op jit(solution)/shard_map/jit(argsort)/sort | solution.py:155
  52.0 3.1 %pad_maximum_fusion = f32[2,4,2,256,128]{4,3,2,1,0:T(8,128)} fusion(f32[1,4,2,256,128]{4,3,2,1,0:T(8,128)} %bitcast.24, f32[1,4,2,256,128]{4,3,2,1,0:T(8,128)} %get-tuple-element.15), kind=kLoop, calls=%fused_computation.4 | loop fusion | flops 524288 | bytes 4194304 | tf_op jit(solution)/shard_map/stack | solution.py:161
  55.1 3.2 %gather_fusion.2 = f32[512,128]{1,0:T(8,128)} fusion(f32[4096,128]{1,0:T(8,128)} %bitcast.70, s32[1024]{0:T(1024)S(1)} %pad_clamp_fusion), kind=kCustom, calls=%fused_computation.2 | custom fusion | bytes 526336 | tf_op jit(solution)/shard_map/jit(_take)/gather | solution.py:170
  58.3 5.0 %all-to-all-start = ((f32[8,64,128]{2,1,0:T(8,128)}), f32[8,64,128]{2,1,0:T(8,128)S(1)}, u32[]{:S(2)}, u32[]{:S(2)}) async-start(f32[8,64,128]{2,1,0:T(8,128)} %bitcast.78), calls=%async_computation | async-start | bytes 524288 | tf_op jit(solution)/shard_map/all_to_all | solution.py:171
  63.4 22.6 %all-to-all-done = f32[8,64,128]{2,1,0:T(8,128)S(1)} async-done(((f32[8,64,128]{2,1,0:T(8,128)}), f32[8,64,128]{2,1,0:T(8,128)S(1)}, u32[]{:S(2)}, u32[]{:S(2)}) %all-to-all-start) | async-done | bytes 262176 | tf_op jit(solution)/shard_map/all_to_all | solution.py:171
  87.0 2.1 slice.49
  89.1 1.6 collective-permute-start.4
  92.4 7.3 %shard_map.64 = f32[256,384]{1,0:T(8,128)} custom-call(f32[3072,128]{1,0:T(8,128)} %refs_0_.4, f32[3072,128]{1,0:T(8,128)} %collective-permute-done.refs_1_, f32[3072,128]{1,0:T(8,128)} %refs_0_.5, f32[3072,128]{1,0:T(8,128)} %collective-permute-done.1.refs_3_.refs_1_, f32[3072,128]{1,0:T(8,128)} %collective-permute-done.2.refs_4_.refs_2_), custom_call_target="tpu_custom_call" | custom-call | flops 1811939328 | bytes 7864320 | tf_op jit(solution)/shard_map/pallas_call | solution.py:85
  99.7 8.2 %collective-permute-done.4.refs_3_.refs_4_ = f32[1536,128]{1,0:T(8,128)} collective-permute-done((f32[1536,128]{1,0:T(8,128)}, f32[1536,128]{1,0:T(8,128)}, u32[]{:S(2)}, u32[]{:S(2)}) %collective-permute-start.4) | collective-permute-done | bytes 786464 | tf_op jit(solution)/shard_map/ppermute | solution.py:19
  108.0 3.5 %collective-permute-done.3.refs_2_.refs_3_ = f32[1536,128]{1,0:T(8,128)S(1)} collective-permute-done((f32[1536,128]{1,0:T(8,128)S(1)}, f32[1536,128]{1,0:T(8,128)S(1)}, u32[]{:S(2)}, u32[]{:S(2)}) %collective-permute-start.3) | collective-permute-done | bytes 786464 | tf_op jit(solution)/shard_map/ppermute | solution.py:19
  112.4 5.9 %shard_map.65 = f32[256,128]{1,0:T(8,128)} custom-call(f32[3072,128]{1,0:T(8,128)} %refs_0_.4, f32[3072,128]{1,0:T(8,128)} %collective-permute-done.refs_1_, f32[1536,128]{1,0:T(8,128)} %copy-done.6, f32[1536,128]{1,0:T(8,128)} %collective-permute-done.4.refs_3_.refs_4_), custom_call_target="tpu_custom_call" | custom-call | flops 603979776 | bytes 4718592 | tf_op jit(solution)/shard_map/pallas_call | solution.py:85
  122.0 1.7 collective-permute-start.8
  123.7 1.5 collective-permute-start.7
  125.2 3.5 %collective-permute-done.6 = f32[32,512]{1,0:T(8,128)S(1)} collective-permute-done((f32[32,512]{1,0:T(8,128)S(1)}, f32[32,512]{1,0:T(8,128)S(1)}, u32[]{:S(2)}, u32[]{:S(2)}) %collective-permute-start.6) | collective-permute-done | bytes 65568 | tf_op jit(solution)/shard_map/ppermute | solution.py:19
  129.3 2.6 %collective-permute-start.9 = (f32[32,512]{1,0:T(8,128)S(1)}, f32[32,512]{1,0:T(8,128)S(1)}, u32[]{:S(2)}, u32[]{:S(2)}) collective-permute-start(f32[32,512]{1,0:T(8,128)S(1)} %fusion.7), channel_id=1, source_target_pairs={{0,16},{16,0},{1,17},{17,1},{2,18},{18,2},{3,19},{19,3},{4,20},{20... | collective-permute-start | bytes 196616 | tf_op jit(solution)/shard_map/ppermute | solution.py:19
  132.0 3.2 %collective-permute-done.9 = f32[32,512]{1,0:T(8,128)S(1)} collective-permute-done((f32[32,512]{1,0:T(8,128)S(1)}, f32[32,512]{1,0:T(8,128)S(1)}, u32[]{:S(2)}, u32[]{:S(2)}) %collective-permute-start.9) | collective-permute-done | bytes 65568 | tf_op jit(solution)/shard_map/ppermute | solution.py:19
  136.5 3.3 %collective-permute-done.10 = f32[32,512]{1,0:T(8,128)S(1)} collective-permute-done((f32[32,512]{1,0:T(8,128)S(1)}, f32[32,512]{1,0:T(8,128)S(1)}, u32[]{:S(2)}, u32[]{:S(2)}) %collective-permute-start.10) | collective-permute-done | bytes 65568 | tf_op jit(solution)/shard_map/ppermute | solution.py:19
  139.9 2.0 collective-permute-start.11
  141.9 2.9 %collective-permute-done.12 = f32[32,1024]{1,0:T(8,128)S(1)} collective-permute-done((f32[32,1024]{1,0:T(8,128)S(1)}, f32[32,1024]{1,0:T(8,128)S(1)}, u32[]{:S(2)}, u32[]{:S(2)}) %collective-permute-start.12) | collective-permute-done | bytes 131104 | tf_op jit(solution)/shard_map/ppermute | solution.py:19
  146.2 2.2 collective-permute-done.13
  149.2 2.9 %fusion.18 = f32[128,512]{1,0:T(8,128)S(1)} fusion(f32[128,1024]{1,0:T(8,128)} %bitcast.75, f32[512,1024]{1,0:T(8,128)} %all-gather.2.cloned.1.call-done), kind=kOutput, calls=%fused_computation.88 | convolution fusion | flops 402653184 | bytes 2883584 | tf_op jit(solution)/shard_map/dot_general | solution.py:235
  153.1 2.8 %collective-permute-start.20 = (f32[128,512]{1,0:T(8,128)S(1)}, f32[128,512]{1,0:T(8,128)S(1)}, u32[]{:S(2)}, u32[]{:S(2)}) collective-permute-start(f32[128,512]{1,0:T(8,128)S(1)} %fusion.18), channel_id=1, source_target_pairs={{0,96},{32,0},{64,32},{96,64},{1,97},{33,1},{65,33},{97,65},{2,98}... | collective-permute-start | bytes 786440 | tf_op jit(solution)/shard_map/ppermute | solution.py:19
  158.2 2.2 collective-permute-done.21
  160.4 3.0 %collective-permute-done.20 = f32[128,512]{1,0:T(8,128)S(1)} collective-permute-done((f32[128,512]{1,0:T(8,128)S(1)}, f32[128,512]{1,0:T(8,128)S(1)}, u32[]{:S(2)}, u32[]{:S(2)}) %collective-permute-start.20) | collective-permute-done | bytes 262176 | tf_op jit(solution)/shard_map/ppermute | solution.py:19
  163.5 1.6 fusion.16
  165.1 14.0 %collective-permute-done.23.refs_5_ = f32[1024,128]{1,0:T(8,128)} collective-permute-done((f32[1024,128]{1,0:T(8,128)S(1)}, f32[1024,128]{1,0:T(8,128)}, u32[]{:S(2)}, u32[]{:S(2)}) %collective-permute-start.23) | collective-permute-done | bytes 524320 | tf_op jit(solution)/shard_map/ppermute | solution.py:19
  179.8 2.5 %collective-permute-start.30 = (f32[1280,128]{1,0:T(8,128)}, f32[1280,128]{1,0:T(8,128)}, u32[]{:S(2)}, u32[]{:S(2)}) collective-permute-start(f32[1280,128]{1,0:T(8,128)} %collective-permute-done.24.refs_6_), channel_id=1, source_target_pairs={{0,6},{2,0},{4,2},{6,4},{1,7},{3,1},{5,3},{7,5},{8,14},{10,8},{12,... | collective-permute-start | bytes 1966088 | tf_op jit(solution)/shard_map/ppermute | solution.py:19
  182.4 3.2 %collective-permute-start.29 = (f32[1024,128]{1,0:T(8,128)}, f32[1024,128]{1,0:T(8,128)}, u32[]{:S(2)}, u32[]{:S(2)}) collective-permute-start(f32[1024,128]{1,0:T(8,128)} %collective-permute-done.23.refs_5_), channel_id=1, source_target_pairs={{0,6},{2,0},{4,2},{6,4},{1,7},{3,1},{5,3},{7,5},{8,14},{10,8},{12,... | collective-permute-start | bytes 1572872 | tf_op jit(solution)/shard_map/ppermute | solution.py:19
  185.6 9.9 %collective-permute-done.26.refs_8_ = f32[1024,128]{1,0:T(8,128)} collective-permute-done((f32[1024,128]{1,0:T(8,128)}, f32[1024,128]{1,0:T(8,128)}, u32[]{:S(2)}, u32[]{:S(2)}) %collective-permute-start.26) | collective-permute-done | bytes 524320 | tf_op jit(solution)/shard_map/ppermute | solution.py:19
  196.9 1.8 slice.53
  198.7 1.8 slice.52
  201.6 3.2 %collective-permute-start.33 = (f32[1280,128]{1,0:T(8,128)}, f32[1280,128]{1,0:T(8,128)}, u32[]{:S(2)}, u32[]{:S(2)}) collective-permute-start(f32[1280,128]{1,0:T(8,128)} %collective-permute-done.30.refs_12_), channel_id=1, source_target_pairs={{0,6},{2,0},{4,2},{6,4},{1,7},{3,1},{5,3},{7,5},{8,14},{10,8},{12,... | collective-permute-start | bytes 1966088 | tf_op jit(solution)/shard_map/ppermute | solution.py:19
  204.8 1.4 pad_maximum_fusion.1
  211.8 1.5 copy.10
  213.3 2.9 %copy.11.z_ref = f32[512,1024]{1,0:T(8,128)} copy(f32[512,1024]{0,1:T(8,128)} %bitcast.71) | data formatting | bytes 4194304 | tf_op jit(solution)/shard_map/reshape | solution.py:245
  217.1 4.2 %collective-permute-done.28.refs_10_ = f32[768,128]{1,0:T(8,128)S(1)} collective-permute-done((f32[768,128]{1,0:T(8,128)}, f32[768,128]{1,0:T(8,128)S(1)}, u32[]{:S(2)}, u32[]{:S(2)}) %collective-permute-start.28) | collective-permute-done | bytes 393248 | tf_op jit(solution)/shard_map/ppermute | solution.py:19
  221.3 4.2 %collective-permute-done.34.refs_16_ = f32[768,128]{1,0:T(8,128)S(1)} collective-permute-done((f32[768,128]{1,0:T(8,128)S(1)}, f32[768,128]{1,0:T(8,128)S(1)}, u32[]{:S(2)}, u32[]{:S(2)}) %collective-permute-start.34) | collective-permute-done | bytes 393248 | tf_op jit(solution)/shard_map/ppermute | solution.py:19
  226.3 18.1 %shard_map.66 = f32[512,3072]{1,0:T(8,128)} custom-call(f32[512,1024]{1,0:T(8,128)} %copy.11.z_ref, f32[3072,128]{1,0:T(8,128)} %refs_0_.5, f32[3072,128]{1,0:T(8,128)} %collective-permute-done.1.refs_3_.refs_1_, f32[3072,128]{1,0:T(8,128)} %collective-permute-done.2.refs_4_.refs_2_, f32[1536,128]{1,0:T(8,128)} %copy-done.6, ...), custom_call_target="tpu_custom_call" | custom-call | flops 9663676416 | bytes 18874368 | tf_op jit(solution)/shard_map/pallas_call | solution.py:133
  (111 shorter events, 28.0 us)
Async XLA Ops:
  6.5 8.7 %copy-start = (f32[3072,128]{1,0:T(8,128)S(1)}, f32[3072,128]{1,0:T(8,128)}, u32[]{:S(2)}) copy-start(f32[3072,128]{1,0:T(8,128)} %param.7) | copy-start | bytes 4718596
  16.0 26.0 %copy-start.2 = (f32[3072,128]{1,0:T(8,128)S(1)}, f32[3072,128]{1,0:T(8,128)}, u32[]{:S(2)}) copy-start(f32[3072,128]{1,0:T(8,128)} %refs_0_.5) | copy-start | bytes 4718596
  16.0 7.5 %collective-permute-start.14 = (f32[256,128]{1,0:T(8,128)S(1)}, f32[256,128]{1,0:T(8,128)S(1)}, u32[]{:S(2)}, u32[]{:S(2)}) collective-permute-start(f32[256,128]{1,0:T(8,128)S(1)} %gather_fusion.1), channel_id=1, source_target_pairs={{0,16},{16,0},{1,17},{17,1},{2,18},{18,2},{3,19},{19,3},{4,20},{20... | collective-permute-start | bytes 393224 | tf_op jit(solution)/shard_map/ppermute | solution.py:19
  23.6 13.5 %collective-permute-start.16 = (f32[2,256,128]{2,1,0:T(8,128)S(1)}, f32[2,256,128]{2,1,0:T(8,128)S(1)}, u32[]{:S(2)}, u32[]{:S(2)}) collective-permute-start(f32[2,256,128]{2,1,0:T(8,128)S(1)} %get-tuple-element.18), channel_id=1, source_target_pairs={{0,96},{32,0},{64,32},{96,64},{1,97},{33,1},{65,33},{97,65},{2,98}... | collective-permute-start | bytes 786440 | tf_op jit(solution)/shard_map/ppermute | solution.py:19
  26.4 14.0 %collective-permute-start.15 = (f32[2,256,128]{2,1,0:T(8,128)S(1)}, f32[2,256,128]{2,1,0:T(8,128)S(1)}, u32[]{:S(2)}, u32[]{:S(2)}) collective-permute-start(f32[2,256,128]{2,1,0:T(8,128)S(1)} %get-tuple-element.18), channel_id=1, source_target_pairs={{0,32},{32,64},{64,96},{96,0},{1,33},{33,65},{65,97},{97,1},{2,34}... | collective-permute-start | bytes 786440 | tf_op jit(solution)/shard_map/ppermute | solution.py:19
  26.4 14.0 %collective-permute-start.17 = (f32[2,256,128]{2,1,0:T(8,128)S(1)}, f32[2,256,128]{2,1,0:T(8,128)S(1)}, u32[]{:S(2)}, u32[]{:S(2)}) collective-permute-start(f32[2,256,128]{2,1,0:T(8,128)S(1)} %get-tuple-element.18), channel_id=1, source_target_pairs={{0,64},{32,96},{64,0},{96,32},{1,65},{33,97},{65,1},{97,33},{2,66}... | collective-permute-start | bytes 786440 | tf_op jit(solution)/shard_map/ppermute | solution.py:19
  42.0 10.0 %collective-permute-start.18 = (f32[4,2,256,128]{3,2,1,0:T(8,128)}, f32[4,2,256,128]{3,2,1,0:T(8,128)}, u32[]{:S(2)}, u32[]{:S(2)}) collective-permute-start(f32[4,2,256,128]{3,2,1,0:T(8,128)} %get-tuple-element.16), channel_id=1, source_target_pairs={{0,8},{8,0},{1,9},{9,1},{2,10},{10,2},{3,11},{11,3},{4,12},{12,4},... | collective-permute-start | bytes 3145736 | tf_op jit(solution)/shard_map/ppermute | solution.py:19
  42.0 45.0 %collective-permute-start.2 = (f32[3072,128]{1,0:T(8,128)S(1)}, f32[3072,128]{1,0:T(8,128)}, u32[]{:S(2)}, u32[]{:S(2)}) collective-permute-start(f32[3072,128]{1,0:T(8,128)S(1)} %copy-done.2), channel_id=1, source_target_pairs={{0,6},{2,0},{4,2},{6,4},{1,7},{3,1},{5,3},{7,5},{8,14},{10,8},{12,... | collective-permute-start | bytes 4718600 | tf_op jit(solution)/shard_map/ppermute | solution.py:19
  45.0 45.6 %collective-permute-start.1 = (f32[3072,128]{1,0:T(8,128)S(1)}, f32[3072,128]{1,0:T(8,128)}, u32[]{:S(2)}, u32[]{:S(2)}) collective-permute-start(f32[3072,128]{1,0:T(8,128)S(1)} %copy-done.2), channel_id=1, source_target_pairs={{0,2},{2,4},{4,6},{6,0},{1,3},{3,5},{5,7},{7,1},{8,10},{10,12},{12... | collective-permute-start | bytes 4718600 | tf_op jit(solution)/shard_map/ppermute | solution.py:19
  45.0 47.4 %collective-permute-start = (f32[3072,128]{1,0:T(8,128)}, f32[3072,128]{1,0:T(8,128)}, u32[]{:S(2)}, u32[]{:S(2)}) collective-permute-start(f32[3072,128]{1,0:T(8,128)} %refs_0_.4), channel_id=1, source_target_pairs={{0,1},{1,0},{2,3},{3,2},{4,5},{5,4},{6,7},{7,6},{8,9},{9,8},{10,11... | collective-permute-start | bytes 4718600 | tf_op jit(solution)/shard_map/ppermute | solution.py:19
  58.3 27.7 %all-to-all-start = ((f32[8,64,128]{2,1,0:T(8,128)}), f32[8,64,128]{2,1,0:T(8,128)S(1)}, u32[]{:S(2)}, u32[]{:S(2)}) async-start(f32[8,64,128]{2,1,0:T(8,128)} %bitcast.78), calls=%async_computation | async-start | bytes 524288 | tf_op jit(solution)/shard_map/all_to_all | solution.py:171
  63.3 85.9 %all-gather.2.cloned.1.call-start = ((), (), s32[]{:S(2)}) async-start(), calls=%async_computation.1 | async-start | bytes 2359296 | tf_op jit(solution)/shard_map/all_gather | solution.py:174
  89.1 18.9 %collective-permute-start.4 = (f32[1536,128]{1,0:T(8,128)}, f32[1536,128]{1,0:T(8,128)}, u32[]{:S(2)}, u32[]{:S(2)}) collective-permute-start(f32[1536,128]{1,0:T(8,128)} %slice.49), channel_id=1, source_target_pairs={{0,6},{2,0},{4,2},{6,4},{1,7},{3,1},{5,3},{7,5},{8,14},{10,8},{12,... | collective-permute-start | bytes 2359304 | tf_op jit(solution)/shard_map/ppermute | solution.py:19
  91.8 19.6 %collective-permute-start.3 = (f32[1536,128]{1,0:T(8,128)S(1)}, f32[1536,128]{1,0:T(8,128)S(1)}, u32[]{:S(2)}, u32[]{:S(2)}) collective-permute-start(f32[1536,128]{1,0:T(8,128)S(1)} %slice.48), channel_id=1, source_target_pairs={{0,2},{2,4},{4,6},{6,0},{1,3},{3,5},{5,7},{7,1},{8,10},{10,12},{12... | collective-permute-start | bytes 2359304 | tf_op jit(solution)/shard_map/ppermute | solution.py:19
  99.7 18.5 %copy-start.1 = (f32[256,384]{1,0:T(8,128)S(1)}, f32[256,384]{1,0:T(8,128)}, u32[]{:S(2)}) copy-start(f32[256,384]{1,0:T(8,128)} %shard_map.64) | copy-start | bytes 1179652
  111.5 0.9 copy-start.6
  118.2 1.8 copy-start.5
  118.2 3.0 %copy-start.7 = (f32[1024]{0:T(1024)S(1)}, f32[1024]{0:T(1024)}, u32[]{:S(2)}) copy-start(f32[1024]{0:T(1024)} %param.9) | copy-start | bytes 12292
  120.2 1.6 collective-permute-start.5
  121.9 6.8 %collective-permute-start.6 = (f32[32,512]{1,0:T(8,128)S(1)}, f32[32,512]{1,0:T(8,128)S(1)}, u32[]{:S(2)}, u32[]{:S(2)}) collective-permute-start(f32[32,512]{1,0:T(8,128)S(1)} %get-tuple-element.19), channel_id=1, source_target_pairs={{0,32},{32,64},{64,96},{96,0},{1,33},{33,65},{65,97},{97,1},{2,34}... | collective-permute-start | bytes 196616 | tf_op jit(solution)/shard_map/ppermute | solution.py:19
  122.0 6.7 %collective-permute-start.8 = (f32[32,512]{1,0:T(8,128)S(1)}, f32[32,512]{1,0:T(8,128)S(1)}, u32[]{:S(2)}, u32[]{:S(2)}) collective-permute-start(f32[32,512]{1,0:T(8,128)S(1)} %get-tuple-element.20), channel_id=1, source_target_pairs={{0,64},{32,96},{64,0},{96,32},{1,65},{33,97},{65,1},{97,33},{2,66}... | collective-permute-start | bytes 196616 | tf_op jit(solution)/shard_map/ppermute | solution.py:19
  123.7 5.6 %collective-permute-start.7 = (f32[32,512]{1,0:T(8,128)S(1)}, f32[32,512]{1,0:T(8,128)S(1)}, u32[]{:S(2)}, u32[]{:S(2)}) collective-permute-start(f32[32,512]{1,0:T(8,128)S(1)} %get-tuple-element.21), channel_id=1, source_target_pairs={{0,96},{32,0},{64,32},{96,64},{1,97},{33,1},{65,33},{97,65},{2,98}... | collective-permute-start | bytes 196616 | tf_op jit(solution)/shard_map/ppermute | solution.py:19
  129.3 5.8 %collective-permute-start.9 = (f32[32,512]{1,0:T(8,128)S(1)}, f32[32,512]{1,0:T(8,128)S(1)}, u32[]{:S(2)}, u32[]{:S(2)}) collective-permute-start(f32[32,512]{1,0:T(8,128)S(1)} %fusion.7), channel_id=1, source_target_pairs={{0,16},{16,0},{1,17},{17,1},{2,18},{18,2},{3,19},{19,3},{4,20},{20... | collective-permute-start | bytes 196616 | tf_op jit(solution)/shard_map/ppermute | solution.py:19
  135.5 20.5 %copy-start.3 = (f32[3072,128]{1,0:T(8,128)S(1)}, f32[3072,128]{1,0:T(8,128)}, u32[]{:S(2)}) copy-start(f32[3072,128]{1,0:T(8,128)} %refs_0_.5) | copy-start | bytes 4718596
  135.5 4.3 %collective-permute-start.10 = (f32[32,512]{1,0:T(8,128)S(1)}, f32[32,512]{1,0:T(8,128)S(1)}, u32[]{:S(2)}, u32[]{:S(2)}) collective-permute-start(f32[32,512]{1,0:T(8,128)S(1)} %fusion.5), channel_id=1, source_target_pairs={{0,1},{1,0},{2,3},{3,2},{4,5},{5,4},{6,7},{7,6},{8,9},{9,8},{10,11... | collective-permute-start | bytes 196616 | tf_op jit(solution)/shard_map/ppermute | solution.py:19
  139.8 5.0 %collective-permute-start.12 = (f32[32,1024]{1,0:T(8,128)S(1)}, f32[32,1024]{1,0:T(8,128)S(1)}, u32[]{:S(2)}, u32[]{:S(2)}) collective-permute-start(f32[32,1024]{1,0:T(8,128)S(1)} %get-tuple-element.23), channel_id=1, source_target_pairs={{0,6},{2,0},{4,2},{6,4},{1,7},{3,1},{5,3},{7,5},{8,14},{10,8},{12,... | collective-permute-start | bytes 393224 | tf_op jit(solution)/shard_map/ppermute | solution.py:19
  139.9 6.2 %collective-permute-start.11 = (f32[32,1024]{1,0:T(8,128)S(1)}, f32[32,1024]{1,0:T(8,128)S(1)}, u32[]{:S(2)}, u32[]{:S(2)}) collective-permute-start(f32[32,1024]{1,0:T(8,128)S(1)} %get-tuple-element.23), channel_id=1, source_target_pairs={{0,2},{2,4},{4,6},{6,0},{1,3},{3,5},{5,7},{7,1},{8,10},{10,12},{12... | collective-permute-start | bytes 393224 | tf_op jit(solution)/shard_map/ppermute | solution.py:19
  141.9 6.5 %collective-permute-start.13 = (f32[32,1024]{1,0:T(8,128)S(1)}, f32[32,1024]{1,0:T(8,128)S(1)}, u32[]{:S(2)}, u32[]{:S(2)}) collective-permute-start(f32[32,1024]{1,0:T(8,128)S(1)} %get-tuple-element.23), channel_id=1, source_target_pairs={{0,4},{2,6},{4,0},{6,2},{1,5},{3,7},{5,1},{7,3},{8,12},{10,14},{12... | collective-permute-start | bytes 393224 | tf_op jit(solution)/shard_map/ppermute | solution.py:19
  152.2 8.3 %collective-permute-start.21 = (f32[128,512]{1,0:T(8,128)S(1)}, f32[128,512]{1,0:T(8,128)S(1)}, u32[]{:S(2)}, u32[]{:S(2)}) collective-permute-start(f32[128,512]{1,0:T(8,128)S(1)} %fusion.18), channel_id=1, source_target_pairs={{0,64},{32,96},{64,0},{96,32},{1,65},{33,97},{65,1},{97,33},{2,66}... | collective-permute-start | bytes 786440 | tf_op jit(solution)/shard_map/ppermute | solution.py:19
  153.1 10.3 %collective-permute-start.20 = (f32[128,512]{1,0:T(8,128)S(1)}, f32[128,512]{1,0:T(8,128)S(1)}, u32[]{:S(2)}, u32[]{:S(2)}) collective-permute-start(f32[128,512]{1,0:T(8,128)S(1)} %fusion.18), channel_id=1, source_target_pairs={{0,96},{32,0},{64,32},{96,64},{1,97},{33,1},{65,33},{97,65},{2,98}... | collective-permute-start | bytes 786440 | tf_op jit(solution)/shard_map/ppermute | solution.py:19
  156.0 7.6 %collective-permute-start.19 = (f32[128,512]{1,0:T(8,128)S(1)}, f32[128,512]{1,0:T(8,128)S(1)}, u32[]{:S(2)}, u32[]{:S(2)}) collective-permute-start(f32[128,512]{1,0:T(8,128)S(1)} %fusion.18), channel_id=1, source_target_pairs={{0,32},{32,64},{64,96},{96,0},{1,33},{33,65},{65,97},{97,1},{2,34}... | collective-permute-start | bytes 786440 | tf_op jit(solution)/shard_map/ppermute | solution.py:19
  156.0 23.8 %collective-permute-start.24 = (f32[1280,128]{1,0:T(8,128)S(1)}, f32[1280,128]{1,0:T(8,128)}, u32[]{:S(2)}, u32[]{:S(2)}) collective-permute-start(f32[1280,128]{1,0:T(8,128)S(1)} %slice.37), channel_id=1, source_target_pairs={{0,1},{1,0},{2,3},{3,2},{4,5},{5,4},{6,7},{7,6},{8,9},{9,8},{10,11... | collective-permute-start | bytes 1966088 | tf_op jit(solution)/shard_map/ppermute | solution.py:19
  157.1 22.0 %collective-permute-start.23 = (f32[1024,128]{1,0:T(8,128)S(1)}, f32[1024,128]{1,0:T(8,128)}, u32[]{:S(2)}, u32[]{:S(2)}) collective-permute-start(f32[1024,128]{1,0:T(8,128)S(1)} %slice.36), channel_id=1, source_target_pairs={{0,1},{1,0},{2,3},{3,2},{4,5},{5,4},{6,7},{7,6},{8,9},{9,8},{10,11... | collective-permute-start | bytes 1572872 | tf_op jit(solution)/shard_map/ppermute | solution.py:19
  165.1 36.4 %collective-permute-start.22 = (f32[4,128,512]{2,1,0:T(8,128)}, f32[4,128,512]{2,1,0:T(8,128)}, u32[]{:S(2)}, u32[]{:S(2)}) collective-permute-start(f32[4,128,512]{2,1,0:T(8,128)} %get-tuple-element.14), channel_id=1, source_target_pairs={{0,8},{8,0},{1,9},{9,1},{2,10},{10,2},{3,11},{11,3},{4,12},{12,4},... | collective-permute-start | bytes 3145736 | tf_op jit(solution)/shard_map/ppermute | solution.py:19
  179.1 16.4 %collective-permute-start.26 = (f32[1024,128]{1,0:T(8,128)}, f32[1024,128]{1,0:T(8,128)}, u32[]{:S(2)}, u32[]{:S(2)}) collective-permute-start(f32[1024,128]{1,0:T(8,128)} %collective-permute-done.23.refs_5_), channel_id=1, source_target_pairs={{0,2},{2,4},{4,6},{6,0},{1,3},{3,5},{5,7},{7,1},{8,10},{10,12},{12... | collective-permute-start | bytes 1572872 | tf_op jit(solution)/shard_map/ppermute | solution.py:19
  179.8 21.7 %collective-permute-start.30 = (f32[1280,128]{1,0:T(8,128)}, f32[1280,128]{1,0:T(8,128)}, u32[]{:S(2)}, u32[]{:S(2)}) collective-permute-start(f32[1280,128]{1,0:T(8,128)} %collective-permute-done.24.refs_6_), channel_id=1, source_target_pairs={{0,6},{2,0},{4,2},{6,4},{1,7},{3,1},{5,3},{7,5},{8,14},{10,8},{12,... | collective-permute-start | bytes 1966088 | tf_op jit(solution)/shard_map/ppermute | solution.py:19
  182.4 28.1 %collective-permute-start.27 = (f32[1280,128]{1,0:T(8,128)}, f32[1280,128]{1,0:T(8,128)}, u32[]{:S(2)}, u32[]{:S(2)}) collective-permute-start(f32[1280,128]{1,0:T(8,128)} %collective-permute-done.24.refs_6_), channel_id=1, source_target_pairs={{0,2},{2,4},{4,6},{6,0},{1,3},{3,5},{5,7},{7,1},{8,10},{10,12},{12... | collective-permute-start | bytes 1966088 | tf_op jit(solution)/shard_map/ppermute | solution.py:19
  182.4 26.7 %collective-permute-start.29 = (f32[1024,128]{1,0:T(8,128)}, f32[1024,128]{1,0:T(8,128)}, u32[]{:S(2)}, u32[]{:S(2)}) collective-permute-start(f32[1024,128]{1,0:T(8,128)} %collective-permute-done.23.refs_5_), channel_id=1, source_target_pairs={{0,6},{2,0},{4,2},{6,4},{1,7},{3,1},{5,3},{7,5},{8,14},{10,8},{12,... | collective-permute-start | bytes 1572872 | tf_op jit(solution)/shard_map/ppermute | solution.py:19
  185.6 19.2 %copy-start.4 = (f32[1,4,128,512]{3,2,1,0:T(8,128)S(1)}, f32[1,4,128,512]{3,2,1,0:T(8,128)}, u32[]{:S(2)}) copy-start(f32[1,4,128,512]{3,2,1,0:T(8,128)} %get-tuple-element.13) | copy-start | bytes 3145732
  195.5 12.2 %collective-permute-start.25 = (f32[768,128]{1,0:T(8,128)S(1)}, f32[768,128]{1,0:T(8,128)}, u32[]{:S(2)}, u32[]{:S(2)}) collective-permute-start(f32[768,128]{1,0:T(8,128)S(1)} %slice.38), channel_id=1, source_target_pairs={{0,1},{1,0},{2,3},{3,2},{4,5},{5,4},{6,7},{7,6},{8,9},{9,8},{10,11... | collective-permute-start | bytes 1179656 | tf_op jit(solution)/shard_map/ppermute | solution.py:19
  201.5 14.7 %collective-permute-start.32 = (f32[1024,128]{1,0:T(8,128)}, f32[1024,128]{1,0:T(8,128)}, u32[]{:S(2)}, u32[]{:S(2)}) collective-permute-start(f32[1024,128]{1,0:T(8,128)} %collective-permute-done.26.refs_8_), channel_id=1, source_target_pairs={{0,2},{2,4},{4,6},{6,0},{1,3},{3,5},{5,7},{7,1},{8,10},{10,12},{12... | collective-permute-start | bytes 1572872 | tf_op jit(solution)/shard_map/ppermute | solution.py:19
  201.6 15.0 %collective-permute-start.33 = (f32[1280,128]{1,0:T(8,128)}, f32[1280,128]{1,0:T(8,128)}, u32[]{:S(2)}, u32[]{:S(2)}) collective-permute-start(f32[1280,128]{1,0:T(8,128)} %collective-permute-done.30.refs_12_), channel_id=1, source_target_pairs={{0,6},{2,0},{4,2},{6,4},{1,7},{3,1},{5,3},{7,5},{8,14},{10,8},{12,... | collective-permute-start | bytes 1966088 | tf_op jit(solution)/shard_map/ppermute | solution.py:19
  207.7 9.4 %collective-permute-start.31 = (f32[768,128]{1,0:T(8,128)}, f32[768,128]{1,0:T(8,128)S(1)}, u32[]{:S(2)}, u32[]{:S(2)}) collective-permute-start(f32[768,128]{1,0:T(8,128)} %slice.53), channel_id=1, source_target_pairs={{0,1},{1,0},{2,3},{3,2},{4,5},{5,4},{6,7},{7,6},{8,9},{9,8},{10,11... | collective-permute-start | bytes 1179656 | tf_op jit(solution)/shard_map/ppermute | solution.py:19
  209.0 12.2 %collective-permute-start.28 = (f32[768,128]{1,0:T(8,128)}, f32[768,128]{1,0:T(8,128)S(1)}, u32[]{:S(2)}, u32[]{:S(2)}) collective-permute-start(f32[768,128]{1,0:T(8,128)} %slice.52), channel_id=1, source_target_pairs={{0,1},{1,0},{2,3},{3,2},{4,5},{5,4},{6,7},{7,6},{8,9},{9,8},{10,11... | collective-permute-start | bytes 1179656 | tf_op jit(solution)/shard_map/ppermute | solution.py:19
  210.5 15.0 %collective-permute-start.34 = (f32[768,128]{1,0:T(8,128)S(1)}, f32[768,128]{1,0:T(8,128)S(1)}, u32[]{:S(2)}, u32[]{:S(2)}) collective-permute-start(f32[768,128]{1,0:T(8,128)S(1)} %slice.54), channel_id=1, source_target_pairs={{0,1},{1,0},{2,3},{3,2},{4,5},{5,4},{6,7},{7,6},{8,9},{9,8},{10,11... | collective-permute-start | bytes 1179656 | tf_op jit(solution)/shard_map/ppermute | solution.py:19
  217.1 8.4 %copy-start.8 = (f32[768,128]{1,0:T(8,128)}, f32[768,128]{1,0:T(8,128)S(1)}, u32[]{:S(2)}) copy-start(f32[768,128]{1,0:T(8,128)S(1)} %collective-permute-done.31.refs_13_) | copy-start | bytes 1179652
  221.3 4.2 %copy-start.9 = (f32[768,128]{1,0:T(8,128)}, f32[768,128]{1,0:T(8,128)S(1)}, u32[]{:S(2)}) copy-start(f32[768,128]{1,0:T(8,128)S(1)} %collective-permute-done.28.refs_10_) | copy-start | bytes 1179652
  225.5 0.8 copy-start.10
Sparse Core Ops, SparseCore 0:
  87.1 22.4 all-gather.1

commit v2 on v0

v2 whole, which is shorter than its diff:
```python
import jax
import jax.numpy as jnp
from jax import lax
from jax.experimental import pallas as pl
from jax.experimental.pallas import tpu as pltpu
from jax.sharding import Mesh
from jax.sharding import PartitionSpec as P

HARM = ("x", "zh", "c")
MODE = ("y", "zl")
SIZES = {"x": 4, "zh": 2, "c": 2, "y": 4, "zl": 2, ("zh", "zl"): 4}
regular = 0.01
TILE = 384
VMEM = 60 * 1024 * 1024


def shifted(array, axis, step):
    n = SIZES[axis]
    return lax.ppermute(array, axis, [(i, (i + step) % n) for i in range(n)])


def pick(parts, number):
    return lax.dynamic_index_in_dim(parts, number, 0, keepdims=False)


def slot_of(offset):
    return jnp.where(offset == 0, 0, jnp.where(offset == 3, 1, jnp.where(offset == 1, 2, 3)))


def ring_parts(array, axis):
    return [array, shifted(array, axis, 1), shifted(array, axis, -1), shifted(array, axis, 2)]


def split(value):
    high = value.astype(jnp.bfloat16)
    low = (value - high.astype(jnp.float32)).astype(jnp.bfloat16)
    return high, low


def three_pass(a, b, dims):
    a_high, a_low = a
    b_high, b_low = b
    def dot(p, q):
        return lax.dot_general(p, q, (dims, ((), ())), preferred_element_type=jnp.float32)
    return dot(a_high, b_high) + dot(a_high, b_low) + dot(a_low, b_high)


SMALL = pl.CostEstimate(flops=1000, bytes_accessed=1000, transcendentals=0)
ANY = pl.BlockSpec(memory_space=pl.ANY)
STEP = 384
PARAMS = pltpu.CompilerParams(vmem_limit_bytes=VMEM)


def rows_of(array, first, count, after=()):
    step = 3 * STEP
    start = first // step

    def body(source, *refs):
        refs[-1][...] = source[...]

    return pl.pallas_call(
        body,
        grid=(count // step,),
        in_specs=[pl.BlockSpec((step, 128), lambda i: (start + i, 0))] + [ANY] * len(after),
        out_specs=pl.BlockSpec((step, 128), lambda i: (i, 0)),
        out_shape=jax.ShapeDtypeStruct((count, 128), array.dtype),
        compiler_params=PARAMS,
        cost_estimate=SMALL,
    )(array, *after)


def held(array, after):
    def body(source, *refs):
        refs[-1][...] = source[...]

    return pl.pallas_call(
        body,
        in_specs=[pl.BlockSpec(memory_space=pltpu.VMEM)] + [ANY] * len(after),
        out_specs=pl.BlockSpec(memory_space=pltpu.VMEM),
        out_shape=jax.ShapeDtypeStruct(array.shape, array.dtype),
        cost_estimate=SMALL,
    )(array, *after)


def released(array, after):
    def body(*refs):
        pass

    return pl.pallas_call(
        body,
        in_specs=[ANY] * (1 + len(after)),
        out_specs=ANY,
        out_shape=jax.ShapeDtypeStruct(array.shape, array.dtype),
        input_output_aliases={0: 0},
        cost_estimate=SMALL,
    )(array, *after)


def x_parts(kept, came):
    def body(kept_ref, came_ref, *refs):
        x = lax.axis_index("x")
        for ref, offset in zip(refs[-4:], (0, 1, 3, 2), strict=True):
            share = lax.rem(x + offset, 4)
            ref[...] = kept_ref[share] + came_ref[share]

    return pl.pallas_call(
        body,
        in_specs=[pl.BlockSpec(kept.shape, lambda: (0, 0, 0))] * 2,
        out_shape=[jax.ShapeDtypeStruct(kept.shape[1:], kept.dtype)] * 4,
        compiler_params=PARAMS,
        cost_estimate=SMALL,
    )(kept, came)


def cot_ready(own, other):
    rows = own.shape[0]

    def body(own_ref, other_ref, high, low):
        high[...], low[...] = split(jnp.concatenate([own_ref[...].T, other_ref[...].T], axis=0))

    shape = jax.ShapeDtypeStruct((256, rows), jnp.bfloat16)
    return pl.pallas_call(
        body,
        grid=(rows // STEP,),
        in_specs=[pl.BlockSpec((STEP, 128), lambda i: (i, 0))] * 2,
        out_specs=[pl.BlockSpec((256, STEP), lambda i: (0, i))] * 2,
        out_shape=[shape, shape],
        compiler_params=PARAMS,
        cost_estimate=SMALL,
    )(own, other)


def wide(ref):
    return jnp.concatenate([ref[k] for k in range(4)], axis=1)


def gram_shares(cot, whole_x, cut, after):
    rows = whole_x.shape[1]
    steps, start = rows // STEP, cut // STEP

    def body(cot_high, cot_low, x_ref, *refs):
        kept, sent, tail, total = refs[-4:]
        step = pl.program_id(0)
        c, zl = lax.axis_index("c"), lax.axis_index("zl")

        @pl.when(step == 0)
        def _():
            total[...] = jnp.zeros_like(total)

        total[...] += three_pass((cot_high[...], cot_low[...]), split(wide(x_ref)), ((1,), (0,)))

        @pl.when(step >= start)
        def _():
            tail[...] = x_ref[...]

        @pl.when(step == steps - 1)
        def _():
            for s in range(4):
                for ref, core in ((kept, c), (sent, 1 - c)):
                    row = pl.multiple_of(lax.rem(s * 64 + core * 32 + 128 * zl, 256), 32)
                    ref[s] = total[pl.ds(row, 32), :]

    shape = jax.ShapeDtypeStruct((4, 32, 512), jnp.float32)
    whole = pl.BlockSpec((4, 32, 512), lambda i: (0, 0, 0))
    return pl.pallas_call(
        body,
        grid=(steps,),
        in_specs=[pl.BlockSpec((256, STEP), lambda i: (0, i))] * 2
        + [pl.BlockSpec((4, STEP, 128), lambda i: (0, i, 0))]
        + [ANY] * len(after),
        out_specs=[whole, whole, pl.BlockSpec((4, STEP, 128), lambda i: (0, jnp.maximum(i - start, 0), 0))],
        out_shape=[shape, shape, jax.ShapeDtypeStruct((4, rows - cut, 128), jnp.float32)],
        scratch_shapes=[pltpu.VMEM((256, 512), jnp.float32)],
        compiler_params=PARAMS,
        cost_estimate=SMALL,
    )(*cot, whole_x, *after)


def z_part(weighted, own, other):
    share, depth = own[0].shape

    def body(*refs):
        weighted_refs, own_refs, other_refs = refs[:4], refs[4:8], refs[8:12]
        out, tall, rows = refs[-3:]
        x, c, y = lax.axis_index("x"), lax.axis_index("c"), lax.axis_index("y")
        for slot, offset in enumerate((0, 3, 1, 2)):
            tall[pl.ds(pl.multiple_of(lax.rem(y + offset, 4) * 32, 32), 32), :] = weighted_refs[slot][...]
            source = lax.rem(x + offset, 4)
            for which, value in ((c, own_refs[slot][...]), (1 - c, other_refs[slot][...])):
                rows[pl.ds(pl.multiple_of((source * 2 + which) * share, share), share), :] = value
        out[...] = three_pass(split(tall[...]), split(rows[...]), ((1,), (1,)))

    return pl.pallas_call(
        body,
        out_shape=jax.ShapeDtypeStruct((128, 8 * share), jnp.float32),
        scratch_shapes=[pltpu.VMEM((128, depth), jnp.float32), pltpu.VMEM((8 * share, depth), jnp.float32)],
        compiler_params=PARAMS,
        cost_estimate=SMALL,
    )(*weighted, *own, *other)


def z_ready(own_z, other_z):
    depth, height = 1024, own_z[0].shape[1]

    def body(*refs):
        sets, (z_high, z_low, z_tall) = (refs[:4], refs[4:8]), refs[8:]
        x, c, zl = lax.axis_index("x"), lax.axis_index("c"), lax.axis_index("zl")
        for slot, offset in enumerate((0, 3, 1, 2)):
            source = lax.rem(x + offset, 4)
            side = lax.rem(source // 2 + zl, 2)
            for part in range(4):
                for which, held in ((c, sets[0]), (1 - c, sets[1])):
                    row = side * 512 + part * 128 + lax.rem(source, 2) * 64 + which * 32
                    z_tall[pl.ds(pl.multiple_of(row, 32), 32), :] = held[slot][part * 32 : part * 32 + 32, :]
        for part in range(depth // 128):
            cols = slice(part * 128, part * 128 + 128)
            z_high[:, cols], z_low[:, cols] = split(z_tall[cols, :].T)

    shape = jax.ShapeDtypeStruct((height, depth), jnp.bfloat16)
    return pl.pallas_call(
        body,
        out_shape=[shape, shape],
        scratch_shapes=[pltpu.VMEM((depth, height), jnp.float32)],
        compiler_params=PARAMS,
        cost_estimate=SMALL,
    )(*own_z, *other_z)


def slab_part(z, own_x, own_first, other_x, slab, first, count, total):
    steps = count // STEP
    own_start, start = own_first // STEP, first // STEP
    height, depth = z[0].shape

    def body(z_high, z_low, own_ref, other_ref, *refs):
        x_tile = split(jnp.concatenate([wide(own_ref), wide(other_ref)], axis=1))
        refs[-1][...] = three_pass((z_high[...], z_low[...]), x_tile, ((1,), (1,)))

    return pl.pallas_call(
        body,
        grid=(steps,),
        in_specs=[pl.BlockSpec((height, depth), lambda i: (0, 0))] * 2
        + [
            pl.BlockSpec((4, STEP, 128), lambda i: (0, own_start + i, 0)),
            pl.BlockSpec((4, STEP, 128), lambda i: (0, i, 0)),
        ]
        + ([] if slab is None else [ANY]),
        out_specs=pl.BlockSpec((height, STEP), lambda i: (0, start + i)),
        out_shape=jax.ShapeDtypeStruct((height, total), jnp.float32),
        input_output_aliases={} if slab is None else {4: 0},
        compiler_params=PARAMS,
        cost_estimate=SMALL,
    )(*z, own_x, other_x, *([] if slab is None else [slab]))


def places(slab_rows, height, count):
    total = slab_rows.shape[0]
    kinds = total // count
    block_of = slab_rows // height
    member = (block_of[:, None] == jnp.arange(kinds)[None, :]).astype(jnp.float32).reshape(-1, 128, kinds)
    before = jnp.tril(jnp.ones((128, 128), jnp.float32), -1)
    within = jnp.einsum("ab,cbh->cah", before, member, preferred_element_type=jnp.float32)
    chunks = member.shape[0]
    sums = member.sum(1)
    ahead = jnp.dot(jnp.tril(jnp.ones((chunks, chunks), jnp.float32), -1), sums, preferred_element_type=jnp.float32)
    rank = ((within + ahead[:, None, :]) * member).sum(2).reshape(total)
    return block_of * count + rank.astype(jnp.int32)


def slab_weights(weights, slab_rows, x, zh, c):
    height = weights.shape[0]
    total = slab_rows.shape[0]
    count = total // 16
    harm = (x * 2 + zh) * 2 + c
    place = places(slab_rows, height, count)
    ids = harm * count + jnp.arange(count, dtype=jnp.int32)
    own = jnp.where(place[None, :] == ids[:, None], slab_rows[None, :] - harm * height, 0).sum(1)
    rows = jnp.take(weights, own, axis=0, mode="clip")
    pair = jnp.stack([rows, shifted(rows, "zh", 1)])
    ring = jnp.stack(ring_parts(pair, "x"))
    every = jnp.stack([ring, shifted(ring, "c", 1)])
    every = every.reshape(-1, 128)
    share = total // 8 // 8
    wanted = lax.dynamic_slice_in_dim(place.reshape(8, 8, share), x * 2 + c, 1, axis=1).reshape(-1)
    source, row = wanted // count, wanted % count
    source_x, source_zh, source_c = source // 4, (source // 2) % 2, source % 2
    held = (
        ((source_c != c) * 4 + slot_of((source_x - x) % 4)) * 2 + (source_zh != zh)
    ) * count + row
    return jnp.take(every, held, axis=0, mode="clip").reshape(8, share, 128)


def slab_share(chosen, zl):
    share = chosen.shape[1]
    came = lax.all_to_all(chosen, MODE, 0, 0, tiled=True).reshape(4, 2, share, 128)
    came = jnp.where(zl == 0, came, came[:, ::-1])
    return came.transpose(2, 1, 0, 3).reshape(share, 1024)


def local(mode_vectors, weights, cotangent, eigenvalues, eigen_cotangent, slab_rows):
    x, zh, c, y, zl = (lax.axis_index(a) for a in ("x", "zh", "c", "y", "zl"))
    rows = mode_vectors.shape[0]
    cut = rows * 3 // 4
    own_x = lax.all_gather(mode_vectors, "y")
    other_cot = shifted(cotangent, "zl", 1)
    chosen = slab_weights(weights, slab_rows, x, zh, c)
    share = slab_share(held(chosen, (other_cot,)), zl)
    other_rows = shifted(rows_of(mode_vectors, 0, cut, (other_cot, share)), "zl", 1)
    own_share = ring_parts(share, "x")
    other_share = [shifted(part, "c", 1) for part in own_share]
    cot = cot_ready(cotangent, other_cot)

    kept, sent, tail = gram_shares(cot, own_x, cut, own_share)
    other_low = lax.all_gather(rows_of(other_rows, 0, cut, (kept,)), "y")
    to_self, to_above, to_below, to_far = x_parts(kept, shifted(sent, "c", 1))
    total = to_self + shifted(to_above, "x", 1) + shifted(to_below, "x", -1) + shifted(to_far, "x", 2)
    own, below, above, far = ring_parts(total, ("zh", "zl"))
    total = jnp.concatenate([own + far, below + above], axis=1)
    j_first = (y * 2 + x // 2) * 128 + ((x % 2) * 2 + c) * 32
    eigen_j = lax.dynamic_slice_in_dim(eigenvalues, j_first, 32)
    slope_j = lax.dynamic_slice_in_dim(eigen_cotangent, j_first, 32)
    sides = eigenvalues.reshape(4, 2, 128).transpose(1, 0, 2).reshape(2, 512)
    eigen_i = jnp.where(zl == 0, sides, sides[::-1]).reshape(1024)
    differ = eigen_j[:, None] - eigen_i[None]
    factor = differ / (differ * differ + regular)
    j_ids = j_first + lax.broadcasted_iota(jnp.int32, (32, 1024), 0)
    col = lax.broadcasted_iota(jnp.int32, (32, 1024), 1)
    i_ids = (col % 512 // 128 * 2 + (zl + col // 512) % 2) * 128 + col % 128
    weighted = factor * total + jnp.where(j_ids == i_ids, slope_j[:, None], 0.0)

    other_high = shifted(released(tail, (weighted,)), "zl", 1)
    z_own = ring_parts(z_part(ring_parts(weighted, "y"), own_share, other_share), "x")
    z_other = [shifted(part, "c", 1) for part in z_own]
    z = z_ready(z_own, z_other)
    slab = slab_part(z, own_x, 0, other_low, None, 0, cut, rows)
    return slab_part(z, own_x, cut, other_high, slab, cut, rows - cut, rows)


def solution(mesh):
    torus = Mesh(mesh.devices.reshape(4, 2, 2, 4, 2), ("x", "zh", "c", "y", "zl"))
    return jax.shard_map(
        local,
        mesh=torus,
        in_specs=(P(HARM, MODE), P(HARM, MODE), P(HARM, MODE), P(), P(), P()),
        out_specs=P(MODE, HARM),
        check_vma=False,
    )
```

time: 409 us -> 202 us (0.49)
  waiting for transfers between devices: 216 us -> 74 us
  matrix products: 70 us -> 0.49 us
  Pallas kernels: 0 us -> 52.4 us
  blocking collectives: 48.2 us -> 0 us
  local copies, waits for them, and re-layouts: 41.6 us -> 12.8 us
  starting transfers between devices: 11.2 us -> 38.9 us
    all_gather x3 -> x2, waiting for transfers between devices: 193 us -> 0.01 us  [the longest x1 0.01 us: local(): own_x = lax.all_gather(mode_vectors, 'y')]
    dot_general x3 -> x2, matrix products: 70 us -> 0.49 us  [the longest x1 0.3 us: places(): jnp.einsum('ab,cbh->cah', before, member, preferred_element_type=jnp.floa...]
    ppermute x0 -> x32, waiting for transfers between devices: none -> 63.8 us  [shifted(): return lax.ppermute(array, axis, [(i, (i + step) % n) for i in range(n)])]
    pallas_call x0 -> x11, Pallas kernels: none -> 52.4 us  [the longest x2 20.6 us: slab_part(): pl.pallas_call(body, grid=(steps,), in_specs=[pl.BlockSpec((height, depth...]
    all_to_all x2 -> x0, blocking collectives: 48.2 us -> none  [the longest x1 31.2 us: local(): lax.all_to_all(ordered_z, MODE, split_axis=0, concat_axis=1, tiled=True)]
    ppermute x0 -> x32, starting transfers between devices: none -> 34 us  [shifted(): return lax.ppermute(array, axis, [(i, (i + step) % n) for i in range(n)])]
    gather x4 -> x2, local copies, waits for them, and re-layouts: 22.5 us -> 3.95 us  [the longest x1 3.22 us: slab_weights(): return jnp.take(every, held, axis=0, mode='clip').reshape(8, share, 128)]
    scatter x1 -> x0, local copies, waits for them, and re-layouts: 15.5 us -> none  [local(): inverse = jnp.zeros((total_rows,), jnp.int32).at[arranged].set(jnp.arange...]
  transfers between devices with their start and end apart: 5 -> 35, of which waited for: 5 -> 22; matrix products, arithmetic and copies ran while one was open for 7% -> 7% of each run, Pallas kernels for 0% -> 22%
where the time goes in v2:
time: 202 us; the launch traced here: 200 us
  waiting for transfers between devices  74 us (37%)
  Pallas kernels  52.4 us (26%)
  starting transfers between devices  38.9 us (19%)
  between operations  13.8 us (7%)
  local copies, waits for them, and re-layouts  12.8 us (6%)
  other arithmetic  8 us (4%)
    ppermute x32, waiting for transfers between devices, shifted(): return lax.ppermute(array, axis, [(i, (i + step) % n) for i in range(n)])  63.8 us
    ppermute x32, starting transfers between devices, shifted(): return lax.ppermute(array, axis, [(i, (i + step) % n) for i in range(n)])  34 us
    pallas_call x2, Pallas kernels, slab_part(): pl.pallas_call(body, grid=(steps,), in_specs=[pl.BlockSpec((height, depth...  20.6 us
    pallas_call x1, Pallas kernels, gram_shares(): pl.pallas_call(body, grid=(steps,), in_specs=[pl.BlockSpec((256, STEP), l...  9.71 us
    all_to_all x1, waiting for transfers between devices, slab_share(): lax.all_to_all(chosen, MODE, 0, 0, tiled=True).reshape(4, 2, share, 128)  9.49 us
    pallas_call x1, Pallas kernels, cot_ready(): pl.pallas_call(body, grid=(rows // STEP,), in_specs=[pl.BlockSpec((STEP,...  6.94 us
    unnamed x53, local copies, waits for them, and re-layouts  6.69 us
    all_to_all x1, starting transfers between devices, slab_share(): lax.all_to_all(chosen, MODE, 0, 0, tiled=True).reshape(4, 2, share, 128)  4.88 us
  transfers between devices with their start and end apart: 35, of which 22 were waited for; matrix products, arithmetic and copies ran while one was open for 7% of the time, Pallas kernels for 22%

profile of v2, /device:TPU:0, one launch (start us, length us, event | category | flops | bytes accessed | tf_op | source)
XLA Modules:
  0.0 200.3 jit_solution(6470406299942972843)
XLA Ops:
  10.1 4.0 %collective-permute-start.1 = (f32[256,128]{1,0:T(8,128)S(1)}, f32[256,128]{1,0:T(8,128)S(1)}, u32[]{:S(2)}, u32[]{:S(2)}) collective-permute-start(f32[256,128]{1,0:T(8,128)S(1)} %gather_fusion), channel_id=1, source_target_pairs={{0,16},{16,0},{1,17},{17,1},{2,18},{18,2},{3,19},{19,3},{4,20},{20... | collective-permute-start | bytes 393224 | tf_op jit(solution)/shard_map/ppermute | solution.py:19
  14.1 3.5 %collective-permute-done.1 = f32[256,128]{1,0:T(8,128)S(1)} collective-permute-done((f32[256,128]{1,0:T(8,128)S(1)}, f32[256,128]{1,0:T(8,128)S(1)}, u32[]{:S(2)}, u32[]{:S(2)}) %collective-permute-start.1) | collective-permute-done | bytes 131104 | tf_op jit(solution)/shard_map/ppermute | solution.py:19
  17.6 2.8 %collective-permute-start.3 = (f32[2,256,128]{2,1,0:T(8,128)S(1)}, f32[2,256,128]{2,1,0:T(8,128)S(1)}, u32[]{:S(2)}, u32[]{:S(2)}) collective-permute-start(f32[2,256,128]{2,1,0:T(8,128)S(1)} %get-tuple-element.30), channel_id=1, source_target_pairs={{0,96},{32,0},{64,32},{96,64},{1,97},{33,1},{65,33},{97,65},{2,98}... | collective-permute-start | bytes 786440 | tf_op jit(solution)/shard_map/ppermute | solution.py:19
  20.5 2.3 %collective-permute-start.4 = (f32[2,256,128]{2,1,0:T(8,128)S(1)}, f32[2,256,128]{2,1,0:T(8,128)S(1)}, u32[]{:S(2)}, u32[]{:S(2)}) collective-permute-start(f32[2,256,128]{2,1,0:T(8,128)S(1)} %get-tuple-element.30), channel_id=1, source_target_pairs={{0,64},{32,96},{64,0},{96,32},{1,65},{33,97},{65,1},{97,33},{2,66}... | collective-permute-start | bytes 786440 | tf_op jit(solution)/shard_map/ppermute | solution.py:19
  22.8 1.3 collective-permute-start
  24.0 7.1 %collective-permute-done.3 = f32[2,256,128]{2,1,0:T(8,128)S(1)} collective-permute-done((f32[2,256,128]{2,1,0:T(8,128)S(1)}, f32[2,256,128]{2,1,0:T(8,128)S(1)}, u32[]{:S(2)}, u32[]{:S(2)}) %collective-permute-start.3) | collective-permute-done | bytes 262176 | tf_op jit(solution)/shard_map/ppermute | solution.py:19
  31.1 3.4 %collective-permute-done.2 = f32[2,256,128]{2,1,0:T(8,128)S(1)} collective-permute-done((f32[2,256,128]{2,1,0:T(8,128)S(1)}, f32[2,256,128]{2,1,0:T(8,128)S(1)}, u32[]{:S(2)}, u32[]{:S(2)}) %collective-permute-start.2) | collective-permute-done | bytes 262176 | tf_op jit(solution)/shard_map/ppermute | solution.py:19
  34.5 1.5 fusion.51
  36.3 2.7 %collective-permute-done.5 = f32[4,2,256,128]{3,2,1,0:T(8,128)} collective-permute-done((f32[4,2,256,128]{3,2,1,0:T(8,128)}, f32[4,2,256,128]{3,2,1,0:T(8,128)}, u32[]{:S(2)}, u32[]{:S(2)}) %collective-permute-start.5) | collective-permute-done | bytes 1048608 | tf_op jit(solution)/shard_map/ppermute | solution.py:19
  39.1 3.1 %pad_maximum_fusion = f32[2,4,2,256,128]{4,3,2,1,0:T(8,128)} fusion(f32[1,4,2,256,128]{4,3,2,1,0:T(8,128)} %bitcast.17, f32[1,4,2,256,128]{4,3,2,1,0:T(8,128)} %get-tuple-element.27), kind=kLoop, calls=%fused_computation.3 | loop fusion | flops 524288 | bytes 4194304 | tf_op jit(solution)/shard_map/stack | solution.py:280
  42.1 3.2 %gather_fusion.1 = f32[512,128]{1,0:T(8,128)} fusion(f32[4096,128]{1,0:T(8,128)} %bitcast.43, s32[1024]{0:T(1024)S(1)} %pad_clamp_fusion), kind=kCustom, calls=%fused_computation.1 | custom fusion | bytes 526336 | tf_op jit(solution)/shard_map/jit(_take)/gather | solution.py:289
  45.3 12.4 %collective-permute-done.other_ref.refs_0_ = f32[3072,128]{1,0:T(8,128)S(1)} collective-permute-done((f32[3072,128]{1,0:T(8,128)}, f32[3072,128]{1,0:T(8,128)S(1)}, u32[]{:S(2)}, u32[]{:S(2)}) %collective-permute-start) | collective-permute-done | bytes 1572896 | tf_op jit(solution)/shard_map/ppermute | solution.py:19
  57.7 1.1 copy-done.1
  58.8 1.7 shard_map.65
  60.5 4.9 %all-to-all-start = ((f32[8,64,128]{2,1,0:T(8,128)}), f32[8,64,128]{2,1,0:T(8,128)S(1)}, u32[]{:S(2)}, u32[]{:S(2)}) async-start(f32[8,64,128]{2,1,0:T(8,128)} %shard_map.65), calls=%async_computation | async-start | bytes 524288 | tf_op jit(solution)/shard_map/all_to_all | solution.py:294
  65.4 9.5 %all-to-all-done = f32[8,64,128]{2,1,0:T(8,128)S(1)} async-done(((f32[8,64,128]{2,1,0:T(8,128)}), f32[8,64,128]{2,1,0:T(8,128)S(1)}, u32[]{:S(2)}, u32[]{:S(2)}) %all-to-all-start) | async-done | bytes 262176 | tf_op jit(solution)/shard_map/all_to_all | solution.py:294
  76.0 2.2 %shard_map.71 = f32[2304,128]{1,0:T(8,128)} custom-call(f32[3072,128]{1,0:T(8,128)} %source.1, f32[3072,128]{1,0:T(8,128)} %copy-done.1, f32[64,1024]{1,0:T(8,128)} %reshape.364.refs_0_.refs_4_.refs_1_), custom_call_target="tpu_custom_call" | custom-call | flops 1000 | bytes 1000 | tf_op jit(solution)/shard_map/pallas_call | solution.py:61
  78.1 1.5 collective-permute-start.31
  79.6 1.6 collective-permute-start.8
  81.2 2.9 %collective-permute-start.7 = (f32[64,1024]{1,0:T(8,128)S(1)}, f32[64,1024]{1,0:T(8,128)S(1)}, u32[]{:S(2)}, u32[]{:S(2)}) collective-permute-start(f32[64,1024]{1,0:T(8,128)S(1)} %copy-done.2), channel_id=1, source_target_pairs={{0,96},{32,0},{64,32},{96,64},{1,97},{33,1},{65,33},{97,65},{2,98}... | collective-permute-start | bytes 786440 | tf_op jit(solution)/shard_map/ppermute | solution.py:19
  84.1 6.9 %shard_map.64 = (bf16[256,3072]{1,0:T(8,128)(2,1)}, bf16[256,3072]{1,0:T(8,128)(2,1)}) custom-call(f32[3072,128]{1,0:T(8,128)} %own_ref.1, f32[3072,128]{1,0:T(8,128)} %copy-done.1), custom_call_target="tpu_custom_call" | custom-call | flops 1000 | bytes 1000 | tf_op jit(solution)/shard_map/pallas_call | solution.py:122
  92.4 9.7 %shard_map.66 = (f32[4,32,512]{2,1,0:T(8,128)}, f32[4,32,512]{2,1,0:T(8,128)}, f32[4,768,128]{2,1,0:T(8,128)}) custom-call(bf16[256,3072]{1,0:T(8,128)(2,1)} %get-tuple-element.16.cot_high, bf16[256,3072]{1,0:T(8,128)(2,1)} %get-tuple-element.17.cot_low, f32[4,3072,128]{2,1,0:T(8,128)} %bitcast.40, f32[64,1024]{1,0:T(8,128)} %reshape.364.refs_0_.refs_4_.refs_1_, ...), custom_call_target="tpu_custom_call" | custom-call | flops 1000 | bytes 1000 | tf_op jit(solution)/shard_map/pallas_call | solution.py:165
  102.2 1.0 copy-done.6
  103.2 2.1 %shard_map.72 = f32[2304,128]{1,0:T(8,128)} custom-call(f32[2304,128]{1,0:T(8,128)} %copy-done.6, f32[4,32,512]{2,1,0:T(8,128)} %get-tuple-element.18.kept_ref.refs_0_), custom_call_target="tpu_custom_call" | custom-call | flops 1000 | bytes 1000 | tf_op jit(solution)/shard_map/pallas_call | solution.py:61
  107.8 1.7 shard_map.67
  109.6 1.8 collective-permute-start.10
  111.4 1.4 collective-permute-start.11
  112.8 0.9 collective-permute-start.12
  113.7 1.5 collective-permute-done.10
  115.3 1.0 collective-permute-done.11
  116.3 2.5 %collective-permute-done.12 = f32[32,512]{1,0:T(8,128)S(1)} collective-permute-done((f32[32,512]{1,0:T(8,128)}, f32[32,512]{1,0:T(8,128)S(1)}, u32[]{:S(2)}, u32[]{:S(2)}) %collective-permute-start.12) | collective-permute-done | bytes 65568 | tf_op jit(solution)/shard_map/ppermute | solution.py:19
  118.8 0.9 add_add_fusion
  119.7 3.9 %collective-permute-start.15 = (f32[32,512]{1,0:T(8,128)S(1)}, f32[32,512]{1,0:T(8,128)S(1)}, u32[]{:S(2)}, u32[]{:S(2)}) collective-permute-start(f32[32,512]{1,0:T(8,128)S(1)} %add_add_fusion), channel_id=1, source_target_pairs={{0,17},{1,0},{16,1},{17,16},{2,19},{3,2},{18,3},{19,18},{4,21},{5,... | collective-permute-start | bytes 196616 | tf_op jit(solution)/shard_map/ppermute | solution.py:19
  123.6 1.8 collective-permute-start.13
  125.4 4.1 %collective-permute-done.13 = f32[32,512]{1,0:T(8,128)S(1)} collective-permute-done((f32[32,512]{1,0:T(8,128)S(1)}, f32[32,512]{1,0:T(8,128)S(1)}, u32[]{:S(2)}, u32[]{:S(2)}) %collective-permute-start.13) | collective-permute-done | bytes 65568 | tf_op jit(solution)/shard_map/ppermute | solution.py:19
  131.8 0.9 collective-permute-done.19.refs_8_
  133.2 2.7 %collective-permute-start.17 = (f32[32,1024]{1,0:T(8,128)S(1)}, f32[32,1024]{1,0:T(8,128)S(1)}, u32[]{:S(2)}, u32[]{:S(2)}) collective-permute-start(f32[32,1024]{1,0:T(8,128)S(1)} %copy-done.5), channel_id=1, source_target_pairs={{0,6},{2,0},{4,2},{6,4},{1,7},{3,1},{5,3},{7,5},{8,14},{10,8},{12,... | collective-permute-start | bytes 393224 | tf_op jit(solution)/shard_map/ppermute | solution.py:19
  135.9 7.4 %collective-permute-done.18.refs_3_ = f32[32,1024]{1,0:T(8,128)S(1)} collective-permute-done((f32[32,1024]{1,0:T(8,128)S(1)}, f32[32,1024]{1,0:T(8,128)S(1)}, u32[]{:S(2)}, u32[]{:S(2)}) %collective-permute-start.18) | collective-permute-done | bytes 131104 | tf_op jit(solution)/shard_map/ppermute | solution.py:19
  143.3 3.6 %collective-permute-done.17.refs_2_ = f32[32,1024]{1,0:T(8,128)S(1)} collective-permute-done((f32[32,1024]{1,0:T(8,128)S(1)}, f32[32,1024]{1,0:T(8,128)S(1)}, u32[]{:S(2)}, u32[]{:S(2)}) %collective-permute-start.17) | collective-permute-done | bytes 131104 | tf_op jit(solution)/shard_map/ppermute | solution.py:19
  147.5 3.8 %shard_map.68.refs_0_ = f32[128,512]{1,0:T(8,128)} custom-call(f32[32,1024]{1,0:T(8,128)} %fusion.6.refs_0_.refs_1_, f32[32,1024]{1,0:T(8,128)} %collective-permute-done.16.refs_1_, f32[32,1024]{1,0:T(8,128)} %copy-done.22, f32[32,1024]{1,0:T(8,128)} %copy-done.21, f32[64,1024]{1,0:T(8,128)} %reshape.364.refs_0_.refs_4_.refs_1_, f32[64,1024]{1,0:T(8,128)} %copy-done.9, ...), custom_call_target="tpu_custom_call" | custom-call | flops 1000 | bytes 1000 | tf_op jit(solution)/shard_map/pallas_call | solution.py:193
  152.0 2.5 %collective-permute-start.24 = (f32[128,512]{1,0:T(8,128)}, f32[128,512]{1,0:T(8,128)S(1)}, u32[]{:S(2)}, u32[]{:S(2)}) collective-permute-start(f32[128,512]{1,0:T(8,128)} %shard_map.68.refs_0_), channel_id=1, source_target_pairs={{0,96},{32,0},{64,32},{96,64},{1,97},{33,1},{65,33},{97,65},{2,98}... | collective-permute-start | bytes 786440 | tf_op jit(solution)/shard_map/ppermute | solution.py:19
  154.5 7.7 %collective-permute-done.25.refs_3_ = f32[128,512]{1,0:T(8,128)S(1)} collective-permute-done((f32[128,512]{1,0:T(8,128)}, f32[128,512]{1,0:T(8,128)S(1)}, u32[]{:S(2)}, u32[]{:S(2)}) %collective-permute-start.25) | collective-permute-done | bytes 262176 | tf_op jit(solution)/shard_map/ppermute | solution.py:19
  162.3 2.3 %collective-permute-done.24.refs_2_ = f32[128,512]{1,0:T(8,128)S(1)} collective-permute-done((f32[128,512]{1,0:T(8,128)}, f32[128,512]{1,0:T(8,128)S(1)}, u32[]{:S(2)}, u32[]{:S(2)}) %collective-permute-start.24) | collective-permute-done | bytes 262176 | tf_op jit(solution)/shard_map/ppermute | solution.py:19
  164.5 1.7 collective-permute-done.23.refs_1_
  167.9 3.7 %shard_map.69 = (bf16[512,1024]{1,0:T(8,128)(2,1)}, bf16[512,1024]{1,0:T(8,128)(2,1)}) custom-call(f32[128,512]{1,0:T(8,128)} %shard_map.68.refs_0_, f32[128,512]{1,0:T(8,128)} %copy-done.16, f32[128,512]{1,0:T(8,128)} %copy-done.14, f32[128,512]{1,0:T(8,128)} %copy-done.12, f32[128,512]{1,0:T(8,128)} %copy-done.18, ...), custom_call_target="tpu_custom_call" | custom-call | flops 1000 | bytes 1000 | tf_op jit(solution)/shard_map/pallas_call | solution.py:220
  171.6 14.0 %shard_map.73.refs_0_ = f32[512,3072]{1,0:T(8,128)} custom-call(bf16[512,1024]{1,0:T(8,128)(2,1)} %get-tuple-element.24.z_high, bf16[512,1024]{1,0:T(8,128)(2,1)} %get-tuple-element.25.z_low, f32[4,3072,128]{2,1,0:T(8,128)} %bitcast.41, f32[4,2304,128]{2,1,0:T(8,128)} %bitcast.44), custom_call_target="tpu_custom_call" | custom-call | flops 1000 | bytes 1000 | tf_op jit(solution)/shard_map/pallas_call | solution.py:238
  185.6 1.2 copy-done.4
  186.9 6.6 %shard_map.74 = f32[512,3072]{1,0:T(8,128)} custom-call(bf16[512,1024]{1,0:T(8,128)(2,1)} %get-tuple-element.24.z_high, bf16[512,1024]{1,0:T(8,128)(2,1)} %get-tuple-element.25.z_low, f32[4,3072,128]{2,1,0:T(8,128)} %bitcast.42, f32[4,768,128]{2,1,0:T(8,128)} %copy-done.4, f32[512,3072]{1,0:T(8,128)} %shard_map.73.refs_0_), custom_call_target="tpu_custom_call", output_to_operand_aliasing={{}: (4, {})} | custom-call | flops 1000 | bytes 1000 | tf_op jit(solution)/shard_map/pallas_call | solution.py:238
  (125 shorter events, 14.5 us)
Async XLA Ops:
  6.5 2.8 %copy-start = (f32[3072,128]{1,0:T(8,128)S(1)}, f32[3072,128]{1,0:T(8,128)}, u32[]{:S(2)}) copy-start(f32[3072,128]{1,0:T(8,128)} %param.7) | copy-start | bytes 4718596
  6.5 2.2 %copy-start.23 = (s32[4096]{0:T(1024)S(1)}, s32[4096]{0:T(1024)}, u32[]{:S(2)}) copy-start(s32[4096]{0:T(1024)} %param.11) | copy-start | bytes 49156
  6.5 85.1 %all-gather.5.cloned.1.call-start = ((), (), s32[]{:S(2)}) async-start(), calls=%async_computation.1 | async-start | bytes 7864320 | tf_op jit(solution)/shard_map/all_gather | solution.py:303
  10.1 7.5 %collective-permute-start.1 = (f32[256,128]{1,0:T(8,128)S(1)}, f32[256,128]{1,0:T(8,128)S(1)}, u32[]{:S(2)}, u32[]{:S(2)}) collective-permute-start(f32[256,128]{1,0:T(8,128)S(1)} %gather_fusion), channel_id=1, source_target_pairs={{0,16},{16,0},{1,17},{17,1},{2,18},{18,2},{3,19},{19,3},{4,20},{20... | collective-permute-start | bytes 393224 | tf_op jit(solution)/shard_map/ppermute | solution.py:19
  17.6 13.5 %collective-permute-start.3 = (f32[2,256,128]{2,1,0:T(8,128)S(1)}, f32[2,256,128]{2,1,0:T(8,128)S(1)}, u32[]{:S(2)}, u32[]{:S(2)}) collective-permute-start(f32[2,256,128]{2,1,0:T(8,128)S(1)} %get-tuple-element.30), channel_id=1, source_target_pairs={{0,96},{32,0},{64,32},{96,64},{1,97},{33,1},{65,33},{97,65},{2,98}... | collective-permute-start | bytes 786440 | tf_op jit(solution)/shard_map/ppermute | solution.py:19
  20.5 14.0 %collective-permute-start.2 = (f32[2,256,128]{2,1,0:T(8,128)S(1)}, f32[2,256,128]{2,1,0:T(8,128)S(1)}, u32[]{:S(2)}, u32[]{:S(2)}) collective-permute-start(f32[2,256,128]{2,1,0:T(8,128)S(1)} %get-tuple-element.30), channel_id=1, source_target_pairs={{0,32},{32,64},{64,96},{96,0},{1,33},{33,65},{65,97},{97,1},{2,34}... | collective-permute-start | bytes 786440 | tf_op jit(solution)/shard_map/ppermute | solution.py:19
  20.5 14.0 %collective-permute-start.4 = (f32[2,256,128]{2,1,0:T(8,128)S(1)}, f32[2,256,128]{2,1,0:T(8,128)S(1)}, u32[]{:S(2)}, u32[]{:S(2)}) collective-permute-start(f32[2,256,128]{2,1,0:T(8,128)S(1)} %get-tuple-element.30), channel_id=1, source_target_pairs={{0,64},{32,96},{64,0},{96,32},{1,65},{33,97},{65,1},{97,33},{2,66}... | collective-permute-start | bytes 786440 | tf_op jit(solution)/shard_map/ppermute | solution.py:19
  22.8 34.9 %collective-permute-start = (f32[3072,128]{1,0:T(8,128)}, f32[3072,128]{1,0:T(8,128)S(1)}, u32[]{:S(2)}, u32[]{:S(2)}) collective-permute-start(f32[3072,128]{1,0:T(8,128)} %own_ref.1), channel_id=1, source_target_pairs={{0,1},{1,0},{2,3},{3,2},{4,5},{5,4},{6,7},{7,6},{8,9},{9,8},{10,11... | collective-permute-start | bytes 4718600 | tf_op jit(solution)/shard_map/ppermute | solution.py:19
  36.0 3.0 %collective-permute-start.5 = (f32[4,2,256,128]{3,2,1,0:T(8,128)}, f32[4,2,256,128]{3,2,1,0:T(8,128)}, u32[]{:S(2)}, u32[]{:S(2)}) collective-permute-start(f32[4,2,256,128]{3,2,1,0:T(8,128)} %get-tuple-element.28), channel_id=1, source_target_pairs={{0,8},{8,0},{1,9},{9,1},{2,10},{10,2},{3,11},{11,3},{4,12},{12,4},... | collective-permute-start | bytes 3145736 | tf_op jit(solution)/shard_map/ppermute | solution.py:19
  60.5 14.4 %all-to-all-start = ((f32[8,64,128]{2,1,0:T(8,128)}), f32[8,64,128]{2,1,0:T(8,128)S(1)}, u32[]{:S(2)}, u32[]{:S(2)}) async-start(f32[8,64,128]{2,1,0:T(8,128)} %shard_map.65), calls=%async_computation | async-start | bytes 524288 | tf_op jit(solution)/shard_map/all_to_all | solution.py:294
  65.4 106.2 %all-gather.7.cloned.1.call-start = ((), (), s32[]{:S(2)}) async-start(), calls=%async_computation.2 | async-start | bytes 5898240 | tf_op jit(solution)/shard_map/all_gather | solution.py:313
  76.0 3.6 %copy-start.2 = (f32[64,1024]{1,0:T(8,128)S(1)}, f32[64,1024]{1,0:T(8,128)}, u32[]{:S(2)}) copy-start(f32[64,1024]{1,0:T(8,128)} %reshape.364.refs_0_.refs_4_.refs_1_) | copy-start | bytes 786436
  78.1 24.0 %collective-permute-start.31 = (f32[2304,128]{1,0:T(8,128)}, f32[2304,128]{1,0:T(8,128)S(1)}, u32[]{:S(2)}, u32[]{:S(2)}) collective-permute-start(f32[2304,128]{1,0:T(8,128)} %shard_map.71), channel_id=1, source_target_pairs={{0,1},{1,0},{2,3},{3,2},{4,5},{5,4},{6,7},{7,6},{8,9},{9,8},{10,11... | collective-permute-start | bytes 3538952 | tf_op jit(solution)/shard_map/ppermute | solution.py:19
  79.6 11.4 %collective-permute-start.8 = (f32[64,1024]{1,0:T(8,128)S(1)}, f32[64,1024]{1,0:T(8,128)S(1)}, u32[]{:S(2)}, u32[]{:S(2)}) collective-permute-start(f32[64,1024]{1,0:T(8,128)S(1)} %copy-done.2), channel_id=1, source_target_pairs={{0,64},{32,96},{64,0},{96,32},{1,65},{33,97},{65,1},{97,33},{2,66}... | collective-permute-start | bytes 786440 | tf_op jit(solution)/shard_map/ppermute | solution.py:19
  81.2 9.8 %collective-permute-start.7 = (f32[64,1024]{1,0:T(8,128)S(1)}, f32[64,1024]{1,0:T(8,128)S(1)}, u32[]{:S(2)}, u32[]{:S(2)}) collective-permute-start(f32[64,1024]{1,0:T(8,128)S(1)} %copy-done.2), channel_id=1, source_target_pairs={{0,96},{32,0},{64,32},{96,64},{1,97},{33,1},{65,33},{97,65},{2,98}... | collective-permute-start | bytes 786440 | tf_op jit(solution)/shard_map/ppermute | solution.py:19
  84.1 7.6 %collective-permute-start.6 = (f32[64,1024]{1,0:T(8,128)S(1)}, f32[64,1024]{1,0:T(8,128)S(1)}, u32[]{:S(2)}, u32[]{:S(2)}) collective-permute-start(f32[64,1024]{1,0:T(8,128)S(1)} %copy-done.2), channel_id=1, source_target_pairs={{0,32},{32,64},{64,96},{96,0},{1,33},{33,65},{65,97},{97,1},{2,34}... | collective-permute-start | bytes 786440 | tf_op jit(solution)/shard_map/ppermute | solution.py:19
  102.1 3.3 %copy-start.24 = (f32[1024]{0:T(1024)S(1)}, f32[1024]{0:T(1024)}, u32[]{:S(2)}) copy-start(f32[1024]{0:T(1024)} %param.9) | copy-start | bytes 12292
  102.1 3.4 %copy-start.25 = (f32[4,32,512]{2,1,0:T(8,128)S(1)}, f32[4,32,512]{2,1,0:T(8,128)}, u32[]{:S(2)}) copy-start(f32[4,32,512]{2,1,0:T(8,128)} %get-tuple-element.19) | copy-start | bytes 786436
  105.5 1.6 collective-permute-start.9
  109.6 5.7 %collective-permute-start.10 = (f32[32,512]{1,0:T(8,128)}, f32[32,512]{1,0:T(8,128)S(1)}, u32[]{:S(2)}, u32[]{:S(2)}) collective-permute-start(f32[32,512]{1,0:T(8,128)} %get-tuple-element.21), channel_id=1, source_target_pairs={{0,32},{32,64},{64,96},{96,0},{1,33},{33,65},{65,97},{97,1},{2,34}... | collective-permute-start | bytes 196616 | tf_op jit(solution)/shard_map/ppermute | solution.py:19
  111.4 4.9 %collective-permute-start.11 = (f32[32,512]{1,0:T(8,128)}, f32[32,512]{1,0:T(8,128)S(1)}, u32[]{:S(2)}, u32[]{:S(2)}) collective-permute-start(f32[32,512]{1,0:T(8,128)} %get-tuple-element.22), channel_id=1, source_target_pairs={{0,96},{32,0},{64,32},{96,64},{1,97},{33,1},{65,33},{97,65},{2,98}... | collective-permute-start | bytes 196616 | tf_op jit(solution)/shard_map/ppermute | solution.py:19
  112.8 6.0 %collective-permute-start.12 = (f32[32,512]{1,0:T(8,128)}, f32[32,512]{1,0:T(8,128)S(1)}, u32[]{:S(2)}, u32[]{:S(2)}) collective-permute-start(f32[32,512]{1,0:T(8,128)} %get-tuple-element.23), channel_id=1, source_target_pairs={{0,64},{32,96},{64,0},{96,32},{1,65},{33,97},{65,1},{97,33},{2,66}... | collective-permute-start | bytes 196616 | tf_op jit(solution)/shard_map/ppermute | solution.py:19
  118.8 12.0 %copy-start.3 = (f32[64,1024]{1,0:T(8,128)S(1)}, f32[64,1024]{1,0:T(8,128)}, u32[]{:S(2)}) copy-start(f32[64,1024]{1,0:T(8,128)} %reshape.364.refs_0_.refs_4_.refs_1_) | copy-start | bytes 786436
  119.7 9.8 %collective-permute-start.15 = (f32[32,512]{1,0:T(8,128)S(1)}, f32[32,512]{1,0:T(8,128)S(1)}, u32[]{:S(2)}, u32[]{:S(2)}) collective-permute-start(f32[32,512]{1,0:T(8,128)S(1)} %add_add_fusion), channel_id=1, source_target_pairs={{0,17},{1,0},{16,1},{17,16},{2,19},{3,2},{18,3},{19,18},{4,21},{5,... | collective-permute-start | bytes 196616 | tf_op jit(solution)/shard_map/ppermute | solution.py:19
  123.6 6.2 %collective-permute-start.14 = (f32[32,512]{1,0:T(8,128)S(1)}, f32[32,512]{1,0:T(8,128)S(1)}, u32[]{:S(2)}, u32[]{:S(2)}) collective-permute-start(f32[32,512]{1,0:T(8,128)S(1)} %add_add_fusion), channel_id=1, source_target_pairs={{0,1},{1,16},{16,17},{17,0},{2,3},{3,18},{18,19},{19,2},{4,5},{5,2... | collective-permute-start | bytes 196616 | tf_op jit(solution)/shard_map/ppermute | solution.py:19
  123.6 5.9 %collective-permute-start.13 = (f32[32,512]{1,0:T(8,128)S(1)}, f32[32,512]{1,0:T(8,128)S(1)}, u32[]{:S(2)}, u32[]{:S(2)}) collective-permute-start(f32[32,512]{1,0:T(8,128)S(1)} %add_add_fusion), channel_id=1, source_target_pairs={{0,16},{1,17},{16,0},{17,1},{2,18},{3,19},{18,2},{19,3},{4,20},{5,... | collective-permute-start | bytes 196616 | tf_op jit(solution)/shard_map/ppermute | solution.py:19
  130.6 55.1 %collective-permute-start.30 = (f32[4,768,128]{2,1,0:T(8,128)}, f32[4,768,128]{2,1,0:T(8,128)S(1)}, u32[]{:S(2)}, u32[]{:S(2)}) collective-permute-start(f32[4,768,128]{2,1,0:T(8,128)} %shard_map.70), channel_id=1, source_target_pairs={{0,1},{1,0},{2,3},{3,2},{4,5},{5,4},{6,7},{7,6},{8,9},{9,8},{10,11... | collective-permute-start | bytes 4718600 | tf_op jit(solution)/shard_map/ppermute | solution.py:19
  130.8 1.9 collective-permute-start.19
  130.8 2.5 %collective-permute-start.22 = (f32[64,1024]{1,0:T(8,128)}, f32[64,1024]{1,0:T(8,128)S(1)}, u32[]{:S(2)}, u32[]{:S(2)}) collective-permute-start(f32[64,1024]{1,0:T(8,128)} %copy-done.7), channel_id=1, source_target_pairs={{0,8},{8,0},{1,9},{9,1},{2,10},{10,2},{3,11},{11,3},{4,12},{12,4},... | collective-permute-start | bytes 786440 | tf_op jit(solution)/shard_map/ppermute | solution.py:19
  131.3 4.6 %collective-permute-start.21 = (f32[64,1024]{1,0:T(8,128)}, f32[64,1024]{1,0:T(8,128)S(1)}, u32[]{:S(2)}, u32[]{:S(2)}) collective-permute-start(f32[64,1024]{1,0:T(8,128)} %copy-done.8), channel_id=1, source_target_pairs={{0,8},{8,0},{1,9},{9,1},{2,10},{10,2},{3,11},{11,3},{4,12},{12,4},... | collective-permute-start | bytes 786440 | tf_op jit(solution)/shard_map/ppermute | solution.py:19
  131.3 4.6 %collective-permute-start.20 = (f32[64,1024]{1,0:T(8,128)}, f32[64,1024]{1,0:T(8,128)S(1)}, u32[]{:S(2)}, u32[]{:S(2)}) collective-permute-start(f32[64,1024]{1,0:T(8,128)} %copy-done.9), channel_id=1, source_target_pairs={{0,8},{8,0},{1,9},{9,1},{2,10},{10,2},{3,11},{11,3},{4,12},{12,4},... | collective-permute-start | bytes 786440 | tf_op jit(solution)/shard_map/ppermute | solution.py:19
  132.6 14.5 %copy-start.11 = (f32[64,1024]{1,0:T(8,128)}, f32[64,1024]{1,0:T(8,128)S(1)}, u32[]{:S(2)}) copy-start(f32[64,1024]{1,0:T(8,128)S(1)} %collective-permute-done.19.refs_8_) | copy-start | bytes 786436
  132.6 10.6 %collective-permute-start.18 = (f32[32,1024]{1,0:T(8,128)S(1)}, f32[32,1024]{1,0:T(8,128)S(1)}, u32[]{:S(2)}, u32[]{:S(2)}) collective-permute-start(f32[32,1024]{1,0:T(8,128)S(1)} %copy-done.5), channel_id=1, source_target_pairs={{0,4},{2,6},{4,0},{6,2},{1,5},{3,7},{5,1},{7,3},{8,12},{10,14},{12... | collective-permute-start | bytes 393224 | tf_op jit(solution)/shard_map/ppermute | solution.py:19
  133.2 13.9 %copy-start.13 = (f32[64,1024]{1,0:T(8,128)}, f32[64,1024]{1,0:T(8,128)S(1)}, u32[]{:S(2)}) copy-start(f32[64,1024]{1,0:T(8,128)S(1)} %collective-permute-done.22.refs_11_) | copy-start | bytes 786436
  133.2 13.7 %collective-permute-start.17 = (f32[32,1024]{1,0:T(8,128)S(1)}, f32[32,1024]{1,0:T(8,128)S(1)}, u32[]{:S(2)}, u32[]{:S(2)}) collective-permute-start(f32[32,1024]{1,0:T(8,128)S(1)} %copy-done.5), channel_id=1, source_target_pairs={{0,6},{2,0},{4,2},{6,4},{1,7},{3,1},{5,3},{7,5},{8,14},{10,8},{12,... | collective-permute-start | bytes 393224 | tf_op jit(solution)/shard_map/ppermute | solution.py:19
  135.9 11.0 %copy-start.15 = (f32[64,1024]{1,0:T(8,128)}, f32[64,1024]{1,0:T(8,128)S(1)}, u32[]{:S(2)}) copy-start(f32[64,1024]{1,0:T(8,128)S(1)} %collective-permute-done.21.refs_10_) | copy-start | bytes 786436
  135.9 11.3 %collective-permute-start.16 = (f32[32,1024]{1,0:T(8,128)S(1)}, f32[32,1024]{1,0:T(8,128)}, u32[]{:S(2)}, u32[]{:S(2)}) collective-permute-start(f32[32,1024]{1,0:T(8,128)S(1)} %copy-done.5), channel_id=1, source_target_pairs={{0,2},{2,4},{4,6},{6,0},{1,3},{3,5},{5,7},{7,1},{8,10},{10,12},{12... | collective-permute-start | bytes 393224 | tf_op jit(solution)/shard_map/ppermute | solution.py:19
  135.9 11.0 %copy-start.17 = (f32[64,1024]{1,0:T(8,128)}, f32[64,1024]{1,0:T(8,128)S(1)}, u32[]{:S(2)}) copy-start(f32[64,1024]{1,0:T(8,128)S(1)} %collective-permute-done.20.refs_9_) | copy-start | bytes 786436
  143.3 3.9 %copy-start.21 = (f32[32,1024]{1,0:T(8,128)}, f32[32,1024]{1,0:T(8,128)S(1)}, u32[]{:S(2)}) copy-start(f32[32,1024]{1,0:T(8,128)S(1)} %collective-permute-done.18.refs_3_) | copy-start | bytes 393220
  151.3 11.0 %collective-permute-start.25 = (f32[128,512]{1,0:T(8,128)}, f32[128,512]{1,0:T(8,128)S(1)}, u32[]{:S(2)}, u32[]{:S(2)}) collective-permute-start(f32[128,512]{1,0:T(8,128)} %shard_map.68.refs_0_), channel_id=1, source_target_pairs={{0,64},{32,96},{64,0},{96,32},{1,65},{33,97},{65,1},{97,33},{2,66}... | collective-permute-start | bytes 786440 | tf_op jit(solution)/shard_map/ppermute | solution.py:19
  152.0 12.5 %collective-permute-start.24 = (f32[128,512]{1,0:T(8,128)}, f32[128,512]{1,0:T(8,128)S(1)}, u32[]{:S(2)}, u32[]{:S(2)}) collective-permute-start(f32[128,512]{1,0:T(8,128)} %shard_map.68.refs_0_), channel_id=1, source_target_pairs={{0,96},{32,0},{64,32},{96,64},{1,97},{33,1},{65,33},{97,65},{2,98}... | collective-permute-start | bytes 786440 | tf_op jit(solution)/shard_map/ppermute | solution.py:19
  154.5 11.7 %collective-permute-start.23 = (f32[128,512]{1,0:T(8,128)}, f32[128,512]{1,0:T(8,128)S(1)}, u32[]{:S(2)}, u32[]{:S(2)}) collective-permute-start(f32[128,512]{1,0:T(8,128)} %shard_map.68.refs_0_), channel_id=1, source_target_pairs={{0,32},{32,64},{64,96},{96,0},{1,33},{33,65},{65,97},{97,1},{2,34}... | collective-permute-start | bytes 786440 | tf_op jit(solution)/shard_map/ppermute | solution.py:19
  154.5 11.7 %collective-permute-start.26 = (f32[128,512]{1,0:T(8,128)}, f32[128,512]{1,0:T(8,128)S(1)}, u32[]{:S(2)}, u32[]{:S(2)}) collective-permute-start(f32[128,512]{1,0:T(8,128)} %shard_map.68.refs_0_), channel_id=1, source_target_pairs={{0,8},{8,0},{1,9},{9,1},{2,10},{10,2},{3,11},{11,3},{4,12},{12,4},... | collective-permute-start | bytes 786440 | tf_op jit(solution)/shard_map/ppermute | solution.py:19
  162.3 5.6 %copy-start.12 = (f32[128,512]{1,0:T(8,128)}, f32[128,512]{1,0:T(8,128)S(1)}, u32[]{:S(2)}) copy-start(f32[128,512]{1,0:T(8,128)S(1)} %collective-permute-done.25.refs_3_) | copy-start | bytes 786436
  162.3 4.0 %collective-permute-start.29 = (f32[128,512]{1,0:T(8,128)S(1)}, f32[128,512]{1,0:T(8,128)S(1)}, u32[]{:S(2)}, u32[]{:S(2)}) collective-permute-start(f32[128,512]{1,0:T(8,128)S(1)} %collective-permute-done.25.refs_3_), channel_id=1, source_target_pairs={{0,8},{8,0},{1,9},{9,1},{2,10},{10,2},{3,11},{11,3},{4,12},{12,4},... | collective-permute-start | bytes 786440 | tf_op jit(solution)/shard_map/ppermute | solution.py:19
  164.5 3.4 %copy-start.14 = (f32[128,512]{1,0:T(8,128)}, f32[128,512]{1,0:T(8,128)S(1)}, u32[]{:S(2)}) copy-start(f32[128,512]{1,0:T(8,128)S(1)} %collective-permute-done.24.refs_2_) | copy-start | bytes 786436
  164.5 1.7 collective-permute-start.28
  166.2 1.7 collective-permute-start.27
  (13 other events, 12.9 us)
Sparse Core Ops, SparseCore 0:
  9.0 70.9 all-gather.4
  105.4 57.8 all-gather.6

commit v3 on v2

v3 whole, which is shorter than its diff:
```python
import jax
import jax.numpy as jnp
from jax import lax
from jax.experimental import pallas as pl
from jax.experimental.pallas import tpu as pltpu
from jax.sharding import Mesh
from jax.sharding import PartitionSpec as P

HARM = ("x", "zh", "c")
MODE = ("y", "zl")
SIZES = {"x": 4, "zh": 2, "c": 2, "y": 4, "zl": 2, ("zh", "zl"): 4}
regular = 0.01
TILE = 384
VMEM = 60 * 1024 * 1024


def shifted(array, axis, step):
    n = SIZES[axis]
    return lax.ppermute(array, axis, [(i, (i + step) % n) for i in range(n)])


def pick(parts, number):
    return lax.dynamic_index_in_dim(parts, number, 0, keepdims=False)


def slot_of(offset):
    return jnp.where(offset == 0, 0, jnp.where(offset == 3, 1, jnp.where(offset == 1, 2, 3)))


def ring_parts(array, axis):
    return [array, shifted(array, axis, 1), shifted(array, axis, -1), shifted(array, axis, 2)]


def split(value):
    high = value.astype(jnp.bfloat16)
    low = (value - high.astype(jnp.float32)).astype(jnp.bfloat16)
    return high, low


def three_pass(both, b, dims):
    high, low = b
    rows = both.shape[0] // 2

    def dot(p, q):
        return lax.dot_general(p, q, (dims, ((), ())), preferred_element_type=jnp.float32)

    first = dot(both, high)
    return first[:rows] + first[rows:] + dot(both[:rows], low)


SMALL = pl.CostEstimate(flops=1000, bytes_accessed=1000, transcendentals=0)
ANY = pl.BlockSpec(memory_space=pl.ANY)
STEP = 384
WIDE = 768
PARAMS = pltpu.CompilerParams(vmem_limit_bytes=VMEM)


def with_rows(small, array, count, after):
    rows = count // 2

    def body(array_ref, small_ref, *refs):
        refs[-1][...] = array_ref[...]

    return pl.pallas_call(
        body,
        grid=(2,),
        in_specs=[pl.BlockSpec((rows, 128), lambda i: (i, 0)), ANY] + [ANY] * len(after),
        out_specs=[ANY, pl.BlockSpec((rows, 128), lambda i: (i, 0))],
        out_shape=[
            jax.ShapeDtypeStruct(small.shape, small.dtype),
            jax.ShapeDtypeStruct((count, 128), array.dtype),
        ],
        input_output_aliases={1: 0},
        compiler_params=PARAMS,
        cost_estimate=SMALL,
    )(array, small, *after)


def released(array, after):
    def body(*refs):
        pass

    return pl.pallas_call(
        body,
        in_specs=[ANY] * (1 + len(after)),
        out_specs=ANY,
        out_shape=jax.ShapeDtypeStruct(array.shape, array.dtype),
        input_output_aliases={0: 0},
        cost_estimate=SMALL,
    )(array, *after)


def x_parts(kept, came, after):
    def body(kept_ref, came_ref, *refs):
        x = lax.axis_index("x")
        for ref, offset in zip(refs[-4:], (0, 1, 3, 2), strict=True):
            share = lax.rem(x + offset, 4)
            ref[...] = kept_ref[share] + came_ref[share]

    return pl.pallas_call(
        body,
        in_specs=[pl.BlockSpec(kept.shape, lambda: (0, 0, 0))] * 2 + [ANY] * len(after),
        out_shape=[jax.ShapeDtypeStruct(kept.shape[1:], kept.dtype)] * 4,
        compiler_params=PARAMS,
        cost_estimate=SMALL,
    )(kept, came, *after)


def cot_ready(own, first, second):
    rows = own.shape[0]
    split_at = first.shape[0] // STEP

    def body(own_ref, first_ref, second_ref, both):
        other = jnp.where(pl.program_id(0) < split_at, first_ref[...], second_ref[...])
        high, low = split(jnp.concatenate([own_ref[...].T, other.T], axis=0))
        both[:256], both[256:] = high, low

    return pl.pallas_call(
        body,
        grid=(rows // STEP,),
        in_specs=[
            pl.BlockSpec((STEP, 128), lambda i: (i, 0)),
            pl.BlockSpec((STEP, 128), lambda i: (jnp.minimum(i, split_at - 1), 0)),
            pl.BlockSpec((STEP, 128), lambda i: (jnp.maximum(i - split_at, 0), 0)),
        ],
        out_specs=pl.BlockSpec((512, STEP), lambda i: (0, i)),
        out_shape=jax.ShapeDtypeStruct((512, rows), jnp.bfloat16),
        compiler_params=PARAMS,
        cost_estimate=SMALL,
    )(own, first, second)


def wide(ref):
    return jnp.concatenate([ref[k] for k in range(4)], axis=1)


def gram_shares(cot, whole_x, cut, after):
    rows = whole_x.shape[1]
    step_rows = rows - cut
    steps, start = rows // step_rows, cut // step_rows

    def body(cot_ref, x_ref, *refs):
        kept, sent, tail, total = refs[-4:]
        step = pl.program_id(0)
        c, zl = lax.axis_index("c"), lax.axis_index("zl")

        @pl.when(step == 0)
        def _():
            total[...] = jnp.zeros_like(total)

        total[...] += three_pass(cot_ref[...], split(wide(x_ref)), ((1,), (0,)))

        @pl.when(step >= start)
        def _():
            tail[...] = x_ref[...]

        @pl.when(step == steps - 1)
        def _():
            for s in range(4):
                for ref, core in ((kept, c), (sent, 1 - c)):
                    row = pl.multiple_of(lax.rem(s * 64 + core * 32 + 128 * zl, 256), 32)
                    ref[s] = total[pl.ds(row, 32), :]

    shape = jax.ShapeDtypeStruct((4, 32, 512), jnp.float32)
    whole = pl.BlockSpec((4, 32, 512), lambda i: (0, 0, 0))
    return pl.pallas_call(
        body,
        grid=(steps,),
        in_specs=[pl.BlockSpec((512, step_rows), lambda i: (0, i))]
        + [pl.BlockSpec((4, step_rows, 128), lambda i: (0, i, 0))]
        + [ANY] * len(after),
        out_specs=[whole, whole, pl.BlockSpec((4, step_rows, 128), lambda i: (0, 0, 0))],
        out_shape=[shape, shape, jax.ShapeDtypeStruct((4, rows - cut, 128), jnp.float32)],
        scratch_shapes=[pltpu.VMEM((256, 512), jnp.float32)],
        compiler_params=PARAMS,
        cost_estimate=SMALL,
    )(cot, whole_x, *after)


def z_part(weighted, picked):
    height, depth = picked.shape

    def body(*refs):
        weighted_refs, picked_ref = refs[:4], refs[4]
        out, tall = refs[-2:]
        y = lax.axis_index("y")
        for slot, offset in enumerate((0, 3, 1, 2)):
            tall[pl.ds(pl.multiple_of(lax.rem(y + offset, 4) * 32, 32), 32), :] = weighted_refs[slot][...]
        out[...] = three_pass(jnp.concatenate(split(tall[...]), axis=0), split(picked_ref[...]), ((1,), (1,)))

    return pl.pallas_call(
        body,
        out_shape=jax.ShapeDtypeStruct((128, height), jnp.float32),
        scratch_shapes=[pltpu.VMEM((128, depth), jnp.float32)],
        compiler_params=PARAMS,
        cost_estimate=SMALL,
    )(*weighted, picked)


def z_ready(own_z, other_z):
    depth, height = 1024, own_z[0].shape[1]

    def body(*refs):
        sets, (both, z_tall) = (refs[:4], refs[4:8]), refs[8:]
        x, c, zl = lax.axis_index("x"), lax.axis_index("c"), lax.axis_index("zl")
        for slot, offset in enumerate((0, 3, 1, 2)):
            source = lax.rem(x + offset, 4)
            side = lax.rem(source // 2 + zl, 2)
            for part in range(4):
                for which, held in ((c, sets[0]), (1 - c, sets[1])):
                    row = side * 512 + part * 128 + lax.rem(source, 2) * 64 + which * 32
                    z_tall[pl.ds(pl.multiple_of(row, 32), 32), :] = held[slot][part * 32 : part * 32 + 32, :]
        for part in range(depth // 128):
            cols = slice(part * 128, part * 128 + 128)
            both[:height, cols], both[height:, cols] = split(z_tall[cols, :].T)

    return pl.pallas_call(
        body,
        out_shape=jax.ShapeDtypeStruct((2 * height, depth), jnp.bfloat16),
        scratch_shapes=[pltpu.VMEM((depth, height), jnp.float32)],
        compiler_params=PARAMS,
        cost_estimate=SMALL,
    )(*own_z, *other_z)


def slab_part(z, own_x, other_low, other_high):
    total = own_x.shape[1]
    split_at = other_low.shape[1] // WIDE
    height, depth = z.shape[0] // 2, z.shape[1]

    def body(z_ref, own_ref, low_ref, high_ref, out):
        step = pl.program_id(0)

        def product(other_ref):
            x_tile = split(jnp.concatenate([wide(own_ref), wide(other_ref)], axis=1))
            out[...] = three_pass(z_ref[...], x_tile, ((1,), (1,)))

        @pl.when(step < split_at)
        def _():
            product(low_ref)

        @pl.when(step >= split_at)
        def _():
            product(high_ref)

    return pl.pallas_call(
        body,
        grid=(total // WIDE,),
        in_specs=[
            pl.BlockSpec(z.shape, lambda i: (0, 0)),
            pl.BlockSpec((4, WIDE, 128), lambda i: (0, i, 0)),
            pl.BlockSpec((4, WIDE, 128), lambda i: (0, jnp.minimum(i, split_at - 1), 0)),
            pl.BlockSpec((4, WIDE, 128), lambda i: (0, jnp.maximum(i - split_at, 0), 0)),
        ],
        out_specs=pl.BlockSpec((height, WIDE), lambda i: (0, i)),
        out_shape=jax.ShapeDtypeStruct((height, total), jnp.float32),
        compiler_params=PARAMS,
        cost_estimate=SMALL,
    )(z, own_x, other_low, other_high)


def places(slab_rows, height, count):
    total = slab_rows.shape[0]
    kinds = total // count
    block_of = slab_rows // height
    member = (block_of[:, None] == jnp.arange(kinds)[None, :]).astype(jnp.float32).reshape(-1, 128, kinds)
    before = jnp.tril(jnp.ones((128, 128), jnp.float32), -1)
    within = jnp.einsum("ab,cbh->cah", before, member, preferred_element_type=jnp.float32)
    chunks = member.shape[0]
    sums = member.sum(1)
    ahead = jnp.dot(jnp.tril(jnp.ones((chunks, chunks), jnp.float32), -1), sums, preferred_element_type=jnp.float32)
    rank = ((within + ahead[:, None, :]) * member).sum(2).reshape(total)
    return block_of * count + rank.astype(jnp.int32)


def slab_weights(weights, slab_rows, x, zh, c, zl, cots, mode_vectors, cut):
    height = weights.shape[0]
    total = slab_rows.shape[0]
    count = total // 16
    harm = (x * 2 + zh) * 2 + c
    place = places(slab_rows, height, count)
    ids = harm * count + jnp.arange(count, dtype=jnp.int32)
    local_rows = jnp.where(place[None, :] == ids[:, None], slab_rows[None, :] - harm * height, 0).sum(1)
    own, below, above, far = ring_parts(jnp.take(weights, local_rows, axis=0, mode="clip"), ("zh", "zl"))
    near = jnp.concatenate([own, jnp.where(zl == 0, above, below)], axis=1)
    away = jnp.concatenate([far, jnp.where(zl == 0, below, above)], axis=1)
    pair, first_rows = with_rows(jnp.stack([near, away]), mode_vectors, cut, cots[:1])
    ring = jnp.stack(ring_parts(pair, "x")).reshape(-1, 256)
    share = total // 64
    places_here = pick(place.reshape(4, 2, 4, 2, share).swapaxes(0, 1), zl)
    places_here = lax.dynamic_index_in_dim(places_here, x, 1, keepdims=False)

    def chosen(core):
        wanted = lax.dynamic_index_in_dim(places_here, core, 1, keepdims=False).reshape(-1)
        source, row = wanted // count, wanted % count
        source_x, source_zh, source_c = source // 4, (source // 2) % 2, source % 2
        number = (slot_of((source_x - x) % 4) * 2 + (source_zh != zh)) * count + row
        return number, source_c == c

    numbers, mine = zip(chosen(c), chosen(1 - c), strict=True)
    taken = jnp.take(ring, jnp.concatenate(numbers), axis=0, mode="clip")
    taken = jnp.where(jnp.concatenate(mine)[:, None], taken, 0.0).reshape(2, 4, share, 256)
    taken = released(taken, cots[1:])
    return taken[0] + shifted(taken[1], "c", 1), first_rows


def slab_share(chosen, y):
    share = chosen.shape[1]
    came = jnp.stack(
        [
            pick(chosen, y),
            shifted(pick(chosen, (y + 1) % 4), "y", 1),
            shifted(pick(chosen, (y + 3) % 4), "y", -1),
            shifted(pick(chosen, (y + 2) % 4), "y", 2),
        ]
    )
    came = jnp.stack([pick(came, slot_of((k - y) % 4)) for k in range(4)])
    return came.reshape(4, share, 2, 128).transpose(1, 2, 0, 3).reshape(share, 1024)


def local(mode_vectors, weights, cotangent, eigenvalues, eigen_cotangent, slab_rows):
    x, zh, c, y, zl = (lax.axis_index(a) for a in ("x", "zh", "c", "y", "zl"))
    rows = mode_vectors.shape[0]
    cut = rows * 3 // 4
    own_x = lax.all_gather(mode_vectors, "y")
    early = rows // 4
    cots = (shifted(cotangent[:early], "zl", 1), shifted(cotangent[early:], "zl", 1))
    chosen, first_rows = slab_weights(weights, slab_rows, x, zh, c, zl, cots, mode_vectors, cut)
    other_rows = shifted(released(first_rows, cots), "zl", 1)
    share = slab_share(chosen, y)
    picked = lax.all_gather(share, ("x", "c"), tiled=True)
    cot = cot_ready(cotangent, *cots)

    kept, sent, tail = gram_shares(cot, own_x, cut, (share,))
    to_self, to_above, to_below, to_far = x_parts(kept, shifted(sent, "c", 1), ())
    other_low = lax.all_gather(released(other_rows, (to_self,)), "y")
    total = to_self + shifted(to_above, "x", 1) + shifted(to_below, "x", -1) + shifted(to_far, "x", 2)
    own, below, above, far = ring_parts(total, ("zh", "zl"))
    total = jnp.concatenate([own + far, below + above], axis=1)
    j_first = (y * 2 + x // 2) * 128 + ((x % 2) * 2 + c) * 32
    eigen_j = lax.dynamic_slice_in_dim(eigenvalues, j_first, 32)
    slope_j = lax.dynamic_slice_in_dim(eigen_cotangent, j_first, 32)
    sides = eigenvalues.reshape(4, 2, 128).transpose(1, 0, 2).reshape(2, 512)
    eigen_i = jnp.where(zl == 0, sides, sides[::-1]).reshape(1024)
    differ = eigen_j[:, None] - eigen_i[None]
    factor = differ / (differ * differ + regular)
    j_ids = j_first + lax.broadcasted_iota(jnp.int32, (32, 1024), 0)
    col = lax.broadcasted_iota(jnp.int32, (32, 1024), 1)
    i_ids = (col % 512 // 128 * 2 + (zl + col // 512) % 2) * 128 + col % 128
    weighted = factor * total + jnp.where(j_ids == i_ids, slope_j[:, None], 0.0)

    other_high = shifted(released(tail, (weighted,)), "zl", 1)
    z_own = ring_parts(z_part(ring_parts(weighted, "y"), picked), "x")
    z_other = [shifted(part, "c", 1) for part in z_own]
    z = z_ready(z_own, z_other)
    return slab_part(z, own_x, other_low, other_high)


def solution(mesh):
    torus = Mesh(mesh.devices.reshape(4, 2, 2, 4, 2), ("x", "zh", "c", "y", "zl"))
    return jax.shard_map(
        local,
        mesh=torus,
        in_specs=(P(HARM, MODE), P(HARM, MODE), P(HARM, MODE), P(), P(), P()),
        out_specs=P(MODE, HARM),
        check_vma=False,
    )
```

time: 202 us -> 192 us (0.950)
  Pallas kernels: 52.4 us -> 40.4 us
  local copies, waits for them, and re-layouts: 12.8 us -> 17.2 us
  waiting for transfers between devices: 74 us -> 69.8 us
  other arithmetic: 8 us -> 10.7 us
    pallas_call x8 -> x5, Pallas kernels: 43.7 us -> 31.8 us  [the longest x1 14.9 us: slab_part(): pl.pallas_call(body, grid=(total // WIDE,), in_specs=[pl.BlockSpec(z.shap...]
    all_to_all x1 -> x0, waiting for transfers between devices: 9.49 us -> none  [slab_share(): lax.all_to_all(chosen, MODE, 0, 0, tiled=True).reshape(4, 2, share, 128)]
    all_to_all x1 -> x0, starting transfers between devices: 4.88 us -> none  [slab_share(): lax.all_to_all(chosen, MODE, 0, 0, tiled=True).reshape(4, 2, share, 128)]
    ppermute x32 -> x31, starting transfers between devices: 34 us -> 37.9 us  [shifted(): return lax.ppermute(array, axis, [(i, (i + step) % n) for i in range(n)])]
    all_gather x1 -> x2, waiting for transfers between devices: 0.01 us -> 2.77 us  [the longest x1 2.77 us: local(): other_low = lax.all_gather(released(other_rows, (to_self,)), 'y')]
    ppermute x32 -> x31, waiting for transfers between devices: 63.8 us -> 66.3 us  [shifted(): return lax.ppermute(array, axis, [(i, (i + step) % n) for i in range(n)])]
    another operation x3 -> x6, other arithmetic: 4.64 us -> 5.27 us  [the longest x3 2.72 us: slab_weights(): jnp.stack([near, away])]
    unnamed x53 -> x45, local copies, waits for them, and re-layouts: 6.69 us -> 6.38 us
  transfers between devices with their start and end apart: 35 -> 34, of which waited for: 22 -> 21; matrix products, arithmetic and copies ran while one was open for 7% -> 12% of each run, Pallas kernels for 22% -> 13%
where the time goes in v3:
time: 192 us; the launch traced here: 190 us
  waiting for transfers between devices  69.8 us (36%)
  Pallas kernels  40.4 us (21%)
  starting transfers between devices  37.9 us (20%)
  local copies, waits for them, and re-layouts  17.2 us (9%)
  between operations  13.6 us (7%)
  other arithmetic  10.7 us (6%)
    ppermute x31, waiting for transfers between devices, shifted(): return lax.ppermute(array, axis, [(i, (i + step) % n) for i in range(n)])  66.3 us
    ppermute x31, starting transfers between devices, shifted(): return lax.ppermute(array, axis, [(i, (i + step) % n) for i in range(n)])  37.9 us
    pallas_call x1, Pallas kernels, slab_part(): pl.pallas_call(body, grid=(total // WIDE,), in_specs=[pl.BlockSpec(z.shap...  14.9 us
    pallas_call x1, Pallas kernels, gram_shares(): pl.pallas_call(body, grid=(steps,), in_specs=[pl.BlockSpec((512, step_row...  7.4 us
    pallas_call x1, Pallas kernels, cot_ready(): pl.pallas_call(body, grid=(rows // STEP,), in_specs=[pl.BlockSpec((STEP,...  6.76 us
    unnamed x45, local copies, waits for them, and re-layouts  6.38 us
  transfers between devices with their start and end apart: 34, of which 21 were waited for; matrix products, arithmetic and copies ran while one was open for 12% of the time, Pallas kernels for 13%

profile of v3, /device:TPU:0, one launch (start us, length us, event | category | flops | bytes accessed | tf_op | source)
XLA Modules:
  0.0 190.2 jit_solution(2520746691091067477)
XLA Ops:
  9.5 1.3 gather_fusion
  10.8 2.0 %collective-permute-start.3 = (f32[256,128]{1,0:T(8,128)}, f32[256,128]{1,0:T(8,128)}, u32[]{:S(2)}, u32[]{:S(2)}) collective-permute-start(f32[256,128]{1,0:T(8,128)} %gather_fusion), channel_id=1, source_target_pairs={{0,1},{1,16},{16,17},{17,0},{2,3},{3,18},{18,19},{19,2},{4,5},{5,2... | collective-permute-start | bytes 393224 | tf_op jit(solution)/shard_map/ppermute | solution.py:19
  12.8 2.1 %collective-permute-start.2 = (f32[256,128]{1,0:T(8,128)}, f32[256,128]{1,0:T(8,128)}, u32[]{:S(2)}, u32[]{:S(2)}) collective-permute-start(f32[256,128]{1,0:T(8,128)} %gather_fusion), channel_id=1, source_target_pairs={{0,17},{1,0},{16,1},{17,16},{2,19},{3,2},{18,3},{19,18},{4,21},{5,... | collective-permute-start | bytes 393224 | tf_op jit(solution)/shard_map/ppermute | solution.py:19
  15.0 1.9 collective-permute-start.4
  17.6 1.0 collective-permute-start
  18.6 1.1 slice.13
  19.7 1.0 collective-permute-start.1
  22.2 1.0 broadcast_select_fusion.2
  25.9 5.0 %collective-permute-done.first_ref.refs_0_.refs_1_ = f32[768,128]{1,0:T(8,128)S(1)} collective-permute-done((f32[768,128]{1,0:T(8,128)}, f32[768,128]{1,0:T(8,128)S(1)}, u32[]{:S(2)}, u32[]{:S(2)}) %collective-permute-start) | collective-permute-done | bytes 393248 | tf_op jit(solution)/shard_map/ppermute | solution.py:19
  31.6 2.2 %shard_map.65 = (f32[2,256,256]{2,1,0:T(8,128)}, f32[2304,128]{1,0:T(8,128)}) custom-call(f32[3072,128]{1,0:T(8,128)} %array_ref.1, f32[2,256,256]{2,1,0:T(8,128)} %pad_maximum_fusion.1.small_ref, f32[768,128]{1,0:T(8,128)} %copy-done.4), custom_call_target="tpu_custom_call", output_to_operand_aliasing={{0}: (1, {})} | custom-call | flops 1000 | bytes 1000 | tf_op jit(solution)/shard_map/pallas_call | solution.py:64
  33.9 3.0 %collective-permute-start.7 = (f32[2,256,256]{2,1,0:T(8,128)}, f32[2,256,256]{2,1,0:T(8,128)S(1)}, u32[]{:S(2)}, u32[]{:S(2)}) collective-permute-start(f32[2,256,256]{2,1,0:T(8,128)} %get-tuple-element.14), channel_id=1, source_target_pairs={{0,64},{32,96},{64,0},{96,32},{1,65},{33,97},{65,1},{97,33},{2,66}... | collective-permute-start | bytes 1572872 | tf_op jit(solution)/shard_map/ppermute | solution.py:19
  36.9 1.1 collective-permute-start.6
  39.0 11.5 %collective-permute-done.7 = f32[2,256,256]{2,1,0:T(8,128)S(1)} collective-permute-done((f32[2,256,256]{2,1,0:T(8,128)}, f32[2,256,256]{2,1,0:T(8,128)S(1)}, u32[]{:S(2)}, u32[]{:S(2)}) %collective-permute-start.7) | collective-permute-done | bytes 524320 | tf_op jit(solution)/shard_map/ppermute | solution.py:19
  50.5 7.7 %collective-permute-done.6 = f32[2,256,256]{2,1,0:T(8,128)S(1)} collective-permute-done((f32[2,256,256]{2,1,0:T(8,128)}, f32[2,256,256]{2,1,0:T(8,128)S(1)}, u32[]{:S(2)}, u32[]{:S(2)}) %collective-permute-start.6) | collective-permute-done | bytes 524320 | tf_op jit(solution)/shard_map/ppermute | solution.py:19
  58.2 2.5 %pad_maximum_fusion = f32[4,2,256,256]{3,2,1,0:T(8,128)} fusion(f32[1,2,256,256]{3,2,1,0:T(8,128)S(1)} %bitcast.61, f32[1,2,256,256]{3,2,1,0:T(8,128)S(1)} %bitcast.62, f32[1,2,256,256]{3,2,1,0:T(8,128)S(1)} %bitcast.63, f32[1,2,256,256]{3,2,1,0:T(8,128)} %bitcast.58), kind=kLoop, calls=%fused_computation.3 | loop fusion | flops 1572864 | bytes 4194304 | tf_op jit(solution)/shard_map/stack | solution.py:288
  60.7 3.2 %gather_fusion.1 = f32[512,256]{1,0:T(8,128)S(1)} fusion(f32[2048,256]{1,0:T(8,128)} %bitcast.56, s32[1024]{0:T(1024)S(1)} %pad_clamp_fusion), kind=kCustom, calls=%fused_computation.1 | custom fusion | bytes 1050624 | tf_op jit(solution)/shard_map/jit(_take)/gather | solution.py:301
  64.8 1.0 copy-done.1
  67.0 1.5 collective-permute-done.8
  69.5 3.3 %collective-permute-start.11 = (f32[64,256]{1,0:T(8,128)S(1)}, f32[64,256]{1,0:T(8,128)S(1)}, u32[]{:S(2)}, u32[]{:S(2)}) collective-permute-start(f32[64,256]{1,0:T(8,128)S(1)} %get-tuple-element.32), channel_id=1, source_target_pairs={{0,4},{2,6},{4,0},{6,2},{1,5},{3,7},{5,1},{7,3},{8,12},{10,14},{12... | collective-permute-start | bytes 196616 | tf_op jit(solution)/shard_map/ppermute | solution.py:19
  72.8 1.1 collective-permute-start.10
  74.8 2.6 %collective-permute-done.11 = f32[64,256]{1,0:T(8,128)S(1)} collective-permute-done((f32[64,256]{1,0:T(8,128)S(1)}, f32[64,256]{1,0:T(8,128)S(1)}, u32[]{:S(2)}, u32[]{:S(2)}) %collective-permute-start.11) | collective-permute-done | bytes 65568 | tf_op jit(solution)/shard_map/ppermute | solution.py:19
  77.4 1.9 %collective-permute-done.10 = f32[64,256]{1,0:T(8,128)S(1)} collective-permute-done((f32[64,256]{1,0:T(8,128)S(1)}, f32[64,256]{1,0:T(8,128)S(1)}, u32[]{:S(2)}, u32[]{:S(2)}) %collective-permute-start.10) | collective-permute-done | bytes 65568 | tf_op jit(solution)/shard_map/ppermute | solution.py:19
  81.0 1.6 collective-permute-start.29
  82.6 6.8 %shard_map.64.cot_ref = bf16[512,3072]{1,0:T(8,128)(2,1)} custom-call(f32[3072,128]{1,0:T(8,128)} %own_ref.1, f32[768,128]{1,0:T(8,128)} %copy-done.4, f32[2304,128]{1,0:T(8,128)} %copy-done.1), custom_call_target="tpu_custom_call" | custom-call | flops 1000 | bytes 1000 | tf_op jit(solution)/shard_map/pallas_call | solution.py:118
  89.4 7.4 %shard_map.67 = (f32[4,32,512]{2,1,0:T(8,128)}, f32[4,32,512]{2,1,0:T(8,128)}, f32[4,768,128]{2,1,0:T(8,128)}) custom-call(bf16[512,3072]{1,0:T(8,128)(2,1)} %shard_map.64.cot_ref, f32[4,3072,128]{2,1,0:T(8,128)} %bitcast.54, f32[64,1024]{1,0:T(8,128)} %reshape.232.refs_0_), custom_call_target="tpu_custom_call" | custom-call | flops 1000 | bytes 1000 | tf_op jit(solution)/shard_map/pallas_call | solution.py:166
  96.8 1.7 collective-permute-done.12.came_ref
  99.2 1.8 shard_map.68
  101.0 7.8 %collective-permute-done.29.refs_0_ = f32[2304,128]{1,0:T(8,128)S(1)} collective-permute-done((f32[2304,128]{1,0:T(8,128)}, f32[2304,128]{1,0:T(8,128)S(1)}, u32[]{:S(2)}, u32[]{:S(2)}) %collective-permute-start.29) | collective-permute-done | bytes 1179680 | tf_op jit(solution)/shard_map/ppermute | solution.py:19
  108.8 1.0 copy-done.3
  110.9 1.6 collective-permute-start.13
  112.5 1.7 collective-permute-start.14
  114.2 1.8 collective-permute-start.15
  116.9 3.1 %collective-permute-done.15 = f32[32,512]{1,0:T(8,128)S(1)} collective-permute-done((f32[32,512]{1,0:T(8,128)S(1)}, f32[32,512]{1,0:T(8,128)S(1)}, u32[]{:S(2)}, u32[]{:S(2)}) %collective-permute-start.15) | collective-permute-done | bytes 65568 | tf_op jit(solution)/shard_map/ppermute | solution.py:19
  120.0 2.9 %collective-permute-start.18 = (f32[32,512]{1,0:T(8,128)S(1)}, f32[32,512]{1,0:T(8,128)S(1)}, u32[]{:S(2)}, u32[]{:S(2)}) collective-permute-start(f32[32,512]{1,0:T(8,128)S(1)} %add_add_fusion), channel_id=1, source_target_pairs={{0,17},{1,0},{16,1},{17,16},{2,19},{3,2},{18,3},{19,18},{4,21},{5,... | collective-permute-start | bytes 196616 | tf_op jit(solution)/shard_map/ppermute | solution.py:19
  123.0 2.2 %collective-permute-start.16 = (f32[32,512]{1,0:T(8,128)S(1)}, f32[32,512]{1,0:T(8,128)S(1)}, u32[]{:S(2)}, u32[]{:S(2)}) collective-permute-start(f32[32,512]{1,0:T(8,128)S(1)} %add_add_fusion), channel_id=1, source_target_pairs={{0,16},{1,17},{16,0},{17,1},{2,18},{3,19},{18,2},{19,3},{4,20},{5,... | collective-permute-start | bytes 196616 | tf_op jit(solution)/shard_map/ppermute | solution.py:19
  125.2 3.6 %collective-permute-done.16 = f32[32,512]{1,0:T(8,128)S(1)} collective-permute-done((f32[32,512]{1,0:T(8,128)S(1)}, f32[32,512]{1,0:T(8,128)S(1)}, u32[]{:S(2)}, u32[]{:S(2)}) %collective-permute-start.16) | collective-permute-done | bytes 65568 | tf_op jit(solution)/shard_map/ppermute | solution.py:19
  130.8 1.8 collective-permute-start.21
  132.6 1.1 collective-permute-start.20
  134.6 6.8 %collective-permute-done.21.refs_3_ = f32[32,1024]{1,0:T(8,128)S(1)} collective-permute-done((f32[32,1024]{1,0:T(8,128)S(1)}, f32[32,1024]{1,0:T(8,128)S(1)}, u32[]{:S(2)}, u32[]{:S(2)}) %collective-permute-start.21) | collective-permute-done | bytes 131104 | tf_op jit(solution)/shard_map/ppermute | solution.py:19
  141.4 3.3 %collective-permute-done.20.refs_2_ = f32[32,1024]{1,0:T(8,128)S(1)} collective-permute-done((f32[32,1024]{1,0:T(8,128)S(1)}, f32[32,1024]{1,0:T(8,128)S(1)}, u32[]{:S(2)}, u32[]{:S(2)}) %collective-permute-start.20) | collective-permute-done | bytes 131104 | tf_op jit(solution)/shard_map/ppermute | solution.py:19
  145.3 3.4 %shard_map.69.refs_0_ = f32[128,512]{1,0:T(8,128)} custom-call(f32[32,1024]{1,0:T(8,128)} %fusion.6.refs_0_.refs_1_, f32[32,1024]{1,0:T(8,128)} %collective-permute-done.19.refs_1_, f32[32,1024]{1,0:T(8,128)} %copy-done.16, f32[32,1024]{1,0:T(8,128)} %copy-done.15, f32[512,1024]{1,0:T(8,128)} %all-gather.6.cloned.1.call-done.refs_4_), custom_call_target="tpu_custom_call" | custom-call | flops 1000 | bytes 1000 | tf_op jit(solution)/shard_map/pallas_call | solution.py:191
  148.8 1.5 collective-permute-start.24
  150.2 1.2 collective-permute-start.23
  152.3 5.5 %collective-permute-done.24.refs_3_ = f32[128,512]{1,0:T(8,128)S(1)} collective-permute-done((f32[128,512]{1,0:T(8,128)}, f32[128,512]{1,0:T(8,128)S(1)}, u32[]{:S(2)}, u32[]{:S(2)}) %collective-permute-start.24) | collective-permute-done | bytes 262176 | tf_op jit(solution)/shard_map/ppermute | solution.py:19
  158.3 2.1 %collective-permute-done.22.refs_1_ = f32[128,512]{1,0:T(8,128)S(1)} collective-permute-done((f32[128,512]{1,0:T(8,128)}, f32[128,512]{1,0:T(8,128)S(1)}, u32[]{:S(2)}, u32[]{:S(2)}) %collective-permute-start.22) | collective-permute-done | bytes 262176 | tf_op jit(solution)/shard_map/ppermute | solution.py:19
  162.1 3.8 %shard_map.70.z_ref = bf16[1024,1024]{1,0:T(8,128)(2,1)} custom-call(f32[128,512]{1,0:T(8,128)} %shard_map.69.refs_0_, f32[128,512]{1,0:T(8,128)} %copy-done.9, f32[128,512]{1,0:T(8,128)} %copy-done.8, f32[128,512]{1,0:T(8,128)} %copy-done.7, f32[128,512]{1,0:T(8,128)} %copy-done.10, f32[128,512]{1,0:T(8,128)} %collective-permute-done.26.refs_5_, ...), custom_call_target="tpu_custom_call" | custom-call | flops 1000 | bytes 1000 | tf_op jit(solution)/shard_map/pallas_call | solution.py:217
  166.0 2.8 %all-gather.10.cloned.1.call-done = f32[9216,128]{1,0:T(8,128)} async-done(((f32[2304,128]{1,0:T(8,128)}), f32[9216,128]{1,0:T(8,128)}) %all-gather.10.cloned.1.call-update) | async-done | bytes 4718608 | tf_op jit(solution)/shard_map/all_gather | solution.py:336
  168.7 14.9 %shard_map.74 = f32[512,3072]{1,0:T(8,128)} custom-call(bf16[1024,1024]{1,0:T(8,128)(2,1)} %shard_map.70.z_ref, f32[4,3072,128]{2,1,0:T(8,128)} %bitcast.55, f32[4,2304,128]{2,1,0:T(8,128)} %bitcast.57, f32[4,768,128]{2,1,0:T(8,128)} %copy-done.5), custom_call_target="tpu_custom_call" | custom-call | flops 1000 | bytes 1000 | tf_op jit(solution)/shard_map/pallas_call | solution.py:246
  (132 shorter events, 24.2 us)
Async XLA Ops:
  6.5 3.0 %copy-start = (f32[3072,128]{1,0:T(8,128)S(1)}, f32[3072,128]{1,0:T(8,128)}, u32[]{:S(2)}) copy-start(f32[3072,128]{1,0:T(8,128)} %param.7) | copy-start | bytes 4718596
  6.5 2.3 %copy-start.17 = (s32[4096]{0:T(1024)S(1)}, s32[4096]{0:T(1024)}, u32[]{:S(2)}) copy-start(s32[4096]{0:T(1024)} %param.11) | copy-start | bytes 49156
  6.5 10.3 %copy-start.2 = (f32[3072,128]{1,0:T(8,128)S(1)}, f32[3072,128]{1,0:T(8,128)}, u32[]{:S(2)}) copy-start(f32[3072,128]{1,0:T(8,128)} %own_ref.1) | copy-start | bytes 4718596
  6.5 82.8 %all-gather.8.cloned.1.call-start = ((), (), s32[]{:S(2)}) async-start(), calls=%async_computation.1 | async-start | bytes 7864320 | tf_op jit(solution)/shard_map/all_gather | solution.py:325
  7.3 127.4 %all-gather.6.cloned.1.call-start = ((), (), s32[]{:S(2)}) async-start(), calls=%async_computation | async-start | bytes 2359296 | tf_op jit(solution)/shard_map/all_gather | solution.py:331
  10.8 11.3 %collective-permute-start.3 = (f32[256,128]{1,0:T(8,128)}, f32[256,128]{1,0:T(8,128)}, u32[]{:S(2)}, u32[]{:S(2)}) collective-permute-start(f32[256,128]{1,0:T(8,128)} %gather_fusion), channel_id=1, source_target_pairs={{0,1},{1,16},{16,17},{17,0},{2,3},{3,18},{18,19},{19,2},{4,5},{5,2... | collective-permute-start | bytes 393224 | tf_op jit(solution)/shard_map/ppermute | solution.py:19
  12.8 9.3 %collective-permute-start.2 = (f32[256,128]{1,0:T(8,128)}, f32[256,128]{1,0:T(8,128)}, u32[]{:S(2)}, u32[]{:S(2)}) collective-permute-start(f32[256,128]{1,0:T(8,128)} %gather_fusion), channel_id=1, source_target_pairs={{0,17},{1,0},{16,1},{17,16},{2,19},{3,2},{18,3},{19,18},{4,21},{5,... | collective-permute-start | bytes 393224 | tf_op jit(solution)/shard_map/ppermute | solution.py:19
  15.0 9.2 %collective-permute-start.4 = (f32[256,128]{1,0:T(8,128)}, f32[256,128]{1,0:T(8,128)}, u32[]{:S(2)}, u32[]{:S(2)}) collective-permute-start(f32[256,128]{1,0:T(8,128)} %gather_fusion), channel_id=1, source_target_pairs={{0,16},{1,17},{16,0},{17,1},{2,18},{3,19},{18,2},{19,3},{4,20},{5,... | collective-permute-start | bytes 393224 | tf_op jit(solution)/shard_map/ppermute | solution.py:19
  17.6 13.3 %collective-permute-start = (f32[768,128]{1,0:T(8,128)}, f32[768,128]{1,0:T(8,128)S(1)}, u32[]{:S(2)}, u32[]{:S(2)}) collective-permute-start(f32[768,128]{1,0:T(8,128)} %slice.12), channel_id=1, source_target_pairs={{0,1},{1,0},{2,3},{3,2},{4,5},{5,4},{6,7},{7,6},{8,9},{9,8},{10,11... | collective-permute-start | bytes 1179656 | tf_op jit(solution)/shard_map/ppermute | solution.py:19
  19.7 45.1 %collective-permute-start.1 = (f32[2304,128]{1,0:T(8,128)}, f32[2304,128]{1,0:T(8,128)S(1)}, u32[]{:S(2)}, u32[]{:S(2)}) collective-permute-start(f32[2304,128]{1,0:T(8,128)} %slice.13), channel_id=1, source_target_pairs={{0,1},{1,0},{2,3},{3,2},{4,5},{5,4},{6,7},{7,6},{8,9},{9,8},{10,11... | collective-permute-start | bytes 3538952 | tf_op jit(solution)/shard_map/ppermute | solution.py:19
  33.9 16.6 %collective-permute-start.7 = (f32[2,256,256]{2,1,0:T(8,128)}, f32[2,256,256]{2,1,0:T(8,128)S(1)}, u32[]{:S(2)}, u32[]{:S(2)}) collective-permute-start(f32[2,256,256]{2,1,0:T(8,128)} %get-tuple-element.14), channel_id=1, source_target_pairs={{0,64},{32,96},{64,0},{96,32},{1,65},{33,97},{65,1},{97,33},{2,66}... | collective-permute-start | bytes 1572872 | tf_op jit(solution)/shard_map/ppermute | solution.py:19
  36.9 21.3 %collective-permute-start.6 = (f32[2,256,256]{2,1,0:T(8,128)}, f32[2,256,256]{2,1,0:T(8,128)S(1)}, u32[]{:S(2)}, u32[]{:S(2)}) collective-permute-start(f32[2,256,256]{2,1,0:T(8,128)} %get-tuple-element.14), channel_id=1, source_target_pairs={{0,96},{32,0},{64,32},{96,64},{1,97},{33,1},{65,33},{97,65},{2,98}... | collective-permute-start | bytes 1572872 | tf_op jit(solution)/shard_map/ppermute | solution.py:19
  38.0 20.2 %collective-permute-start.5 = (f32[2,256,256]{2,1,0:T(8,128)}, f32[2,256,256]{2,1,0:T(8,128)S(1)}, u32[]{:S(2)}, u32[]{:S(2)}) collective-permute-start(f32[2,256,256]{2,1,0:T(8,128)} %get-tuple-element.14), channel_id=1, source_target_pairs={{0,32},{32,64},{64,96},{96,0},{1,33},{33,65},{65,97},{97,1},{2,34}... | collective-permute-start | bytes 1572872 | tf_op jit(solution)/shard_map/ppermute | solution.py:19
  64.8 1.0 copy-start.1
  66.9 1.6 collective-permute-start.8
  69.5 7.9 %collective-permute-start.11 = (f32[64,256]{1,0:T(8,128)S(1)}, f32[64,256]{1,0:T(8,128)S(1)}, u32[]{:S(2)}, u32[]{:S(2)}) collective-permute-start(f32[64,256]{1,0:T(8,128)S(1)} %get-tuple-element.32), channel_id=1, source_target_pairs={{0,4},{2,6},{4,0},{6,2},{1,5},{3,7},{5,1},{7,3},{8,12},{10,14},{12... | collective-permute-start | bytes 196616 | tf_op jit(solution)/shard_map/ppermute | solution.py:19
  72.8 6.6 %collective-permute-start.10 = (f32[64,256]{1,0:T(8,128)S(1)}, f32[64,256]{1,0:T(8,128)S(1)}, u32[]{:S(2)}, u32[]{:S(2)}) collective-permute-start(f32[64,256]{1,0:T(8,128)S(1)} %get-tuple-element.33), channel_id=1, source_target_pairs={{0,6},{2,0},{4,2},{6,4},{1,7},{3,1},{5,3},{7,5},{8,14},{10,8},{12,... | collective-permute-start | bytes 196616 | tf_op jit(solution)/shard_map/ppermute | solution.py:19
  73.8 5.9 %collective-permute-start.9 = (f32[64,256]{1,0:T(8,128)S(1)}, f32[64,256]{1,0:T(8,128)S(1)}, u32[]{:S(2)}, u32[]{:S(2)}) collective-permute-start(f32[64,256]{1,0:T(8,128)S(1)} %get-tuple-element.34), channel_id=1, source_target_pairs={{0,2},{2,4},{4,6},{6,0},{1,3},{3,5},{5,7},{7,1},{8,10},{10,12},{12... | collective-permute-start | bytes 196616 | tf_op jit(solution)/shard_map/ppermute | solution.py:19
  80.9 87.8 %all-gather.10.cloned.1.call-start = ((), (), s32[]{:S(2)}) async-start(), calls=%async_computation.2 | async-start | bytes 5898240 | tf_op jit(solution)/shard_map/all_gather | solution.py:336
  81.0 27.9 %collective-permute-start.29 = (f32[2304,128]{1,0:T(8,128)}, f32[2304,128]{1,0:T(8,128)S(1)}, u32[]{:S(2)}, u32[]{:S(2)}) collective-permute-start(f32[2304,128]{1,0:T(8,128)} %shard_map.71), channel_id=1, source_target_pairs={{0,1},{1,0},{2,3},{3,2},{4,5},{5,4},{6,7},{7,6},{8,9},{9,8},{10,11... | collective-permute-start | bytes 3538952 | tf_op jit(solution)/shard_map/ppermute | solution.py:19
  96.8 13.9 %copy-start.18 = (f32[1024]{0:T(1024)S(1)}, f32[1024]{0:T(1024)}, u32[]{:S(2)}) copy-start(f32[1024]{0:T(1024)} %param.9) | copy-start | bytes 12292
  96.8 1.7 collective-permute-start.12
  101.0 9.9 %copy-start.21 = (f32[32,512]{1,0:T(8,128)S(1)}, f32[32,512]{1,0:T(8,128)}, u32[]{:S(2)}) copy-start(f32[32,512]{1,0:T(8,128)} %get-tuple-element.18) | copy-start | bytes 196612
  101.0 11.5 %copy-start.20 = (f32[32,512]{1,0:T(8,128)S(1)}, f32[32,512]{1,0:T(8,128)}, u32[]{:S(2)}) copy-start(f32[32,512]{1,0:T(8,128)} %get-tuple-element.19) | copy-start | bytes 196612
  101.0 13.2 %copy-start.19 = (f32[32,512]{1,0:T(8,128)S(1)}, f32[32,512]{1,0:T(8,128)}, u32[]{:S(2)}) copy-start(f32[32,512]{1,0:T(8,128)} %get-tuple-element.20) | copy-start | bytes 196612
  101.0 19.0 %copy-start.13 = (f32[32,512]{1,0:T(8,128)S(1)}, f32[32,512]{1,0:T(8,128)}, u32[]{:S(2)}) copy-start(f32[32,512]{1,0:T(8,128)} %get-tuple-element.17.refs_1_) | copy-start | bytes 196612
  110.9 5.5 %collective-permute-start.13 = (f32[32,512]{1,0:T(8,128)S(1)}, f32[32,512]{1,0:T(8,128)S(1)}, u32[]{:S(2)}, u32[]{:S(2)}) collective-permute-start(f32[32,512]{1,0:T(8,128)S(1)} %copy-done.21), channel_id=1, source_target_pairs={{0,32},{32,64},{64,96},{96,0},{1,33},{33,65},{65,97},{97,1},{2,34}... | collective-permute-start | bytes 196616 | tf_op jit(solution)/shard_map/ppermute | solution.py:19
  112.5 4.4 %collective-permute-start.14 = (f32[32,512]{1,0:T(8,128)S(1)}, f32[32,512]{1,0:T(8,128)S(1)}, u32[]{:S(2)}, u32[]{:S(2)}) collective-permute-start(f32[32,512]{1,0:T(8,128)S(1)} %copy-done.20), channel_id=1, source_target_pairs={{0,96},{32,0},{64,32},{96,64},{1,97},{33,1},{65,33},{97,65},{2,98}... | collective-permute-start | bytes 196616 | tf_op jit(solution)/shard_map/ppermute | solution.py:19
  114.2 5.8 %collective-permute-start.15 = (f32[32,512]{1,0:T(8,128)S(1)}, f32[32,512]{1,0:T(8,128)S(1)}, u32[]{:S(2)}, u32[]{:S(2)}) collective-permute-start(f32[32,512]{1,0:T(8,128)S(1)} %copy-done.19), channel_id=1, source_target_pairs={{0,64},{32,96},{64,0},{96,32},{1,65},{33,97},{65,1},{97,33},{2,66}... | collective-permute-start | bytes 196616 | tf_op jit(solution)/shard_map/ppermute | solution.py:19
  120.0 8.8 %collective-permute-start.18 = (f32[32,512]{1,0:T(8,128)S(1)}, f32[32,512]{1,0:T(8,128)S(1)}, u32[]{:S(2)}, u32[]{:S(2)}) collective-permute-start(f32[32,512]{1,0:T(8,128)S(1)} %add_add_fusion), channel_id=1, source_target_pairs={{0,17},{1,0},{16,1},{17,16},{2,19},{3,2},{18,3},{19,18},{4,21},{5,... | collective-permute-start | bytes 196616 | tf_op jit(solution)/shard_map/ppermute | solution.py:19
  123.0 6.2 %collective-permute-start.17 = (f32[32,512]{1,0:T(8,128)S(1)}, f32[32,512]{1,0:T(8,128)S(1)}, u32[]{:S(2)}, u32[]{:S(2)}) collective-permute-start(f32[32,512]{1,0:T(8,128)S(1)} %add_add_fusion), channel_id=1, source_target_pairs={{0,1},{1,16},{16,17},{17,0},{2,3},{3,18},{18,19},{19,2},{4,5},{5,2... | collective-permute-start | bytes 196616 | tf_op jit(solution)/shard_map/ppermute | solution.py:19
  123.0 5.9 %collective-permute-start.16 = (f32[32,512]{1,0:T(8,128)S(1)}, f32[32,512]{1,0:T(8,128)S(1)}, u32[]{:S(2)}, u32[]{:S(2)}) collective-permute-start(f32[32,512]{1,0:T(8,128)S(1)} %add_add_fusion), channel_id=1, source_target_pairs={{0,16},{1,17},{16,0},{17,1},{2,18},{3,19},{18,2},{19,3},{4,20},{5,... | collective-permute-start | bytes 196616 | tf_op jit(solution)/shard_map/ppermute | solution.py:19
  129.9 36.1 %collective-permute-start.30 = (f32[4,768,128]{2,1,0:T(8,128)}, f32[4,768,128]{2,1,0:T(8,128)S(1)}, u32[]{:S(2)}, u32[]{:S(2)}) collective-permute-start(f32[4,768,128]{2,1,0:T(8,128)} %shard_map.73), channel_id=1, source_target_pairs={{0,1},{1,0},{2,3},{3,2},{4,5},{5,4},{6,7},{7,6},{8,9},{9,8},{10,11... | collective-permute-start | bytes 4718600 | tf_op jit(solution)/shard_map/ppermute | solution.py:19
  130.8 10.6 %collective-permute-start.21 = (f32[32,1024]{1,0:T(8,128)S(1)}, f32[32,1024]{1,0:T(8,128)S(1)}, u32[]{:S(2)}, u32[]{:S(2)}) collective-permute-start(f32[32,1024]{1,0:T(8,128)S(1)} %copy-done.6), channel_id=1, source_target_pairs={{0,4},{2,6},{4,0},{6,2},{1,5},{3,7},{5,1},{7,3},{8,12},{10,14},{12... | collective-permute-start | bytes 393224 | tf_op jit(solution)/shard_map/ppermute | solution.py:19
  132.6 12.1 %collective-permute-start.20 = (f32[32,1024]{1,0:T(8,128)S(1)}, f32[32,1024]{1,0:T(8,128)S(1)}, u32[]{:S(2)}, u32[]{:S(2)}) collective-permute-start(f32[32,1024]{1,0:T(8,128)S(1)} %copy-done.6), channel_id=1, source_target_pairs={{0,6},{2,0},{4,2},{6,4},{1,7},{3,1},{5,3},{7,5},{8,14},{10,8},{12,... | collective-permute-start | bytes 393224 | tf_op jit(solution)/shard_map/ppermute | solution.py:19
  133.7 11.0 %collective-permute-start.19 = (f32[32,1024]{1,0:T(8,128)S(1)}, f32[32,1024]{1,0:T(8,128)}, u32[]{:S(2)}, u32[]{:S(2)}) collective-permute-start(f32[32,1024]{1,0:T(8,128)S(1)} %copy-done.6), channel_id=1, source_target_pairs={{0,2},{2,4},{4,6},{6,0},{1,3},{3,5},{5,7},{7,1},{8,10},{10,12},{12... | collective-permute-start | bytes 393224 | tf_op jit(solution)/shard_map/ppermute | solution.py:19
  141.4 3.3 %copy-start.15 = (f32[32,1024]{1,0:T(8,128)}, f32[32,1024]{1,0:T(8,128)S(1)}, u32[]{:S(2)}) copy-start(f32[32,1024]{1,0:T(8,128)S(1)} %collective-permute-done.21.refs_3_) | copy-start | bytes 393220
  148.8 9.0 %collective-permute-start.24 = (f32[128,512]{1,0:T(8,128)}, f32[128,512]{1,0:T(8,128)S(1)}, u32[]{:S(2)}, u32[]{:S(2)}) collective-permute-start(f32[128,512]{1,0:T(8,128)} %shard_map.69.refs_0_), channel_id=1, source_target_pairs={{0,64},{32,96},{64,0},{96,32},{1,65},{33,97},{65,1},{97,33},{2,66}... | collective-permute-start | bytes 786440 | tf_op jit(solution)/shard_map/ppermute | solution.py:19
  150.2 8.1 %collective-permute-start.23 = (f32[128,512]{1,0:T(8,128)}, f32[128,512]{1,0:T(8,128)S(1)}, u32[]{:S(2)}, u32[]{:S(2)}) collective-permute-start(f32[128,512]{1,0:T(8,128)} %shard_map.69.refs_0_), channel_id=1, source_target_pairs={{0,96},{32,0},{64,32},{96,64},{1,97},{33,1},{65,33},{97,65},{2,98}... | collective-permute-start | bytes 786440 | tf_op jit(solution)/shard_map/ppermute | solution.py:19
  151.4 9.0 %collective-permute-start.22 = (f32[128,512]{1,0:T(8,128)}, f32[128,512]{1,0:T(8,128)S(1)}, u32[]{:S(2)}, u32[]{:S(2)}) collective-permute-start(f32[128,512]{1,0:T(8,128)} %shard_map.69.refs_0_), channel_id=1, source_target_pairs={{0,32},{32,64},{64,96},{96,0},{1,33},{33,65},{65,97},{97,1},{2,34}... | collective-permute-start | bytes 786440 | tf_op jit(solution)/shard_map/ppermute | solution.py:19
  152.3 8.2 %collective-permute-start.25 = (f32[128,512]{1,0:T(8,128)}, f32[128,512]{1,0:T(8,128)S(1)}, u32[]{:S(2)}, u32[]{:S(2)}) collective-permute-start(f32[128,512]{1,0:T(8,128)} %shard_map.69.refs_0_), channel_id=1, source_target_pairs={{0,8},{8,0},{1,9},{9,1},{2,10},{10,2},{3,11},{11,3},{4,12},{12,4},... | collective-permute-start | bytes 786440 | tf_op jit(solution)/shard_map/ppermute | solution.py:19
  157.8 4.4 %copy-start.7 = (f32[128,512]{1,0:T(8,128)}, f32[128,512]{1,0:T(8,128)S(1)}, u32[]{:S(2)}) copy-start(f32[128,512]{1,0:T(8,128)S(1)} %collective-permute-done.24.refs_3_) | copy-start | bytes 786436
  157.8 2.7 %collective-permute-start.28 = (f32[128,512]{1,0:T(8,128)S(1)}, f32[128,512]{1,0:T(8,128)S(1)}, u32[]{:S(2)}, u32[]{:S(2)}) collective-permute-start(f32[128,512]{1,0:T(8,128)S(1)} %collective-permute-done.24.refs_3_), channel_id=1, source_target_pairs={{0,8},{8,0},{1,9},{9,1},{2,10},{10,2},{3,11},{11,3},{4,12},{12,4},... | collective-permute-start | bytes 786440 | tf_op jit(solution)/shard_map/ppermute | solution.py:19
  158.3 3.8 %copy-start.8 = (f32[128,512]{1,0:T(8,128)}, f32[128,512]{1,0:T(8,128)S(1)}, u32[]{:S(2)}) copy-start(f32[128,512]{1,0:T(8,128)S(1)} %collective-permute-done.23.refs_2_) | copy-start | bytes 786436
  158.3 2.2 %collective-permute-start.27 = (f32[128,512]{1,0:T(8,128)S(1)}, f32[128,512]{1,0:T(8,128)S(1)}, u32[]{:S(2)}, u32[]{:S(2)}) collective-permute-start(f32[128,512]{1,0:T(8,128)S(1)} %collective-permute-done.23.refs_2_), channel_id=1, source_target_pairs={{0,8},{8,0},{1,9},{9,1},{2,10},{10,2},{3,11},{11,3},{4,12},{12,4},... | collective-permute-start | bytes 786440 | tf_op jit(solution)/shard_map/ppermute | solution.py:19
  160.5 1.7 copy-start.9
  160.5 1.7 collective-permute-start.26
  166.0 2.8 %copy-start.5 = (f32[4,768,128]{2,1,0:T(8,128)}, f32[4,768,128]{2,1,0:T(8,128)S(1)}, u32[]{:S(2)}) copy-start(f32[4,768,128]{2,1,0:T(8,128)S(1)} %collective-permute-done.30.high_ref) | copy-start | bytes 4718596
  (8 other events, 6.2 us)
Sparse Core Ops, SparseCore 0:
  9.0 70.3 all-gather.7
  81.1 26.3 all-gather.5
  110.0 58.7 all-gather.9

commit v4 on v3

--- a/solution.py
+++ b/solution.py
@@ -55,21 +55,28 @@
 PARAMS = pltpu.CompilerParams(vmem_limit_bytes=VMEM)
 
 
-def with_rows(small, array, count, after):
-    rows = count // 2
+def with_pieces(small, array, cut, after):
+    rows = cut // 2
 
     def body(array_ref, small_ref, *refs):
-        refs[-1][...] = array_ref[...]
-
+        first, second = refs[-2:]
+        step = pl.program_id(0)
+
+        @pl.when(step == 0)
+        def _():
+            first[...] = array_ref[...]
+
+        @pl.when(step == 1)
+        def _():
+            second[...] = array_ref[...]
+
+    piece = jax.ShapeDtypeStruct((rows, 128), array.dtype)
     return pl.pallas_call(
         body,
         grid=(2,),
         in_specs=[pl.BlockSpec((rows, 128), lambda i: (i, 0)), ANY] + [ANY] * len(after),
-        out_specs=[ANY, pl.BlockSpec((rows, 128), lambda i: (i, 0))],
-        out_shape=[
-            jax.ShapeDtypeStruct(small.shape, small.dtype),
-            jax.ShapeDtypeStruct((count, 128), array.dtype),
-        ],
+        out_specs=[ANY] + [pl.BlockSpec((rows, 128), lambda i: (0, 0))] * 2,
+        out_shape=[jax.ShapeDtypeStruct(small.shape, small.dtype), piece, piece],
         input_output_aliases={1: 0},
         compiler_params=PARAMS,
         cost_estimate=SMALL,
@@ -104,6 +111,29 @@
         compiler_params=PARAMS,
         cost_estimate=SMALL,
     )(kept, came, *after)
+
+
+def joined(first, second, after):
+    rows = first.shape[0]
+
+    def body(first_ref, second_ref, *refs):
+        @pl.when(pl.program_id(0) == 0)
+        def _():
+            refs[-1][...] = first_ref[...]
+
+        @pl.when(pl.program_id(0) == 1)
+        def _():
+            refs[-1][...] = second_ref[...]
+
+    return pl.pallas_call(
+        body,
+        grid=(2,),
+        in_specs=[pl.BlockSpec((rows, 128), lambda i: (0, 0))] * 2 + [ANY] * len(after),
+        out_specs=pl.BlockSpec((rows, 128), lambda i: (i, 0)),
+        out_shape=jax.ShapeDtypeStruct((2 * rows, 128), first.dtype),
+        compiler_params=PARAMS,
+        cost_estimate=SMALL,
+    )(first, second, *after)
 
 
 def cot_ready(own, first, second):
@@ -126,7 +156,7 @@
         out_specs=pl.BlockSpec((512, STEP), lambda i: (0, i)),
         out_shape=jax.ShapeDtypeStruct((512, rows), jnp.bfloat16),
         compiler_params=PARAMS,
-        cost_estimate=SMALL,
+        cost_estimate=pl.CostEstimate(flops=1000, bytes_accessed=rows * 4096, transcendentals=0),
     )(own, first, second)
 
 
@@ -177,24 +207,27 @@
     )(cot, whole_x, *after)
 
 
-def z_part(weighted, picked):
-    height, depth = picked.shape
+def z_part(weighted, own, other):
+    count, share, depth = own.shape
 
     def body(*refs):
-        weighted_refs, picked_ref = refs[:4], refs[4]
-        out, tall = refs[-2:]
-        y = lax.axis_index("y")
+        weighted_refs, own_ref, other_ref = refs[:4], refs[4], refs[5]
+        out, tall, rows = refs[-3:]
+        y, c = lax.axis_index("y"), lax.axis_index("c")
         for slot, offset in enumerate((0, 3, 1, 2)):
             tall[pl.ds(pl.multiple_of(lax.rem(y + offset, 4) * 32, 32), 32), :] = weighted_refs[slot][...]
-        out[...] = three_pass(jnp.concatenate(split(tall[...]), axis=0), split(picked_ref[...]), ((1,), (1,)))
-
-    return pl.pallas_call(
-        body,
-        out_shape=jax.ShapeDtypeStruct((128, height), jnp.float32),
-        scratch_shapes=[pltpu.VMEM((128, depth), jnp.float32)],
-        compiler_params=PARAMS,
-        cost_estimate=SMALL,
-    )(*weighted, picked)
+        for k in range(count):
+            for which, ref in ((c, own_ref), (1 - c, other_ref)):
+                rows[pl.ds(pl.multiple_of((k * 2 + which) * share, share), share), :] = ref[k]
+        out[...] = three_pass(jnp.concatenate(split(tall[...]), axis=0), split(rows[...]), ((1,), (1,)))
+
+    return pl.pallas_call(
+        body,
+        out_shape=jax.ShapeDtypeStruct((128, 2 * count * share), jnp.float32),
+        scratch_shapes=[pltpu.VMEM((128, depth), jnp.float32), pltpu.VMEM((2 * count * share, depth), jnp.float32)],
+        compiler_params=PARAMS,
+        cost_estimate=SMALL,
+    )(*weighted, own, other)
 
 
 def z_ready(own_z, other_z):
@@ -223,40 +256,62 @@
     )(*own_z, *other_z)
 
 
-def slab_part(z, own_x, other_low, other_high):
+def slab_own(z, own_x):
     total = own_x.shape[1]
-    split_at = other_low.shape[1] // WIDE
-    height, depth = z.shape[0] // 2, z.shape[1]
-
-    def body(z_ref, own_ref, low_ref, high_ref, out):
-        step = pl.program_id(0)
-
-        def product(other_ref):
-            x_tile = split(jnp.concatenate([wide(own_ref), wide(other_ref)], axis=1))
-            out[...] = three_pass(z_ref[...], x_tile, ((1,), (1,)))
-
-        @pl.when(step < split_at)
-        def _():
-            product(low_ref)
-
-        @pl.when(step >= split_at)
-        def _():
-            product(high_ref)
+    height, depth = z.shape[0] // 2, z.shape[1] // 2
+
+    def body(z_ref, own_ref, out):
+        out[...] = three_pass(z_ref[...], split(wide(own_ref)), ((1,), (1,)))
 
     return pl.pallas_call(
         body,
         grid=(total // WIDE,),
         in_specs=[
-            pl.BlockSpec(z.shape, lambda i: (0, 0)),
+            pl.BlockSpec((2 * height, depth), lambda i: (0, 0)),
             pl.BlockSpec((4, WIDE, 128), lambda i: (0, i, 0)),
-            pl.BlockSpec((4, WIDE, 128), lambda i: (0, jnp.minimum(i, split_at - 1), 0)),
-            pl.BlockSpec((4, WIDE, 128), lambda i: (0, jnp.maximum(i - split_at, 0), 0)),
         ],
         out_specs=pl.BlockSpec((height, WIDE), lambda i: (0, i)),
         out_shape=jax.ShapeDtypeStruct((height, total), jnp.float32),
         compiler_params=PARAMS,
-        cost_estimate=SMALL,
-    )(z, own_x, other_low, other_high)
+        cost_estimate=pl.CostEstimate(flops=1000, bytes_accessed=1 << 24, transcendentals=0),
+    )(z, own_x)
+
+
+def slab_other(z, other_low, other_high, slab):
+    total = slab.shape[1]
+    split_at = other_low.shape[1] // WIDE
+    height, depth = z.shape[0] // 2, z.shape[1] // 2
+
+    def body(z_ref, low_ref, high_ref, slab_ref, out):
+        step = pl.program_id(0)
+
+        def product(other_ref):
+            out[...] = slab_ref[...] + three_pass(z_ref[...], split(wide(other_ref)), ((1,), (1,)))
+
+        @pl.when(step < split_at)
+        def _():
+            product(low_ref)
+
+        @pl.when(step >= split_at)
+        def _():
+            product(high_ref)
+
+    tile = pl.BlockSpec((height, WIDE), lambda i: (0, i))
+    return pl.pallas_call(
+        body,
+        grid=(total // WIDE,),
+        in_specs=[
+            pl.BlockSpec((2 * height, depth), lambda i: (0, 1)),
+            pl.BlockSpec((4, WIDE, 128), lambda i: (0, jnp.minimum(i, split_at - 1), 0)),
+            pl.BlockSpec((4, WIDE, 128), lambda i: (0, jnp.maximum(i - split_at, 0), 0)),
+            tile,
+        ],
+        out_specs=tile,
+        out_shape=jax.ShapeDtypeStruct(slab.shape, slab.dtype),
+        input_output_aliases={3: 0},
+        compiler_params=PARAMS,
+        cost_estimate=SMALL,
+    )(z, other_low, other_high, slab)
 
 
 def places(slab_rows, height, count):
@@ -284,7 +339,7 @@
     own, below, above, far = ring_parts(jnp.take(weights, local_rows, axis=0, mode="clip"), ("zh", "zl"))
     near = jnp.concatenate([own, jnp.where(zl == 0, above, below)], axis=1)
     away = jnp.concatenate([far, jnp.where(zl == 0, below, above)], axis=1)
-    pair, first_rows = with_rows(jnp.stack([near, away]), mode_vectors, cut, cots[:1])
+    pair, *pieces = with_pieces(jnp.stack([near, away]), mode_vectors, cut, cots[:1])
     ring = jnp.stack(ring_parts(pair, "x")).reshape(-1, 256)
     share = total // 64
     places_here = pick(place.reshape(4, 2, 4, 2, share).swapaxes(0, 1), zl)
@@ -301,7 +356,7 @@
     taken = jnp.take(ring, jnp.concatenate(numbers), axis=0, mode="clip")
     taken = jnp.where(jnp.concatenate(mine)[:, None], taken, 0.0).reshape(2, 4, share, 256)
     taken = released(taken, cots[1:])
-    return taken[0] + shifted(taken[1], "c", 1), first_rows
+    return taken[0] + shifted(taken[1], "c", 1), pieces
 
 
 def slab_share(chosen, y):
@@ -325,15 +380,17 @@
     own_x = lax.all_gather(mode_vectors, "y")
     early = rows // 4
     cots = (shifted(cotangent[:early], "zl", 1), shifted(cotangent[early:], "zl", 1))
-    chosen, first_rows = slab_weights(weights, slab_rows, x, zh, c, zl, cots, mode_vectors, cut)
-    other_rows = shifted(released(first_rows, cots), "zl", 1)
+    chosen, pieces = slab_weights(weights, slab_rows, x, zh, c, zl, cots, mode_vectors, cut)
+    other_first, other_second = (shifted(piece, "zl", 1) for piece in pieces)
     share = slab_share(chosen, y)
-    picked = lax.all_gather(share, ("x", "c"), tiled=True)
     cot = cot_ready(cotangent, *cots)
+    share = released(share, (other_first, cot))
+    own_picked = lax.all_gather(share, "x")
+    other_picked = shifted(own_picked, "c", 1)
 
     kept, sent, tail = gram_shares(cot, own_x, cut, (share,))
     to_self, to_above, to_below, to_far = x_parts(kept, shifted(sent, "c", 1), ())
-    other_low = lax.all_gather(released(other_rows, (to_self,)), "y")
+    other_low = lax.all_gather(joined(other_first, other_second, (to_self,)), "y")
     total = to_self + shifted(to_above, "x", 1) + shifted(to_below, "x", -1) + shifted(to_far, "x", 2)
     own, below, above, far = ring_parts(total, ("zh", "zl"))
     total = jnp.concatenate([own + far, below + above], axis=1)
@@ -350,10 +407,10 @@
     weighted = factor * total + jnp.where(j_ids == i_ids, slope_j[:, None], 0.0)
 
     other_high = shifted(released(tail, (weighted,)), "zl", 1)
-    z_own = ring_parts(z_part(ring_parts(weighted, "y"), picked), "x")
+    z_own = ring_parts(z_part(ring_parts(weighted, "y"), own_picked, other_picked), "x")
     z_other = [shifted(part, "c", 1) for part in z_own]
     z = z_ready(z_own, z_other)
-    return slab_part(z, own_x, other_low, other_high)
+    return slab_other(z, other_low, other_high, slab_own(z, own_x))
 
 
 def solution(mesh):

time: 192 us -> 189 us (0.984)
  waiting for transfers between devices: 69.8 us -> 55.6 us
  Pallas kernels: 40.4 us -> 48 us
    ppermute x31 -> x33, waiting for transfers between devices: 66.3 us -> 53.3 us  [shifted(): return lax.ppermute(array, axis, [(i, (i + step) % n) for i in range(n)])]
    pallas_call x3 -> x5, Pallas kernels: 20.6 us -> 28.3 us  [the longest x1 10.7 us: slab_other(): pl.pallas_call(body, grid=(total // WIDE,), in_specs=[pl.BlockSpec((2 * h...]
    ppermute x31 -> x33, starting transfers between devices: 37.9 us -> 39.6 us  [shifted(): return lax.ppermute(array, axis, [(i, (i + step) % n) for i in range(n)])]
    unnamed x45 -> x53, local copies, waits for them, and re-layouts: 6.38 us -> 7.67 us
  transfers between devices with their start and end apart: 34 -> 36, of which waited for: 21 -> 18; matrix products, arithmetic and copies ran while one was open for 12% -> 12% of each run, Pallas kernels for 13% -> 20%
where the time goes in v4:
time: 189 us; the launch traced here: 187 us
  waiting for transfers between devices  55.6 us (29%)
  Pallas kernels  48 us (25%)
  starting transfers between devices  39.7 us (21%)
  local copies, waits for them, and re-layouts  18.7 us (10%)
  between operations  13.6 us (7%)
  other arithmetic  10.8 us (6%)
    ppermute x33, waiting for transfers between devices, shifted(): return lax.ppermute(array, axis, [(i, (i + step) % n) for i in range(n)])  53.3 us
    ppermute x33, starting transfers between devices, shifted(): return lax.ppermute(array, axis, [(i, (i + step) % n) for i in range(n)])  39.6 us
    pallas_call x1, Pallas kernels, slab_other(): pl.pallas_call(body, grid=(total // WIDE,), in_specs=[pl.BlockSpec((2 * h...  10.7 us
    pallas_call x1, Pallas kernels, slab_own(): pl.pallas_call(body, grid=(total // WIDE,), in_specs=[pl.BlockSpec((2 * h...  9.25 us
    unnamed x53, local copies, waits for them, and re-layouts  7.67 us
    pallas_call x1, Pallas kernels, gram_shares(): pl.pallas_call(body, grid=(steps,), in_specs=[pl.BlockSpec((512, step_row...  7.36 us
    pallas_call x1, Pallas kernels, cot_ready(): pl.pallas_call(body, grid=(rows // STEP,), in_specs=[pl.BlockSpec((STEP,...  6.76 us
    pallas_call x1, Pallas kernels, z_ready(): pl.pallas_call(body, out_shape=jax.ShapeDtypeStruct((2 * height, depth),...  3.83 us
  transfers between devices with their start and end apart: 36, of which 18 were waited for; matrix products, arithmetic and copies ran while one was open for 12% of the time, Pallas kernels for 20%

profile of v4, /device:TPU:0, one launch (start us, length us, event | category | flops | bytes accessed | tf_op | source)
XLA Modules:
  0.0 186.9 jit_solution(14550910339764223702)
XLA Ops:
  9.5 1.3 gather_fusion
  10.9 2.0 %collective-permute-start.3 = (f32[256,128]{1,0:T(8,128)}, f32[256,128]{1,0:T(8,128)}, u32[]{:S(2)}, u32[]{:S(2)}) collective-permute-start(f32[256,128]{1,0:T(8,128)} %gather_fusion), channel_id=1, source_target_pairs={{0,1},{1,16},{16,17},{17,0},{2,3},{3,18},{18,19},{19,2},{4,5},{5,2... | collective-permute-start | bytes 393224 | tf_op jit(solution)/shard_map/ppermute | solution.py:19
  12.9 2.1 %collective-permute-start.2 = (f32[256,128]{1,0:T(8,128)}, f32[256,128]{1,0:T(8,128)}, u32[]{:S(2)}, u32[]{:S(2)}) collective-permute-start(f32[256,128]{1,0:T(8,128)} %gather_fusion), channel_id=1, source_target_pairs={{0,17},{1,0},{16,1},{17,16},{2,19},{3,2},{18,3},{19,18},{4,21},{5,... | collective-permute-start | bytes 393224 | tf_op jit(solution)/shard_map/ppermute | solution.py:19
  15.0 1.9 collective-permute-start.4
  17.6 1.0 collective-permute-start
  18.6 1.1 slice.13
  19.8 1.0 collective-permute-start.1
  22.4 1.0 broadcast_select_fusion.2
  26.2 4.8 %collective-permute-done.first_ref.refs_0_ = f32[768,128]{1,0:T(8,128)S(1)} collective-permute-done((f32[768,128]{1,0:T(8,128)}, f32[768,128]{1,0:T(8,128)S(1)}, u32[]{:S(2)}, u32[]{:S(2)}) %collective-permute-start) | collective-permute-done | bytes 393248 | tf_op jit(solution)/shard_map/ppermute | solution.py:19
  31.7 2.4 %shard_map.65 = (f32[2,256,256]{2,1,0:T(8,128)}, f32[1152,128]{1,0:T(8,128)}, f32[1152,128]{1,0:T(8,128)}) custom-call(f32[3072,128]{1,0:T(8,128)} %array_ref.1, f32[2,256,256]{2,1,0:T(8,128)} %pad_maximum_fusion.1.small_ref, f32[768,128]{1,0:T(8,128)} %copy-done.5), custom_call_target="tpu_custom_call", output_to_operand_aliasing={{0}: (1, {})} | custom-call | flops 1000 | bytes 1000 | tf_op jit(solution)/shard_map/pallas_call | solution.py:74
  34.0 3.0 %collective-permute-start.7 = (f32[2,256,256]{2,1,0:T(8,128)}, f32[2,256,256]{2,1,0:T(8,128)S(1)}, u32[]{:S(2)}, u32[]{:S(2)}) collective-permute-start(f32[2,256,256]{2,1,0:T(8,128)} %get-tuple-element.15), channel_id=1, source_target_pairs={{0,64},{32,96},{64,0},{96,32},{1,65},{33,97},{65,1},{97,33},{2,66}... | collective-permute-start | bytes 1572872 | tf_op jit(solution)/shard_map/ppermute | solution.py:19
  37.1 1.1 collective-permute-start.6
  39.2 11.5 %collective-permute-done.7 = f32[2,256,256]{2,1,0:T(8,128)S(1)} collective-permute-done((f32[2,256,256]{2,1,0:T(8,128)}, f32[2,256,256]{2,1,0:T(8,128)S(1)}, u32[]{:S(2)}, u32[]{:S(2)}) %collective-permute-start.7) | collective-permute-done | bytes 524320 | tf_op jit(solution)/shard_map/ppermute | solution.py:19
  50.7 7.7 %collective-permute-done.6 = f32[2,256,256]{2,1,0:T(8,128)S(1)} collective-permute-done((f32[2,256,256]{2,1,0:T(8,128)}, f32[2,256,256]{2,1,0:T(8,128)S(1)}, u32[]{:S(2)}, u32[]{:S(2)}) %collective-permute-start.6) | collective-permute-done | bytes 524320 | tf_op jit(solution)/shard_map/ppermute | solution.py:19
  58.4 2.5 %pad_maximum_fusion = f32[4,2,256,256]{3,2,1,0:T(8,128)} fusion(f32[1,2,256,256]{3,2,1,0:T(8,128)S(1)} %bitcast.64, f32[1,2,256,256]{3,2,1,0:T(8,128)S(1)} %bitcast.65, f32[1,2,256,256]{3,2,1,0:T(8,128)S(1)} %bitcast.66, f32[1,2,256,256]{3,2,1,0:T(8,128)} %bitcast.59), kind=kLoop, calls=%fused_computation.3 | loop fusion | flops 1572864 | bytes 4194304 | tf_op jit(solution)/shard_map/stack | solution.py:343
  60.9 3.2 %gather_fusion.1 = f32[512,256]{1,0:T(8,128)S(1)} fusion(f32[2048,256]{1,0:T(8,128)} %bitcast.57, s32[1024]{0:T(1024)S(1)} %pad_clamp_fusion), kind=kCustom, calls=%fused_computation.1 | custom fusion | bytes 1050624 | tf_op jit(solution)/shard_map/jit(_take)/gather | solution.py:356
  65.0 1.1 copy-done.2
  68.7 1.0 fusion.3
  69.7 3.3 %collective-permute-start.11 = (f32[64,256]{1,0:T(8,128)S(1)}, f32[64,256]{1,0:T(8,128)S(1)}, u32[]{:S(2)}, u32[]{:S(2)}) collective-permute-start(f32[64,256]{1,0:T(8,128)S(1)} %get-tuple-element.34), channel_id=1, source_target_pairs={{0,4},{2,6},{4,0},{6,2},{1,5},{3,7},{5,1},{7,3},{8,12},{10,14},{12... | collective-permute-start | bytes 196616 | tf_op jit(solution)/shard_map/ppermute | solution.py:19
  72.9 1.1 collective-permute-start.10
  74.0 1.0 collective-permute-start.9
  75.0 6.8 %shard_map.64.refs_2_.cot_ref = bf16[512,3072]{1,0:T(8,128)(2,1)} custom-call(f32[3072,128]{1,0:T(8,128)} %own_ref.1, f32[768,128]{1,0:T(8,128)} %copy-done.5, f32[2304,128]{1,0:T(8,128)} %copy-done.2), custom_call_target="tpu_custom_call" | custom-call | flops 1000 | bytes 12582912 | tf_op jit(solution)/shard_map/pallas_call | solution.py:148
  84.9 7.4 %shard_map.68 = (f32[4,32,512]{2,1,0:T(8,128)}, f32[4,32,512]{2,1,0:T(8,128)}, f32[4,768,128]{2,1,0:T(8,128)}) custom-call(bf16[512,3072]{1,0:T(8,128)(2,1)} %shard_map.64.refs_2_.cot_ref, f32[4,3072,128]{2,1,0:T(8,128)} %bitcast.55, f32[64,1024]{1,0:T(8,128)} %shard_map.67.refs_0_), custom_call_target="tpu_custom_call" | custom-call | flops 1000 | bytes 1000 | tf_op jit(solution)/shard_map/pallas_call | solution.py:196
  92.3 1.7 collective-permute-done.13.came_ref
  94.7 1.7 shard_map.69
  96.5 2.2 %collective-permute-done.31.second_ref = f32[1152,128]{1,0:T(8,128)S(1)} collective-permute-done((f32[1152,128]{1,0:T(8,128)S(1)}, f32[1152,128]{1,0:T(8,128)S(1)}, u32[]{:S(2)}, u32[]{:S(2)}) %collective-permute-start.31) | collective-permute-done | bytes 589856 | tf_op jit(solution)/shard_map/ppermute | solution.py:19
  99.5 2.3 %shard_map.72 = f32[2304,128]{1,0:T(8,128)} custom-call(f32[1152,128]{1,0:T(8,128)} %copy-done.3, f32[1152,128]{1,0:T(8,128)} %copy-done.7, f32[32,512]{1,0:T(8,128)} %get-tuple-element.19.refs_0_), custom_call_target="tpu_custom_call" | custom-call | flops 1000 | bytes 1000 | tf_op jit(solution)/shard_map/pallas_call | solution.py:128
  102.9 1.5 collective-permute-start.14
  104.4 1.8 collective-permute-start.15
  106.2 1.7 collective-permute-start.16
  107.9 1.8 collective-permute-done.14
  109.7 2.3 %collective-permute-done.16 = f32[32,512]{1,0:T(8,128)S(1)} collective-permute-done((f32[32,512]{1,0:T(8,128)S(1)}, f32[32,512]{1,0:T(8,128)S(1)}, u32[]{:S(2)}, u32[]{:S(2)}) %collective-permute-start.16) | collective-permute-done | bytes 65568 | tf_op jit(solution)/shard_map/ppermute | solution.py:19
  112.0 2.5 %collective-permute-start.19 = (f32[32,512]{1,0:T(8,128)S(1)}, f32[32,512]{1,0:T(8,128)S(1)}, u32[]{:S(2)}, u32[]{:S(2)}) collective-permute-start(f32[32,512]{1,0:T(8,128)S(1)} %add_add_fusion), channel_id=1, source_target_pairs={{0,17},{1,0},{16,1},{17,16},{2,19},{3,2},{18,3},{19,18},{4,21},{5,... | collective-permute-start | bytes 196616 | tf_op jit(solution)/shard_map/ppermute | solution.py:19
  114.5 2.8 %collective-permute-start.17 = (f32[32,512]{1,0:T(8,128)S(1)}, f32[32,512]{1,0:T(8,128)S(1)}, u32[]{:S(2)}, u32[]{:S(2)}) collective-permute-start(f32[32,512]{1,0:T(8,128)S(1)} %add_add_fusion), channel_id=1, source_target_pairs={{0,16},{1,17},{16,0},{17,1},{2,18},{3,19},{18,2},{19,3},{4,20},{5,... | collective-permute-start | bytes 196616 | tf_op jit(solution)/shard_map/ppermute | solution.py:19
  117.3 3.1 %collective-permute-done.17 = f32[32,512]{1,0:T(8,128)S(1)} collective-permute-done((f32[32,512]{1,0:T(8,128)S(1)}, f32[32,512]{1,0:T(8,128)S(1)}, u32[]{:S(2)}, u32[]{:S(2)}) %collective-permute-start.17) | collective-permute-done | bytes 65568 | tf_op jit(solution)/shard_map/ppermute | solution.py:19
  122.4 3.2 %collective-permute-start.22 = (f32[32,1024]{1,0:T(8,128)S(1)}, f32[32,1024]{1,0:T(8,128)S(1)}, u32[]{:S(2)}, u32[]{:S(2)}) collective-permute-start(f32[32,1024]{1,0:T(8,128)S(1)} %copy-done.6), channel_id=1, source_target_pairs={{0,4},{2,6},{4,0},{6,2},{1,5},{3,7},{5,1},{7,3},{8,12},{10,14},{12... | collective-permute-start | bytes 393224 | tf_op jit(solution)/shard_map/ppermute | solution.py:19
  125.5 1.1 collective-permute-start.21
  127.6 4.3 %collective-permute-done.22.refs_3_ = f32[32,1024]{1,0:T(8,128)S(1)} collective-permute-done((f32[32,1024]{1,0:T(8,128)S(1)}, f32[32,1024]{1,0:T(8,128)S(1)}, u32[]{:S(2)}, u32[]{:S(2)}) %collective-permute-start.22) | collective-permute-done | bytes 131104 | tf_op jit(solution)/shard_map/ppermute | solution.py:19
  131.9 4.1 %collective-permute-done.21.refs_2_ = f32[32,1024]{1,0:T(8,128)S(1)} collective-permute-done((f32[32,1024]{1,0:T(8,128)S(1)}, f32[32,1024]{1,0:T(8,128)S(1)}, u32[]{:S(2)}, u32[]{:S(2)}) %collective-permute-start.21) | collective-permute-done | bytes 131104 | tf_op jit(solution)/shard_map/ppermute | solution.py:19
  137.2 3.7 %shard_map.70.refs_0_ = f32[128,512]{1,0:T(8,128)} custom-call(f32[32,1024]{1,0:T(8,128)} %fusion.6.refs_0_.refs_1_, f32[32,1024]{1,0:T(8,128)} %copy-done.18, f32[32,1024]{1,0:T(8,128)} %copy-done.17, f32[32,1024]{1,0:T(8,128)} %copy-done.16, f32[4,64,1024]{2,1,0:T(8,128)} %bitcast.63, f32[4,64,1024]{2,1,0:T(8,128)} %collective-permute-done.23.refs_5_), custom_call_target="tpu_custom_call" | custom-call | flops 1000 | bytes 1000 | tf_op jit(solution)/shard_map/pallas_call | solution.py:224
  140.9 1.7 collective-permute-start.26
  142.6 1.8 collective-permute-start.25
  144.6 6.0 %collective-permute-done.26.refs_3_ = f32[128,512]{1,0:T(8,128)S(1)} collective-permute-done((f32[128,512]{1,0:T(8,128)}, f32[128,512]{1,0:T(8,128)S(1)}, u32[]{:S(2)}, u32[]{:S(2)}) %collective-permute-start.26) | collective-permute-done | bytes 262176 | tf_op jit(solution)/shard_map/ppermute | solution.py:19
  151.1 2.2 %collective-permute-done.24.refs_1_ = f32[128,512]{1,0:T(8,128)S(1)} collective-permute-done((f32[128,512]{1,0:T(8,128)}, f32[128,512]{1,0:T(8,128)S(1)}, u32[]{:S(2)}, u32[]{:S(2)}) %collective-permute-start.24) | collective-permute-done | bytes 262176 | tf_op jit(solution)/shard_map/ppermute | solution.py:19
  155.0 3.8 %shard_map.71.z_ref = bf16[1024,1024]{1,0:T(8,128)(2,1)} custom-call(f32[128,512]{1,0:T(8,128)} %shard_map.70.refs_0_, f32[128,512]{1,0:T(8,128)} %copy-done.10, f32[128,512]{1,0:T(8,128)} %copy-done.9, f32[128,512]{1,0:T(8,128)} %copy-done.8, f32[128,512]{1,0:T(8,128)} %copy-done.11, f32[128,512]{1,0:T(8,128)} %collective-permute-done.28.refs_5_, ...), custom_call_target="tpu_custom_call" | custom-call | flops 1000 | bytes 1000 | tf_op jit(solution)/shard_map/pallas_call | solution.py:250
  158.8 9.3 %shard_map.74.slab_ref = f32[512,3072]{1,0:T(8,128)} custom-call(bf16[1024,1024]{1,0:T(8,128)(2,1)} %shard_map.71.z_ref, f32[4,3072,128]{2,1,0:T(8,128)} %bitcast.56), custom_call_target="tpu_custom_call" | custom-call | flops 1000 | bytes 16777216 | tf_op jit(solution)/shard_map/pallas_call | solution.py:266
  168.1 1.6 all-gather.11.cloned.1.call-done
  169.7 10.7 %shard_map.75 = f32[512,3072]{1,0:T(8,128)} custom-call(bf16[1024,1024]{1,0:T(8,128)(2,1)} %shard_map.71.z_ref, f32[4,2304,128]{2,1,0:T(8,128)} %bitcast.58, f32[4,768,128]{2,1,0:T(8,128)} %copy-done.4, f32[512,3072]{1,0:T(8,128)} %shard_map.74.slab_ref), custom_call_target="tpu_custom_call", output_to_operand_aliasing={{}: (3, {})} | custom-call | flops 1000 | bytes 1000 | tf_op jit(solution)/shard_map/pallas_call | solution.py:300
  (145 shorter events, 25.4 us)
Async XLA Ops:
  6.5 3.0 %copy-start = (f32[3072,128]{1,0:T(8,128)S(1)}, f32[3072,128]{1,0:T(8,128)}, u32[]{:S(2)}) copy-start(f32[3072,128]{1,0:T(8,128)} %param.7) | copy-start | bytes 4718596
  6.5 2.3 %copy-start.19 = (s32[4096]{0:T(1024)S(1)}, s32[4096]{0:T(1024)}, u32[]{:S(2)}) copy-start(s32[4096]{0:T(1024)} %param.11) | copy-start | bytes 49156
  6.5 10.3 %copy-start.1 = (f32[3072,128]{1,0:T(8,128)S(1)}, f32[3072,128]{1,0:T(8,128)}, u32[]{:S(2)}) copy-start(f32[3072,128]{1,0:T(8,128)} %own_ref.1) | copy-start | bytes 4718596
  6.5 78.4 %all-gather.7.cloned.1.call-start = ((), (), s32[]{:S(2)}) async-start(), calls=%async_computation | async-start | bytes 7864320 | tf_op jit(solution)/shard_map/all_gather | solution.py:380
  7.3 110.0 %all-gather.9.cloned.1.call-start = ((), (), s32[]{:S(2)}) async-start(), calls=%async_computation.1 | async-start | bytes 1310720 | tf_op jit(solution)/shard_map/all_gather | solution.py:388
  10.9 11.5 %collective-permute-start.3 = (f32[256,128]{1,0:T(8,128)}, f32[256,128]{1,0:T(8,128)}, u32[]{:S(2)}, u32[]{:S(2)}) collective-permute-start(f32[256,128]{1,0:T(8,128)} %gather_fusion), channel_id=1, source_target_pairs={{0,1},{1,16},{16,17},{17,0},{2,3},{3,18},{18,19},{19,2},{4,5},{5,2... | collective-permute-start | bytes 393224 | tf_op jit(solution)/shard_map/ppermute | solution.py:19
  12.9 9.5 %collective-permute-start.2 = (f32[256,128]{1,0:T(8,128)}, f32[256,128]{1,0:T(8,128)}, u32[]{:S(2)}, u32[]{:S(2)}) collective-permute-start(f32[256,128]{1,0:T(8,128)} %gather_fusion), channel_id=1, source_target_pairs={{0,17},{1,0},{16,1},{17,16},{2,19},{3,2},{18,3},{19,18},{4,21},{5,... | collective-permute-start | bytes 393224 | tf_op jit(solution)/shard_map/ppermute | solution.py:19
  15.0 9.4 %collective-permute-start.4 = (f32[256,128]{1,0:T(8,128)}, f32[256,128]{1,0:T(8,128)}, u32[]{:S(2)}, u32[]{:S(2)}) collective-permute-start(f32[256,128]{1,0:T(8,128)} %gather_fusion), channel_id=1, source_target_pairs={{0,16},{1,17},{16,0},{17,1},{2,18},{3,19},{18,2},{19,3},{4,20},{5,... | collective-permute-start | bytes 393224 | tf_op jit(solution)/shard_map/ppermute | solution.py:19
  17.6 13.3 %collective-permute-start = (f32[768,128]{1,0:T(8,128)}, f32[768,128]{1,0:T(8,128)S(1)}, u32[]{:S(2)}, u32[]{:S(2)}) collective-permute-start(f32[768,128]{1,0:T(8,128)} %slice.12), channel_id=1, source_target_pairs={{0,1},{1,0},{2,3},{3,2},{4,5},{5,4},{6,7},{7,6},{8,9},{9,8},{10,11... | collective-permute-start | bytes 1179656 | tf_op jit(solution)/shard_map/ppermute | solution.py:19
  19.8 45.2 %collective-permute-start.1 = (f32[2304,128]{1,0:T(8,128)}, f32[2304,128]{1,0:T(8,128)S(1)}, u32[]{:S(2)}, u32[]{:S(2)}) collective-permute-start(f32[2304,128]{1,0:T(8,128)} %slice.13), channel_id=1, source_target_pairs={{0,1},{1,0},{2,3},{3,2},{4,5},{5,4},{6,7},{7,6},{8,9},{9,8},{10,11... | collective-permute-start | bytes 3538952 | tf_op jit(solution)/shard_map/ppermute | solution.py:19
  34.0 16.6 %collective-permute-start.7 = (f32[2,256,256]{2,1,0:T(8,128)}, f32[2,256,256]{2,1,0:T(8,128)S(1)}, u32[]{:S(2)}, u32[]{:S(2)}) collective-permute-start(f32[2,256,256]{2,1,0:T(8,128)} %get-tuple-element.15), channel_id=1, source_target_pairs={{0,64},{32,96},{64,0},{96,32},{1,65},{33,97},{65,1},{97,33},{2,66}... | collective-permute-start | bytes 1572872 | tf_op jit(solution)/shard_map/ppermute | solution.py:19
  37.1 21.3 %collective-permute-start.6 = (f32[2,256,256]{2,1,0:T(8,128)}, f32[2,256,256]{2,1,0:T(8,128)S(1)}, u32[]{:S(2)}, u32[]{:S(2)}) collective-permute-start(f32[2,256,256]{2,1,0:T(8,128)} %get-tuple-element.15), channel_id=1, source_target_pairs={{0,96},{32,0},{64,32},{96,64},{1,97},{33,1},{65,33},{97,65},{2,98}... | collective-permute-start | bytes 1572872 | tf_op jit(solution)/shard_map/ppermute | solution.py:19
  38.2 20.2 %collective-permute-start.5 = (f32[2,256,256]{2,1,0:T(8,128)}, f32[2,256,256]{2,1,0:T(8,128)S(1)}, u32[]{:S(2)}, u32[]{:S(2)}) collective-permute-start(f32[2,256,256]{2,1,0:T(8,128)} %get-tuple-element.15), channel_id=1, source_target_pairs={{0,32},{32,64},{64,96},{96,0},{1,33},{33,65},{65,97},{97,1},{2,34}... | collective-permute-start | bytes 1572872 | tf_op jit(solution)/shard_map/ppermute | solution.py:19
  65.0 2.2 %copy-start.22 = (f32[1152,128]{1,0:T(8,128)S(1)}, f32[1152,128]{1,0:T(8,128)}, u32[]{:S(2)}) copy-start(f32[1152,128]{1,0:T(8,128)} %get-tuple-element.16) | copy-start | bytes 1769476
  67.0 1.6 collective-permute-start.8
  67.2 15.8 %collective-permute-start.12 = (f32[1152,128]{1,0:T(8,128)S(1)}, f32[1152,128]{1,0:T(8,128)S(1)}, u32[]{:S(2)}, u32[]{:S(2)}) collective-permute-start(f32[1152,128]{1,0:T(8,128)S(1)} %copy-done.22), channel_id=1, source_target_pairs={{0,1},{1,0},{2,3},{3,2},{4,5},{5,4},{6,7},{7,6},{8,9},{9,8},{10,11... | collective-permute-start | bytes 1769480 | tf_op jit(solution)/shard_map/ppermute | solution.py:19
  69.7 12.0 %collective-permute-start.11 = (f32[64,256]{1,0:T(8,128)S(1)}, f32[64,256]{1,0:T(8,128)S(1)}, u32[]{:S(2)}, u32[]{:S(2)}) collective-permute-start(f32[64,256]{1,0:T(8,128)S(1)} %get-tuple-element.34), channel_id=1, source_target_pairs={{0,4},{2,6},{4,0},{6,2},{1,5},{3,7},{5,1},{7,3},{8,12},{10,14},{12... | collective-permute-start | bytes 196616 | tf_op jit(solution)/shard_map/ppermute | solution.py:19
  72.9 8.8 %collective-permute-start.10 = (f32[64,256]{1,0:T(8,128)S(1)}, f32[64,256]{1,0:T(8,128)S(1)}, u32[]{:S(2)}, u32[]{:S(2)}) collective-permute-start(f32[64,256]{1,0:T(8,128)S(1)} %get-tuple-element.35), channel_id=1, source_target_pairs={{0,6},{2,0},{4,2},{6,4},{1,7},{3,1},{5,3},{7,5},{8,14},{10,8},{12,... | collective-permute-start | bytes 196616 | tf_op jit(solution)/shard_map/ppermute | solution.py:19
  74.0 7.7 %collective-permute-start.9 = (f32[64,256]{1,0:T(8,128)S(1)}, f32[64,256]{1,0:T(8,128)S(1)}, u32[]{:S(2)}, u32[]{:S(2)}) collective-permute-start(f32[64,256]{1,0:T(8,128)S(1)} %get-tuple-element.36), channel_id=1, source_target_pairs={{0,2},{2,4},{4,6},{6,0},{1,3},{3,5},{5,7},{7,1},{8,10},{10,12},{12... | collective-permute-start | bytes 196616 | tf_op jit(solution)/shard_map/ppermute | solution.py:19
  83.9 85.8 %all-gather.11.cloned.1.call-start = ((), (), s32[]{:S(2)}) async-start(), calls=%async_computation.2 | async-start | bytes 5898240 | tf_op jit(solution)/shard_map/all_gather | solution.py:393
  84.2 14.4 %collective-permute-start.31 = (f32[1152,128]{1,0:T(8,128)S(1)}, f32[1152,128]{1,0:T(8,128)S(1)}, u32[]{:S(2)}, u32[]{:S(2)}) collective-permute-start(f32[1152,128]{1,0:T(8,128)S(1)} %copy-done.21), channel_id=1, source_target_pairs={{0,1},{1,0},{2,3},{3,2},{4,5},{5,4},{6,7},{7,6},{8,9},{9,8},{10,11... | collective-permute-start | bytes 1769480 | tf_op jit(solution)/shard_map/ppermute | solution.py:19
  92.3 10.3 %copy-start.20 = (f32[1024]{0:T(1024)S(1)}, f32[1024]{0:T(1024)}, u32[]{:S(2)}) copy-start(f32[1024]{0:T(1024)} %param.9) | copy-start | bytes 12292
  92.3 1.7 collective-permute-start.13
  96.5 6.4 %copy-start.25 = (f32[32,512]{1,0:T(8,128)S(1)}, f32[32,512]{1,0:T(8,128)}, u32[]{:S(2)}) copy-start(f32[32,512]{1,0:T(8,128)} %get-tuple-element.20) | copy-start | bytes 196612
  96.5 7.9 %copy-start.24 = (f32[32,512]{1,0:T(8,128)S(1)}, f32[32,512]{1,0:T(8,128)}, u32[]{:S(2)}) copy-start(f32[32,512]{1,0:T(8,128)} %get-tuple-element.21) | copy-start | bytes 196612
  96.5 9.7 %copy-start.23 = (f32[32,512]{1,0:T(8,128)S(1)}, f32[32,512]{1,0:T(8,128)}, u32[]{:S(2)}) copy-start(f32[32,512]{1,0:T(8,128)} %get-tuple-element.22) | copy-start | bytes 196612
  96.5 15.5 %copy-start.14 = (f32[32,512]{1,0:T(8,128)S(1)}, f32[32,512]{1,0:T(8,128)}, u32[]{:S(2)}) copy-start(f32[32,512]{1,0:T(8,128)} %get-tuple-element.19.refs_0_) | copy-start | bytes 196612
  102.9 6.8 %collective-permute-start.14 = (f32[32,512]{1,0:T(8,128)S(1)}, f32[32,512]{1,0:T(8,128)S(1)}, u32[]{:S(2)}, u32[]{:S(2)}) collective-permute-start(f32[32,512]{1,0:T(8,128)S(1)} %copy-done.25), channel_id=1, source_target_pairs={{0,32},{32,64},{64,96},{96,0},{1,33},{33,65},{65,97},{97,1},{2,34}... | collective-permute-start | bytes 196616 | tf_op jit(solution)/shard_map/ppermute | solution.py:19
  104.4 5.3 %collective-permute-start.15 = (f32[32,512]{1,0:T(8,128)S(1)}, f32[32,512]{1,0:T(8,128)S(1)}, u32[]{:S(2)}, u32[]{:S(2)}) collective-permute-start(f32[32,512]{1,0:T(8,128)S(1)} %copy-done.24), channel_id=1, source_target_pairs={{0,96},{32,0},{64,32},{96,64},{1,97},{33,1},{65,33},{97,65},{2,98}... | collective-permute-start | bytes 196616 | tf_op jit(solution)/shard_map/ppermute | solution.py:19
  106.2 5.8 %collective-permute-start.16 = (f32[32,512]{1,0:T(8,128)S(1)}, f32[32,512]{1,0:T(8,128)S(1)}, u32[]{:S(2)}, u32[]{:S(2)}) collective-permute-start(f32[32,512]{1,0:T(8,128)S(1)} %copy-done.23), channel_id=1, source_target_pairs={{0,64},{32,96},{64,0},{96,32},{1,65},{33,97},{65,1},{97,33},{2,66}... | collective-permute-start | bytes 196616 | tf_op jit(solution)/shard_map/ppermute | solution.py:19
  112.0 8.4 %collective-permute-start.19 = (f32[32,512]{1,0:T(8,128)S(1)}, f32[32,512]{1,0:T(8,128)S(1)}, u32[]{:S(2)}, u32[]{:S(2)}) collective-permute-start(f32[32,512]{1,0:T(8,128)S(1)} %add_add_fusion), channel_id=1, source_target_pairs={{0,17},{1,0},{16,1},{17,16},{2,19},{3,2},{18,3},{19,18},{4,21},{5,... | collective-permute-start | bytes 196616 | tf_op jit(solution)/shard_map/ppermute | solution.py:19
  114.5 6.2 %collective-permute-start.18 = (f32[32,512]{1,0:T(8,128)S(1)}, f32[32,512]{1,0:T(8,128)S(1)}, u32[]{:S(2)}, u32[]{:S(2)}) collective-permute-start(f32[32,512]{1,0:T(8,128)S(1)} %add_add_fusion), channel_id=1, source_target_pairs={{0,1},{1,16},{16,17},{17,0},{2,3},{3,18},{18,19},{19,2},{4,5},{5,2... | collective-permute-start | bytes 196616 | tf_op jit(solution)/shard_map/ppermute | solution.py:19
  114.5 5.9 %collective-permute-start.17 = (f32[32,512]{1,0:T(8,128)S(1)}, f32[32,512]{1,0:T(8,128)S(1)}, u32[]{:S(2)}, u32[]{:S(2)}) collective-permute-start(f32[32,512]{1,0:T(8,128)S(1)} %add_add_fusion), channel_id=1, source_target_pairs={{0,16},{1,17},{16,0},{17,1},{2,18},{3,19},{18,2},{19,3},{4,20},{5,... | collective-permute-start | bytes 196616 | tf_op jit(solution)/shard_map/ppermute | solution.py:19
  117.3 10.3 %collective-permute-start.23 = (f32[4,64,1024]{2,1,0:T(8,128)}, f32[4,64,1024]{2,1,0:T(8,128)}, u32[]{:S(2)}, u32[]{:S(2)}) collective-permute-start(f32[4,64,1024]{2,1,0:T(8,128)} %bitcast.62), channel_id=1, source_target_pairs={{0,8},{8,0},{1,9},{9,1},{2,10},{10,2},{3,11},{11,3},{4,12},{12,4},... | collective-permute-start | bytes 3145736 | tf_op jit(solution)/shard_map/ppermute | solution.py:19
  121.4 46.6 %collective-permute-start.32 = (f32[4,768,128]{2,1,0:T(8,128)}, f32[4,768,128]{2,1,0:T(8,128)S(1)}, u32[]{:S(2)}, u32[]{:S(2)}) collective-permute-start(f32[4,768,128]{2,1,0:T(8,128)} %shard_map.73), channel_id=1, source_target_pairs={{0,1},{1,0},{2,3},{3,2},{4,5},{5,4},{6,7},{7,6},{8,9},{9,8},{10,11... | collective-permute-start | bytes 4718600 | tf_op jit(solution)/shard_map/ppermute | solution.py:19
  122.4 9.5 %collective-permute-start.22 = (f32[32,1024]{1,0:T(8,128)S(1)}, f32[32,1024]{1,0:T(8,128)S(1)}, u32[]{:S(2)}, u32[]{:S(2)}) collective-permute-start(f32[32,1024]{1,0:T(8,128)S(1)} %copy-done.6), channel_id=1, source_target_pairs={{0,4},{2,6},{4,0},{6,2},{1,5},{3,7},{5,1},{7,3},{8,12},{10,14},{12... | collective-permute-start | bytes 393224 | tf_op jit(solution)/shard_map/ppermute | solution.py:19
  125.5 10.4 %collective-permute-start.21 = (f32[32,1024]{1,0:T(8,128)S(1)}, f32[32,1024]{1,0:T(8,128)S(1)}, u32[]{:S(2)}, u32[]{:S(2)}) collective-permute-start(f32[32,1024]{1,0:T(8,128)S(1)} %copy-done.6), channel_id=1, source_target_pairs={{0,6},{2,0},{4,2},{6,4},{1,7},{3,1},{5,3},{7,5},{8,14},{10,8},{12,... | collective-permute-start | bytes 393224 | tf_op jit(solution)/shard_map/ppermute | solution.py:19
  126.6 9.5 %collective-permute-start.20 = (f32[32,1024]{1,0:T(8,128)S(1)}, f32[32,1024]{1,0:T(8,128)S(1)}, u32[]{:S(2)}, u32[]{:S(2)}) collective-permute-start(f32[32,1024]{1,0:T(8,128)S(1)} %copy-done.6), channel_id=1, source_target_pairs={{0,2},{2,4},{4,6},{6,0},{1,3},{3,5},{5,7},{7,1},{8,10},{10,12},{12... | collective-permute-start | bytes 393224 | tf_op jit(solution)/shard_map/ppermute | solution.py:19
  131.9 4.2 %copy-start.16 = (f32[32,1024]{1,0:T(8,128)}, f32[32,1024]{1,0:T(8,128)S(1)}, u32[]{:S(2)}) copy-start(f32[32,1024]{1,0:T(8,128)S(1)} %collective-permute-done.22.refs_3_) | copy-start | bytes 393220
  140.9 9.7 %collective-permute-start.26 = (f32[128,512]{1,0:T(8,128)}, f32[128,512]{1,0:T(8,128)S(1)}, u32[]{:S(2)}, u32[]{:S(2)}) collective-permute-start(f32[128,512]{1,0:T(8,128)} %shard_map.70.refs_0_), channel_id=1, source_target_pairs={{0,64},{32,96},{64,0},{96,32},{1,65},{33,97},{65,1},{97,33},{2,66}... | collective-permute-start | bytes 786440 | tf_op jit(solution)/shard_map/ppermute | solution.py:19
  142.6 8.4 %collective-permute-start.25 = (f32[128,512]{1,0:T(8,128)}, f32[128,512]{1,0:T(8,128)S(1)}, u32[]{:S(2)}, u32[]{:S(2)}) collective-permute-start(f32[128,512]{1,0:T(8,128)} %shard_map.70.refs_0_), channel_id=1, source_target_pairs={{0,96},{32,0},{64,32},{96,64},{1,97},{33,1},{65,33},{97,65},{2,98}... | collective-permute-start | bytes 786440 | tf_op jit(solution)/shard_map/ppermute | solution.py:19
  144.3 8.9 %collective-permute-start.24 = (f32[128,512]{1,0:T(8,128)}, f32[128,512]{1,0:T(8,128)S(1)}, u32[]{:S(2)}, u32[]{:S(2)}) collective-permute-start(f32[128,512]{1,0:T(8,128)} %shard_map.70.refs_0_), channel_id=1, source_target_pairs={{0,32},{32,64},{64,96},{96,0},{1,33},{33,65},{65,97},{97,1},{2,34}... | collective-permute-start | bytes 786440 | tf_op jit(solution)/shard_map/ppermute | solution.py:19
  144.6 8.7 %collective-permute-start.27 = (f32[128,512]{1,0:T(8,128)}, f32[128,512]{1,0:T(8,128)S(1)}, u32[]{:S(2)}, u32[]{:S(2)}) collective-permute-start(f32[128,512]{1,0:T(8,128)} %shard_map.70.refs_0_), channel_id=1, source_target_pairs={{0,8},{8,0},{1,9},{9,1},{2,10},{10,2},{3,11},{11,3},{4,12},{12,4},... | collective-permute-start | bytes 786440 | tf_op jit(solution)/shard_map/ppermute | solution.py:19
  150.6 4.4 %copy-start.8 = (f32[128,512]{1,0:T(8,128)}, f32[128,512]{1,0:T(8,128)S(1)}, u32[]{:S(2)}) copy-start(f32[128,512]{1,0:T(8,128)S(1)} %collective-permute-done.26.refs_3_) | copy-start | bytes 786436
  150.6 2.7 %collective-permute-start.30 = (f32[128,512]{1,0:T(8,128)S(1)}, f32[128,512]{1,0:T(8,128)S(1)}, u32[]{:S(2)}, u32[]{:S(2)}) collective-permute-start(f32[128,512]{1,0:T(8,128)S(1)} %collective-permute-done.26.refs_3_), channel_id=1, source_target_pairs={{0,8},{8,0},{1,9},{9,1},{2,10},{10,2},{3,11},{11,3},{4,12},{12,4},... | collective-permute-start | bytes 786440 | tf_op jit(solution)/shard_map/ppermute | solution.py:19
  150.9 4.0 %copy-start.9 = (f32[128,512]{1,0:T(8,128)}, f32[128,512]{1,0:T(8,128)S(1)}, u32[]{:S(2)}) copy-start(f32[128,512]{1,0:T(8,128)S(1)} %collective-permute-done.25.refs_2_) | copy-start | bytes 786436
  150.9 2.4 %collective-permute-start.29 = (f32[128,512]{1,0:T(8,128)S(1)}, f32[128,512]{1,0:T(8,128)S(1)}, u32[]{:S(2)}, u32[]{:S(2)}) collective-permute-start(f32[128,512]{1,0:T(8,128)S(1)} %collective-permute-done.25.refs_2_), channel_id=1, source_target_pairs={{0,8},{8,0},{1,9},{9,1},{2,10},{10,2},{3,11},{11,3},{4,12},{12,4},... | collective-permute-start | bytes 786440 | tf_op jit(solution)/shard_map/ppermute | solution.py:19
  153.3 1.7 collective-permute-start.28
  (14 other events, 13.2 us)
Sparse Core Ops, SparseCore 0:
  9.0 70.1 all-gather.6
  84.0 26.2 all-gather.8
  111.9 57.6 all-gather.10

commit v5 on v4

--- a/solution.py
+++ b/solution.py
@@ -11,7 +11,7 @@
 SIZES = {"x": 4, "zh": 2, "c": 2, "y": 4, "zl": 2, ("zh", "zl"): 4}
 regular = 0.01
 TILE = 384
-VMEM = 60 * 1024 * 1024
+VMEM = 36 * 1024 * 1024
 
 
 def shifted(array, axis, step):

time: 189 us -> 188 us (level)
  Pallas kernels: 48 us -> 31.1 us
  local copies, waits for them, and re-layouts: 18.7 us -> 34.9 us
    unnamed x53 -> x43, local copies, waits for them, and re-layouts: 7.67 us -> 18 us
    all_gather x1, waiting for transfers between devices: 1.61 us -> 5.06 us  [local(): lax.all_gather(joined(other_first, other_second, (to_self,)), 'y')]
    pallas_call x1, Pallas kernels: 7.36 us -> 4 us  [gram_shares(): pl.pallas_call(body, grid=(steps,), in_specs=[pl.BlockSpec((512, step_row...]
    pallas_call x1, Pallas kernels: 3.83 us -> 0.89 us  [z_ready(): pl.pallas_call(body, out_shape=jax.ShapeDtypeStruct((2 * height, depth),...]
    ppermute x33, waiting for transfers between devices: 53.3 us -> 50.7 us  [shifted(): return lax.ppermute(array, axis, [(i, (i + step) % n) for i in range(n)])]
    pallas_call x1, Pallas kernels: 2.38 us -> 0.11 us  [with_pieces(): pl.pallas_call(body, grid=(2,), in_specs=[pl.BlockSpec((rows, 128), lambd...]
  transfers between devices with their start and end apart: 36 -> 36, of which waited for: 18 -> 19; matrix products, arithmetic and copies ran while one was open for 12% -> 15% of each run, Pallas kernels for 20% -> 12%
where the time goes in v5:
time: 188 us; the launch traced here: 186 us
  waiting for transfers between devices  56.5 us (30%)
  starting transfers between devices  39.3 us (21%)
  local copies, waits for them, and re-layouts  34.9 us (19%)
  Pallas kernels  31.1 us (17%)
  between operations  13.6 us (7%)
  other arithmetic  9.73 us (5%)
    ppermute x33, waiting for transfers between devices, shifted(): return lax.ppermute(array, axis, [(i, (i + step) % n) for i in range(n)])  50.7 us
    ppermute x33, starting transfers between devices, shifted(): return lax.ppermute(array, axis, [(i, (i + step) % n) for i in range(n)])  39.2 us
    unnamed x43, local copies, waits for them, and re-layouts  18 us
    pallas_call x1, Pallas kernels, slab_other(): pl.pallas_call(body, grid=(total // WIDE,), in_specs=[pl.BlockSpec((2 * h...  9.18 us
    pallas_call x1, Pallas kernels, slab_own(): pl.pallas_call(body, grid=(total // WIDE,), in_specs=[pl.BlockSpec((2 * h...  7.4 us
    all_gather x1, waiting for transfers between devices, local(): lax.all_gather(joined(other_first, other_second, (to_self,)), 'y')  5.06 us
    pallas_call x1, Pallas kernels, cot_ready(): pl.pallas_call(body, grid=(rows // STEP,), in_specs=[pl.BlockSpec((STEP,...  4.98 us
    pallas_call x1, Pallas kernels, gram_shares(): pl.pallas_call(body, grid=(steps,), in_specs=[pl.BlockSpec((512, step_row...  4 us
  transfers between devices with their start and end apart: 36, of which 19 were waited for; matrix products, arithmetic and copies ran while one was open for 15% of the time, Pallas kernels for 12%

profile of v5, /device:TPU:0, one launch (start us, length us, event | category | flops | bytes accessed | tf_op | source)
XLA Modules:
  0.0 185.6 jit_solution(5404204833444532665)
XLA Ops:
  9.4 1.3 gather_fusion
  10.7 2.0 %collective-permute-start.3 = (f32[256,128]{1,0:T(8,128)}, f32[256,128]{1,0:T(8,128)}, u32[]{:S(2)}, u32[]{:S(2)}) collective-permute-start(f32[256,128]{1,0:T(8,128)} %gather_fusion), channel_id=1, source_target_pairs={{0,1},{1,16},{16,17},{17,0},{2,3},{3,18},{18,19},{19,2},{4,5},{5,2... | collective-permute-start | bytes 393224 | tf_op jit(solution)/shard_map/ppermute | solution.py:19
  12.7 2.1 %collective-permute-start.2 = (f32[256,128]{1,0:T(8,128)}, f32[256,128]{1,0:T(8,128)}, u32[]{:S(2)}, u32[]{:S(2)}) collective-permute-start(f32[256,128]{1,0:T(8,128)} %gather_fusion), channel_id=1, source_target_pairs={{0,17},{1,0},{16,1},{17,16},{2,19},{3,2},{18,3},{19,18},{4,21},{5,... | collective-permute-start | bytes 393224 | tf_op jit(solution)/shard_map/ppermute | solution.py:19
  14.8 1.9 %collective-permute-start.4 = (f32[256,128]{1,0:T(8,128)}, f32[256,128]{1,0:T(8,128)}, u32[]{:S(2)}, u32[]{:S(2)}) collective-permute-start(f32[256,128]{1,0:T(8,128)} %gather_fusion), channel_id=1, source_target_pairs={{0,16},{1,17},{16,0},{17,1},{2,18},{3,19},{18,2},{19,3},{4,20},{5,... | collective-permute-start | bytes 393224 | tf_op jit(solution)/shard_map/ppermute | solution.py:19
  16.7 1.8 slice.12
  19.5 2.6 %slice.13 = f32[2304,128]{1,0:T(8,128)} slice(f32[3072,128]{1,0:T(8,128)} %own_ref.1), slice={[768:3072], [0:128]} | slice | bytes 2359296 | tf_op jit(solution)/shard_map/slice | solution.py:382
  24.2 1.4 fusion.65
  29.4 1.4 collective-permute-done.first_ref.refs_0_
  30.9 3.1 %collective-permute-start.7 = (f32[2,256,256]{2,1,0:T(8,128)S(1)}, f32[2,256,256]{2,1,0:T(8,128)S(1)}, u32[]{:S(2)}, u32[]{:S(2)}) collective-permute-start(f32[2,256,256]{2,1,0:T(8,128)S(1)} %get-tuple-element.15), channel_id=1, source_target_pairs={{0,64},{32,96},{64,0},{96,32},{1,65},{33,97},{65,1},{97,33},{2,66}... | collective-permute-start | bytes 1572872 | tf_op jit(solution)/shard_map/ppermute | solution.py:19
  36.1 11.3 %collective-permute-done.7 = f32[2,256,256]{2,1,0:T(8,128)S(1)} collective-permute-done((f32[2,256,256]{2,1,0:T(8,128)S(1)}, f32[2,256,256]{2,1,0:T(8,128)S(1)}, u32[]{:S(2)}, u32[]{:S(2)}) %collective-permute-start.7) | collective-permute-done | bytes 524320 | tf_op jit(solution)/shard_map/ppermute | solution.py:19
  47.4 7.8 %collective-permute-done.6 = f32[2,256,256]{2,1,0:T(8,128)S(1)} collective-permute-done((f32[2,256,256]{2,1,0:T(8,128)S(1)}, f32[2,256,256]{2,1,0:T(8,128)S(1)}, u32[]{:S(2)}, u32[]{:S(2)}) %collective-permute-start.6) | collective-permute-done | bytes 524320 | tf_op jit(solution)/shard_map/ppermute | solution.py:19
  55.2 1.5 pad_maximum_fusion
  56.6 3.2 %gather_fusion.1 = f32[512,256]{1,0:T(8,128)S(1)} fusion(f32[2048,256]{1,0:T(8,128)} %bitcast.61, s32[1024]{0:T(1024)S(1)} %pad_clamp_fusion), kind=kCustom, calls=%fused_computation.1 | custom fusion | bytes 1050624 | tf_op jit(solution)/shard_map/jit(_take)/gather | solution.py:356
  60.8 1.8 slice_bitcast_fusion
  66.3 3.2 %collective-permute-start.11 = (f32[64,256]{1,0:T(8,128)}, f32[64,256]{1,0:T(8,128)}, u32[]{:S(2)}, u32[]{:S(2)}) collective-permute-start(f32[64,256]{1,0:T(8,128)} %get-tuple-element.34), channel_id=1, source_target_pairs={{0,4},{2,6},{4,0},{6,2},{1,5},{3,7},{5,1},{7,3},{8,12},{10,14},{12... | collective-permute-start | bytes 196616 | tf_op jit(solution)/shard_map/ppermute | solution.py:19
  71.5 5.0 %shard_map.64.refs_2_.cot_ref = bf16[512,3072]{1,0:T(8,128)(2,1)S(1)} custom-call(f32[3072,128]{1,0:T(8,128)S(1)} %copy-done.8, f32[768,128]{1,0:T(8,128)S(1)} %collective-permute-done.first_ref.refs_0_, f32[2304,128]{1,0:T(8,128)} %collective-permute-done.1.second_ref.refs_1_), custom_call_target="tpu_custom_call" | custom-call | flops 1000 | bytes 12582912 | tf_op jit(solution)/shard_map/pallas_call | solution.py:148
  76.5 1.7 copy-done.1
  82.2 1.9 %copy-done.2 = bf16[512,3072]{1,0:T(8,128)(2,1)S(1)} copy-done((bf16[512,3072]{1,0:T(8,128)(2,1)S(1)}, bf16[512,3072]{1,0:T(8,128)(2,1)}, u32[]{:S(2)}) %copy-start.2) | copy-done | bytes 3145752
  84.1 2.8 %copy-done.3 = f32[12288,128]{1,0:T(8,128)S(1)} copy-done((f32[12288,128]{1,0:T(8,128)S(1)}, f32[12288,128]{1,0:T(8,128)}, u32[]{:S(2)}) %copy-start.3) | copy-done | bytes 6291480
  87.8 4.0 %shard_map.68 = (f32[4,32,512]{2,1,0:T(8,128)S(1)}, f32[4,32,512]{2,1,0:T(8,128)S(1)}, f32[4,768,128]{2,1,0:T(8,128)S(1)}) custom-call(bf16[512,3072]{1,0:T(8,128)(2,1)S(1)} %copy-done.2, f32[4,3072,128]{2,1,0:T(8,128)S(1)} %bitcast.55, f32[64,1024]{1,0:T(8,128)S(1)} %copy-done.10), custom_call_target="tpu_custom_call" | custom-call | flops 1000 | bytes 1000 | tf_op jit(solution)/shard_map/pallas_call | solution.py:196
  93.1 1.5 collective-permute-done.13.came_ref
  94.6 1.2 collective-permute-done.31.second_ref
  95.9 2.1 %shard_map.72 = f32[2304,128]{1,0:T(8,128)} custom-call(f32[1152,128]{1,0:T(8,128)} %collective-permute-done.12.refs_1_.first_ref, f32[1152,128]{1,0:T(8,128)S(1)} %collective-permute-done.31.second_ref, f32[32,512]{1,0:T(8,128)S(1)} %get-tuple-element.19.refs_0_), custom_call_target="tpu_custom_call" | custom-call | flops 1000 | bytes 1000 | tf_op jit(solution)/shard_map/pallas_call | solution.py:128
  99.1 1.5 collective-permute-start.14
  100.6 1.8 collective-permute-start.15
  102.4 1.7 collective-permute-start.16
  104.1 1.8 collective-permute-done.14
  106.1 2.1 %collective-permute-done.16 = f32[32,512]{1,0:T(8,128)S(1)} collective-permute-done((f32[32,512]{1,0:T(8,128)S(1)}, f32[32,512]{1,0:T(8,128)S(1)}, u32[]{:S(2)}, u32[]{:S(2)}) %collective-permute-start.16) | collective-permute-done | bytes 65568 | tf_op jit(solution)/shard_map/ppermute | solution.py:19
  108.2 2.5 %collective-permute-start.19 = (f32[32,512]{1,0:T(8,128)S(1)}, f32[32,512]{1,0:T(8,128)S(1)}, u32[]{:S(2)}, u32[]{:S(2)}) collective-permute-start(f32[32,512]{1,0:T(8,128)S(1)} %add_add_fusion), channel_id=1, source_target_pairs={{0,17},{1,0},{16,1},{17,16},{2,19},{3,2},{18,3},{19,18},{4,21},{5,... | collective-permute-start | bytes 196616 | tf_op jit(solution)/shard_map/ppermute | solution.py:19
  110.7 2.8 %collective-permute-start.17 = (f32[32,512]{1,0:T(8,128)S(1)}, f32[32,512]{1,0:T(8,128)S(1)}, u32[]{:S(2)}, u32[]{:S(2)}) collective-permute-start(f32[32,512]{1,0:T(8,128)S(1)} %add_add_fusion), channel_id=1, source_target_pairs={{0,16},{1,17},{16,0},{17,1},{2,18},{3,19},{18,2},{19,3},{4,20},{5,... | collective-permute-start | bytes 196616 | tf_op jit(solution)/shard_map/ppermute | solution.py:19
  113.5 3.1 %collective-permute-done.17 = f32[32,512]{1,0:T(8,128)S(1)} collective-permute-done((f32[32,512]{1,0:T(8,128)S(1)}, f32[32,512]{1,0:T(8,128)S(1)}, u32[]{:S(2)}, u32[]{:S(2)}) %collective-permute-start.17) | collective-permute-done | bytes 65568 | tf_op jit(solution)/shard_map/ppermute | solution.py:19
  118.6 2.3 %collective-permute-start.22 = (f32[32,1024]{1,0:T(8,128)S(1)}, f32[32,1024]{1,0:T(8,128)S(1)}, u32[]{:S(2)}, u32[]{:S(2)}) collective-permute-start(f32[32,1024]{1,0:T(8,128)S(1)} %copy-done.12), channel_id=1, source_target_pairs={{0,4},{2,6},{4,0},{6,2},{1,5},{3,7},{5,1},{7,3},{8,12},{10,14},{12... | collective-permute-start | bytes 393224 | tf_op jit(solution)/shard_map/ppermute | solution.py:19
  120.9 1.4 collective-permute-start.21
  122.9 3.2 %collective-permute-done.22.refs_3_ = f32[32,1024]{1,0:T(8,128)S(1)} collective-permute-done((f32[32,1024]{1,0:T(8,128)S(1)}, f32[32,1024]{1,0:T(8,128)S(1)}, u32[]{:S(2)}, u32[]{:S(2)}) %collective-permute-start.22) | collective-permute-done | bytes 131104 | tf_op jit(solution)/shard_map/ppermute | solution.py:19
  126.1 5.0 %collective-permute-done.21.refs_2_ = f32[32,1024]{1,0:T(8,128)S(1)} collective-permute-done((f32[32,1024]{1,0:T(8,128)S(1)}, f32[32,1024]{1,0:T(8,128)S(1)}, u32[]{:S(2)}, u32[]{:S(2)}) %collective-permute-start.21) | collective-permute-done | bytes 131104 | tf_op jit(solution)/shard_map/ppermute | solution.py:19
  131.7 1.2 copy-done.13
  133.0 2.4 %shard_map.70.refs_0_ = f32[128,512]{1,0:T(8,128)S(1)} custom-call(f32[32,1024]{1,0:T(8,128)S(1)} %copy-done.12, f32[32,1024]{1,0:T(8,128)S(1)} %collective-permute-done.20.refs_1_, f32[32,1024]{1,0:T(8,128)S(1)} %collective-permute-done.21.refs_2_, f32[32,1024]{1,0:T(8,128)S(1)} %collective-permute-done.22.refs_3_, f32[4,64,1024]{2,1,0:T(8,128)S(1)} %bitcast.60, ...), custom_call_target="tpu_custom_call" | custom-call | flops 1000 | bytes 1000 | tf_op jit(solution)/shard_map/pallas_call | solution.py:224
  135.4 2.0 %collective-permute-start.26 = (f32[128,512]{1,0:T(8,128)S(1)}, f32[128,512]{1,0:T(8,128)S(1)}, u32[]{:S(2)}, u32[]{:S(2)}) collective-permute-start(f32[128,512]{1,0:T(8,128)S(1)} %shard_map.70.refs_0_), channel_id=1, source_target_pairs={{0,64},{32,96},{64,0},{96,32},{1,65},{33,97},{65,1},{97,33},{2,66}... | collective-permute-start | bytes 786440 | tf_op jit(solution)/shard_map/ppermute | solution.py:19
  137.4 1.9 %collective-permute-start.25 = (f32[128,512]{1,0:T(8,128)S(1)}, f32[128,512]{1,0:T(8,128)S(1)}, u32[]{:S(2)}, u32[]{:S(2)}) collective-permute-start(f32[128,512]{1,0:T(8,128)S(1)} %shard_map.70.refs_0_), channel_id=1, source_target_pairs={{0,96},{32,0},{64,32},{96,64},{1,97},{33,1},{65,33},{97,65},{2,98}... | collective-permute-start | bytes 786440 | tf_op jit(solution)/shard_map/ppermute | solution.py:19
  139.4 6.1 %collective-permute-done.26.refs_3_ = f32[128,512]{1,0:T(8,128)S(1)} collective-permute-done((f32[128,512]{1,0:T(8,128)S(1)}, f32[128,512]{1,0:T(8,128)S(1)}, u32[]{:S(2)}, u32[]{:S(2)}) %collective-permute-start.26) | collective-permute-done | bytes 262176 | tf_op jit(solution)/shard_map/ppermute | solution.py:19
  146.0 2.2 %collective-permute-done.24.refs_1_ = f32[128,512]{1,0:T(8,128)S(1)} collective-permute-done((f32[128,512]{1,0:T(8,128)S(1)}, f32[128,512]{1,0:T(8,128)S(1)}, u32[]{:S(2)}, u32[]{:S(2)}) %collective-permute-start.24) | collective-permute-done | bytes 262176 | tf_op jit(solution)/shard_map/ppermute | solution.py:19
  148.3 1.5 collective-permute-done.28.refs_5_
  150.7 2.8 %copy-done.4 = f32[12288,128]{1,0:T(8,128)S(1)} copy-done((f32[12288,128]{1,0:T(8,128)S(1)}, f32[12288,128]{1,0:T(8,128)}, u32[]{:S(2)}) %copy-start.4) | copy-done | bytes 6291480
  153.5 7.4 %shard_map.74.slab_ref = f32[512,3072]{1,0:T(8,128)} custom-call(bf16[1024,1024]{1,0:T(8,128)(2,1)S(1)} %shard_map.71.z_ref, f32[4,3072,128]{2,1,0:T(8,128)S(1)} %bitcast.56), custom_call_target="tpu_custom_call" | custom-call | flops 1000 | bytes 16777216 | tf_op jit(solution)/shard_map/pallas_call | solution.py:266
  160.9 5.1 %all-gather.11.cloned.1.call-done = f32[9216,128]{1,0:T(8,128)} async-done(((f32[2304,128]{1,0:T(8,128)}), f32[9216,128]{1,0:T(8,128)}) %all-gather.11.cloned.1.call-update) | async-done | bytes 4718608 | tf_op jit(solution)/shard_map/all_gather | solution.py:393
  166.0 1.6 copy-done.6
  167.6 2.3 %copy-done.9 = f32[9216,128]{1,0:T(8,128)S(1)} copy-done((f32[9216,128]{1,0:T(8,128)S(1)}, f32[9216,128]{1,0:T(8,128)}, u32[]{:S(2)}) %copy-start.9) | copy-done | bytes 4718616
  169.9 9.2 %shard_map.75 = f32[512,3072]{1,0:T(8,128)} custom-call(bf16[1024,1024]{1,0:T(8,128)(2,1)S(1)} %copy-done.6, f32[4,2304,128]{2,1,0:T(8,128)S(1)} %bitcast.57, f32[4,768,128]{2,1,0:T(8,128)S(1)} %collective-permute-done.32.high_ref, f32[512,3072]{1,0:T(8,128)} %shard_map.74.slab_ref), custom_call_target="tpu_custom_call", output_to_operand_aliasing={{}: (3, {})} | custom-call | flops 1000 | bytes 1000 | tf_op jit(solution)/shard_map/pallas_call | solution.py:300
  (135 shorter events, 30.7 us)
Async XLA Ops:
  6.5 2.8 %copy-start = (f32[3072,128]{1,0:T(8,128)S(1)}, f32[3072,128]{1,0:T(8,128)}, u32[]{:S(2)}) copy-start(f32[3072,128]{1,0:T(8,128)} %param.7) | copy-start | bytes 4718596
  6.5 75.7 %all-gather.7.cloned.1.call-start = ((), (), s32[]{:S(2)}) async-start(), calls=%async_computation | async-start | bytes 7864320 | tf_op jit(solution)/shard_map/all_gather | solution.py:380
  7.3 106.2 %all-gather.9.cloned.1.call-start = ((), (), s32[]{:S(2)}) async-start(), calls=%async_computation.1 | async-start | bytes 1310720 | tf_op jit(solution)/shard_map/all_gather | solution.py:388
  10.7 15.7 %collective-permute-start.3 = (f32[256,128]{1,0:T(8,128)}, f32[256,128]{1,0:T(8,128)}, u32[]{:S(2)}, u32[]{:S(2)}) collective-permute-start(f32[256,128]{1,0:T(8,128)} %gather_fusion), channel_id=1, source_target_pairs={{0,1},{1,16},{16,17},{17,0},{2,3},{3,18},{18,19},{19,2},{4,5},{5,2... | collective-permute-start | bytes 393224 | tf_op jit(solution)/shard_map/ppermute | solution.py:19
  12.7 13.7 %collective-permute-start.2 = (f32[256,128]{1,0:T(8,128)}, f32[256,128]{1,0:T(8,128)}, u32[]{:S(2)}, u32[]{:S(2)}) collective-permute-start(f32[256,128]{1,0:T(8,128)} %gather_fusion), channel_id=1, source_target_pairs={{0,17},{1,0},{16,1},{17,16},{2,19},{3,2},{18,3},{19,18},{4,21},{5,... | collective-permute-start | bytes 393224 | tf_op jit(solution)/shard_map/ppermute | solution.py:19
  14.8 13.5 %collective-permute-start.4 = (f32[256,128]{1,0:T(8,128)}, f32[256,128]{1,0:T(8,128)}, u32[]{:S(2)}, u32[]{:S(2)}) collective-permute-start(f32[256,128]{1,0:T(8,128)} %gather_fusion), channel_id=1, source_target_pairs={{0,16},{1,17},{16,0},{17,1},{2,18},{3,19},{18,2},{19,3},{4,20},{5,... | collective-permute-start | bytes 393224 | tf_op jit(solution)/shard_map/ppermute | solution.py:19
  18.5 12.3 %copy-start.7 = (f32[3072,128]{1,0:T(8,128)S(1)}, f32[3072,128]{1,0:T(8,128)}, u32[]{:S(2)}) copy-start(f32[3072,128]{1,0:T(8,128)} %array_ref.1) | copy-start | bytes 4718596
  18.5 12.3 %collective-permute-start = (f32[768,128]{1,0:T(8,128)}, f32[768,128]{1,0:T(8,128)S(1)}, u32[]{:S(2)}, u32[]{:S(2)}) collective-permute-start(f32[768,128]{1,0:T(8,128)} %slice.12), channel_id=1, source_target_pairs={{0,1},{1,0},{2,3},{3,2},{4,5},{5,4},{6,7},{7,6},{8,9},{9,8},{10,11... | collective-permute-start | bytes 1179656 | tf_op jit(solution)/shard_map/ppermute | solution.py:19
  22.1 38.7 %collective-permute-start.1 = (f32[2304,128]{1,0:T(8,128)}, f32[2304,128]{1,0:T(8,128)}, u32[]{:S(2)}, u32[]{:S(2)}) collective-permute-start(f32[2304,128]{1,0:T(8,128)} %slice.13), channel_id=1, source_target_pairs={{0,1},{1,0},{2,3},{3,2},{4,5},{5,4},{6,7},{7,6},{8,9},{9,8},{10,11... | collective-permute-start | bytes 3538952 | tf_op jit(solution)/shard_map/ppermute | solution.py:19
  28.4 7.7 %copy-start.20 = (s32[256]{0:T(256)S(1)}, s32[256]{0:T(256)}, u32[]{:S(2)}) copy-start(s32[256]{0:T(256)} %reshape.229) | copy-start | bytes 3076
  30.9 25.8 %copy-start.14 = (f32[1152,128]{1,0:T(8,128)}, f32[1152,128]{1,0:T(8,128)S(1)}, u32[]{:S(2)}) copy-start(f32[1152,128]{1,0:T(8,128)S(1)} %get-tuple-element.23) | copy-start | bytes 1769476
  30.9 25.8 %copy-start.16 = (f32[1152,128]{1,0:T(8,128)}, f32[1152,128]{1,0:T(8,128)S(1)}, u32[]{:S(2)}) copy-start(f32[1152,128]{1,0:T(8,128)S(1)} %get-tuple-element.16) | copy-start | bytes 1769476
  30.9 16.5 %collective-permute-start.7 = (f32[2,256,256]{2,1,0:T(8,128)S(1)}, f32[2,256,256]{2,1,0:T(8,128)S(1)}, u32[]{:S(2)}, u32[]{:S(2)}) collective-permute-start(f32[2,256,256]{2,1,0:T(8,128)S(1)} %get-tuple-element.15), channel_id=1, source_target_pairs={{0,64},{32,96},{64,0},{96,32},{1,65},{33,97},{65,1},{97,33},{2,66}... | collective-permute-start | bytes 1572872 | tf_op jit(solution)/shard_map/ppermute | solution.py:19
  34.0 21.2 %collective-permute-start.6 = (f32[2,256,256]{2,1,0:T(8,128)S(1)}, f32[2,256,256]{2,1,0:T(8,128)S(1)}, u32[]{:S(2)}, u32[]{:S(2)}) collective-permute-start(f32[2,256,256]{2,1,0:T(8,128)S(1)} %get-tuple-element.15), channel_id=1, source_target_pairs={{0,96},{32,0},{64,32},{96,64},{1,97},{33,1},{65,33},{97,65},{2,98}... | collective-permute-start | bytes 1572872 | tf_op jit(solution)/shard_map/ppermute | solution.py:19
  35.1 20.0 %collective-permute-start.5 = (f32[2,256,256]{2,1,0:T(8,128)S(1)}, f32[2,256,256]{2,1,0:T(8,128)S(1)}, u32[]{:S(2)}, u32[]{:S(2)}) collective-permute-start(f32[2,256,256]{2,1,0:T(8,128)S(1)} %get-tuple-element.15), channel_id=1, source_target_pairs={{0,32},{32,64},{64,96},{96,0},{1,33},{33,65},{65,97},{97,1},{2,34}... | collective-permute-start | bytes 1572872 | tf_op jit(solution)/shard_map/ppermute | solution.py:19
  60.8 10.7 %copy-start.8 = (f32[3072,128]{1,0:T(8,128)S(1)}, f32[3072,128]{1,0:T(8,128)}, u32[]{:S(2)}) copy-start(f32[3072,128]{1,0:T(8,128)} %own_ref.1) | copy-start | bytes 4718596
  62.6 1.9 %collective-permute-start.8 = (f32[4,64,256]{2,1,0:T(8,128)}, f32[4,64,256]{2,1,0:T(8,128)}, u32[]{:S(2)}, u32[]{:S(2)}) collective-permute-start(f32[4,64,256]{2,1,0:T(8,128)} %slice_bitcast_fusion), channel_id=1, source_target_pairs={{0,8},{8,0},{1,9},{9,1},{2,10},{10,2},{3,11},{11,3},{4,12},{12,4},... | collective-permute-start | bytes 786440 | tf_op jit(solution)/shard_map/ppermute | solution.py:19
  62.6 17.7 %collective-permute-start.12 = (f32[1152,128]{1,0:T(8,128)}, f32[1152,128]{1,0:T(8,128)}, u32[]{:S(2)}, u32[]{:S(2)}) collective-permute-start(f32[1152,128]{1,0:T(8,128)} %copy-done.16), channel_id=1, source_target_pairs={{0,1},{1,0},{2,3},{3,2},{4,5},{5,4},{6,7},{7,6},{8,9},{9,8},{10,11... | collective-permute-start | bytes 1769480 | tf_op jit(solution)/shard_map/ppermute | solution.py:19
  66.3 11.9 %collective-permute-start.11 = (f32[64,256]{1,0:T(8,128)}, f32[64,256]{1,0:T(8,128)}, u32[]{:S(2)}, u32[]{:S(2)}) collective-permute-start(f32[64,256]{1,0:T(8,128)} %get-tuple-element.34), channel_id=1, source_target_pairs={{0,4},{2,6},{4,0},{6,2},{1,5},{3,7},{5,1},{7,3},{8,12},{10,14},{12... | collective-permute-start | bytes 196616 | tf_op jit(solution)/shard_map/ppermute | solution.py:19
  69.4 8.7 %collective-permute-start.10 = (f32[64,256]{1,0:T(8,128)}, f32[64,256]{1,0:T(8,128)}, u32[]{:S(2)}, u32[]{:S(2)}) collective-permute-start(f32[64,256]{1,0:T(8,128)} %get-tuple-element.35), channel_id=1, source_target_pairs={{0,6},{2,0},{4,2},{6,4},{1,7},{3,1},{5,3},{7,5},{8,14},{10,8},{12,... | collective-permute-start | bytes 196616 | tf_op jit(solution)/shard_map/ppermute | solution.py:19
  70.5 7.6 %collective-permute-start.9 = (f32[64,256]{1,0:T(8,128)}, f32[64,256]{1,0:T(8,128)}, u32[]{:S(2)}, u32[]{:S(2)}) collective-permute-start(f32[64,256]{1,0:T(8,128)} %get-tuple-element.36), channel_id=1, source_target_pairs={{0,2},{2,4},{4,6},{6,0},{1,3},{3,5},{5,7},{7,1},{8,10},{10,12},{12... | collective-permute-start | bytes 196616 | tf_op jit(solution)/shard_map/ppermute | solution.py:19
  71.5 6.7 %copy-start.17 = (f32[1,64,256]{2,1,0:T(8,128)S(1)}, f32[1,64,256]{2,1,0:T(8,128)}, u32[]{:S(2)}) copy-start(f32[1,64,256]{2,1,0:T(8,128)} %get-tuple-element.33) | copy-start | bytes 196612
  80.3 85.7 %all-gather.11.cloned.1.call-start = ((), (), s32[]{:S(2)}) async-start(), calls=%async_computation.2 | async-start | bytes 5898240 | tf_op jit(solution)/shard_map/all_gather | solution.py:393
  81.3 14.5 %collective-permute-start.31 = (f32[1152,128]{1,0:T(8,128)S(1)}, f32[1152,128]{1,0:T(8,128)S(1)}, u32[]{:S(2)}, u32[]{:S(2)}) collective-permute-start(f32[1152,128]{1,0:T(8,128)S(1)} %copy-done.15), channel_id=1, source_target_pairs={{0,1},{1,0},{2,3},{3,2},{4,5},{5,4},{6,7},{7,6},{8,9},{9,8},{10,11... | collective-permute-start | bytes 1769480 | tf_op jit(solution)/shard_map/ppermute | solution.py:19
  84.1 2.8 %copy-start.3 = (f32[12288,128]{1,0:T(8,128)S(1)}, f32[12288,128]{1,0:T(8,128)}, u32[]{:S(2)}) copy-start(f32[12288,128]{1,0:T(8,128)} %all-gather.7.cloned.1.call-done) | copy-start | bytes 18874372
  93.1 5.8 %copy-start.19 = (f32[1024]{0:T(1024)S(1)}, f32[1024]{0:T(1024)}, u32[]{:S(2)}) copy-start(f32[1024]{0:T(1024)} %param.9) | copy-start | bytes 12292
  93.1 1.5 collective-permute-start.13
  99.1 6.8 %collective-permute-start.14 = (f32[32,512]{1,0:T(8,128)S(1)}, f32[32,512]{1,0:T(8,128)S(1)}, u32[]{:S(2)}, u32[]{:S(2)}) collective-permute-start(f32[32,512]{1,0:T(8,128)S(1)} %get-tuple-element.20), channel_id=1, source_target_pairs={{0,32},{32,64},{64,96},{96,0},{1,33},{33,65},{65,97},{97,1},{2,34}... | collective-permute-start | bytes 196616 | tf_op jit(solution)/shard_map/ppermute | solution.py:19
  100.6 5.5 %collective-permute-start.15 = (f32[32,512]{1,0:T(8,128)S(1)}, f32[32,512]{1,0:T(8,128)S(1)}, u32[]{:S(2)}, u32[]{:S(2)}) collective-permute-start(f32[32,512]{1,0:T(8,128)S(1)} %get-tuple-element.21), channel_id=1, source_target_pairs={{0,96},{32,0},{64,32},{96,64},{1,97},{33,1},{65,33},{97,65},{2,98}... | collective-permute-start | bytes 196616 | tf_op jit(solution)/shard_map/ppermute | solution.py:19
  102.4 5.8 %collective-permute-start.16 = (f32[32,512]{1,0:T(8,128)S(1)}, f32[32,512]{1,0:T(8,128)S(1)}, u32[]{:S(2)}, u32[]{:S(2)}) collective-permute-start(f32[32,512]{1,0:T(8,128)S(1)} %get-tuple-element.22), channel_id=1, source_target_pairs={{0,64},{32,96},{64,0},{96,32},{1,65},{33,97},{65,1},{97,33},{2,66}... | collective-permute-start | bytes 196616 | tf_op jit(solution)/shard_map/ppermute | solution.py:19
  108.2 8.4 %collective-permute-start.19 = (f32[32,512]{1,0:T(8,128)S(1)}, f32[32,512]{1,0:T(8,128)S(1)}, u32[]{:S(2)}, u32[]{:S(2)}) collective-permute-start(f32[32,512]{1,0:T(8,128)S(1)} %add_add_fusion), channel_id=1, source_target_pairs={{0,17},{1,0},{16,1},{17,16},{2,19},{3,2},{18,3},{19,18},{4,21},{5,... | collective-permute-start | bytes 196616 | tf_op jit(solution)/shard_map/ppermute | solution.py:19
  110.7 6.2 %collective-permute-start.18 = (f32[32,512]{1,0:T(8,128)S(1)}, f32[32,512]{1,0:T(8,128)S(1)}, u32[]{:S(2)}, u32[]{:S(2)}) collective-permute-start(f32[32,512]{1,0:T(8,128)S(1)} %add_add_fusion), channel_id=1, source_target_pairs={{0,1},{1,16},{16,17},{17,0},{2,3},{3,18},{18,19},{19,2},{4,5},{5,2... | collective-permute-start | bytes 196616 | tf_op jit(solution)/shard_map/ppermute | solution.py:19
  110.7 5.9 %collective-permute-start.17 = (f32[32,512]{1,0:T(8,128)S(1)}, f32[32,512]{1,0:T(8,128)S(1)}, u32[]{:S(2)}, u32[]{:S(2)}) collective-permute-start(f32[32,512]{1,0:T(8,128)S(1)} %add_add_fusion), channel_id=1, source_target_pairs={{0,16},{1,17},{16,0},{17,1},{2,18},{3,19},{18,2},{19,3},{4,20},{5,... | collective-permute-start | bytes 196616 | tf_op jit(solution)/shard_map/ppermute | solution.py:19
  113.5 9.4 %collective-permute-start.23 = (f32[4,64,1024]{2,1,0:T(8,128)}, f32[4,64,1024]{2,1,0:T(8,128)}, u32[]{:S(2)}, u32[]{:S(2)}) collective-permute-start(f32[4,64,1024]{2,1,0:T(8,128)} %bitcast.59), channel_id=1, source_target_pairs={{0,8},{8,0},{1,9},{9,1},{2,10},{10,2},{3,11},{11,3},{4,12},{12,4},... | collective-permute-start | bytes 3145736 | tf_op jit(solution)/shard_map/ppermute | solution.py:19
  117.6 43.3 %collective-permute-start.32 = (f32[4,768,128]{2,1,0:T(8,128)}, f32[4,768,128]{2,1,0:T(8,128)S(1)}, u32[]{:S(2)}, u32[]{:S(2)}) collective-permute-start(f32[4,768,128]{2,1,0:T(8,128)} %shard_map.73), channel_id=1, source_target_pairs={{0,1},{1,0},{2,3},{3,2},{4,5},{5,4},{6,7},{7,6},{8,9},{9,8},{10,11... | collective-permute-start | bytes 4718600 | tf_op jit(solution)/shard_map/ppermute | solution.py:19
  118.6 7.5 %collective-permute-start.22 = (f32[32,1024]{1,0:T(8,128)S(1)}, f32[32,1024]{1,0:T(8,128)S(1)}, u32[]{:S(2)}, u32[]{:S(2)}) collective-permute-start(f32[32,1024]{1,0:T(8,128)S(1)} %copy-done.12), channel_id=1, source_target_pairs={{0,4},{2,6},{4,0},{6,2},{1,5},{3,7},{5,1},{7,3},{8,12},{10,14},{12... | collective-permute-start | bytes 393224 | tf_op jit(solution)/shard_map/ppermute | solution.py:19
  120.9 10.2 %collective-permute-start.21 = (f32[32,1024]{1,0:T(8,128)S(1)}, f32[32,1024]{1,0:T(8,128)S(1)}, u32[]{:S(2)}, u32[]{:S(2)}) collective-permute-start(f32[32,1024]{1,0:T(8,128)S(1)} %copy-done.12), channel_id=1, source_target_pairs={{0,6},{2,0},{4,2},{6,4},{1,7},{3,1},{5,3},{7,5},{8,14},{10,8},{12,... | collective-permute-start | bytes 393224 | tf_op jit(solution)/shard_map/ppermute | solution.py:19
  122.3 9.4 %collective-permute-start.20 = (f32[32,1024]{1,0:T(8,128)S(1)}, f32[32,1024]{1,0:T(8,128)S(1)}, u32[]{:S(2)}, u32[]{:S(2)}) collective-permute-start(f32[32,1024]{1,0:T(8,128)S(1)} %copy-done.12), channel_id=1, source_target_pairs={{0,2},{2,4},{4,6},{6,0},{1,3},{3,5},{5,7},{7,1},{8,10},{10,12},{12... | collective-permute-start | bytes 393224 | tf_op jit(solution)/shard_map/ppermute | solution.py:19
  135.4 10.1 %collective-permute-start.26 = (f32[128,512]{1,0:T(8,128)S(1)}, f32[128,512]{1,0:T(8,128)S(1)}, u32[]{:S(2)}, u32[]{:S(2)}) collective-permute-start(f32[128,512]{1,0:T(8,128)S(1)} %shard_map.70.refs_0_), channel_id=1, source_target_pairs={{0,64},{32,96},{64,0},{96,32},{1,65},{33,97},{65,1},{97,33},{2,66}... | collective-permute-start | bytes 786440 | tf_op jit(solution)/shard_map/ppermute | solution.py:19
  137.4 8.5 %collective-permute-start.25 = (f32[128,512]{1,0:T(8,128)S(1)}, f32[128,512]{1,0:T(8,128)S(1)}, u32[]{:S(2)}, u32[]{:S(2)}) collective-permute-start(f32[128,512]{1,0:T(8,128)S(1)} %shard_map.70.refs_0_), channel_id=1, source_target_pairs={{0,96},{32,0},{64,32},{96,64},{1,97},{33,1},{65,33},{97,65},{2,98}... | collective-permute-start | bytes 786440 | tf_op jit(solution)/shard_map/ppermute | solution.py:19
  139.3 8.9 %collective-permute-start.24 = (f32[128,512]{1,0:T(8,128)S(1)}, f32[128,512]{1,0:T(8,128)S(1)}, u32[]{:S(2)}, u32[]{:S(2)}) collective-permute-start(f32[128,512]{1,0:T(8,128)S(1)} %shard_map.70.refs_0_), channel_id=1, source_target_pairs={{0,32},{32,64},{64,96},{96,0},{1,33},{33,65},{65,97},{97,1},{2,34}... | collective-permute-start | bytes 786440 | tf_op jit(solution)/shard_map/ppermute | solution.py:19
  139.4 8.8 %collective-permute-start.27 = (f32[128,512]{1,0:T(8,128)S(1)}, f32[128,512]{1,0:T(8,128)S(1)}, u32[]{:S(2)}, u32[]{:S(2)}) collective-permute-start(f32[128,512]{1,0:T(8,128)S(1)} %shard_map.70.refs_0_), channel_id=1, source_target_pairs={{0,8},{8,0},{1,9},{9,1},{2,10},{10,2},{3,11},{11,3},{4,12},{12,4},... | collective-permute-start | bytes 786440 | tf_op jit(solution)/shard_map/ppermute | solution.py:19
  145.5 2.7 %collective-permute-start.30 = (f32[128,512]{1,0:T(8,128)S(1)}, f32[128,512]{1,0:T(8,128)S(1)}, u32[]{:S(2)}, u32[]{:S(2)}) collective-permute-start(f32[128,512]{1,0:T(8,128)S(1)} %collective-permute-done.26.refs_3_), channel_id=1, source_target_pairs={{0,8},{8,0},{1,9},{9,1},{2,10},{10,2},{3,11},{11,3},{4,12},{12,4},... | collective-permute-start | bytes 786440 | tf_op jit(solution)/shard_map/ppermute | solution.py:19
  145.9 2.3 %collective-permute-start.29 = (f32[128,512]{1,0:T(8,128)S(1)}, f32[128,512]{1,0:T(8,128)S(1)}, u32[]{:S(2)}, u32[]{:S(2)}) collective-permute-start(f32[128,512]{1,0:T(8,128)S(1)} %collective-permute-done.25.refs_2_), channel_id=1, source_target_pairs={{0,8},{8,0},{1,9},{9,1},{2,10},{10,2},{3,11},{11,3},{4,12},{12,4},... | collective-permute-start | bytes 786440 | tf_op jit(solution)/shard_map/ppermute | solution.py:19
  148.2 1.5 collective-permute-start.28
  150.7 2.9 %copy-start.4 = (f32[12288,128]{1,0:T(8,128)S(1)}, f32[12288,128]{1,0:T(8,128)}, u32[]{:S(2)}) copy-start(f32[12288,128]{1,0:T(8,128)} %all-gather.7.cloned.1.call-done) | copy-start | bytes 18874372
  153.5 7.4 %copy-start.5 = (bf16[1024,1024]{1,0:T(8,128)(2,1)}, bf16[1024,1024]{1,0:T(8,128)(2,1)S(1)}, u32[]{:S(2)}) copy-start(bf16[1024,1024]{1,0:T(8,128)(2,1)S(1)} %shard_map.71.z_ref) | copy-start | bytes 6291460
  167.6 2.3 %copy-start.9 = (f32[9216,128]{1,0:T(8,128)S(1)}, f32[9216,128]{1,0:T(8,128)}, u32[]{:S(2)}) copy-start(f32[9216,128]{1,0:T(8,128)} %all-gather.11.cloned.1.call-done) | copy-start | bytes 14155780
  (9 other events, 12.8 us)
Sparse Core Ops, SparseCore 0:
  9.0 70.9 all-gather.6
  81.7 25.3 all-gather.8
  108.8 57.1 all-gather.10
